TPU v7x, 256 devices: a whole 4x4x8 slice. The times are simulated.
256 devices in a mesh: dp: 16 (over z, core), seq: 16 (over x, y).
Axes of the slice: x: 4, y: 4, z: 8, core: 2. Of those that a mesh axis runs over, the one named last changes fastest.
Arguments:
- ssd_input: bfloat16 [65536, 4096], P(('dp', 'seq')), parts along dimension 0, may hold values from -6 to 6
- gate_input: bfloat16 [65536, 4096], P(('dp', 'seq')), parts along dimension 0, may hold values from -6 to 6
- write_map: bfloat16 [65536, 512], P(('dp', 'seq')), parts along dimension 0, may hold values from -6 to 6
- read_map: bfloat16 [65536, 512], P(('dp', 'seq')), parts along dimension 0, may hold values from -6 to 6
- step_size: float32 [65536, 32], P(('dp', 'seq')), parts along dimension 0, may hold values from 0.002 to 51.2, as said below
- decay_log: float32 [32], replicated, as said below
- skip_gain: float32 [32], replicated, may hold values from 0.5 to 1.5
- norm_gain: bfloat16 [4096], replicated, may hold values from 0.099609375 to 1.8984375
- query_rows: bfloat16 [65536, 2048], P(('dp', 'seq')), parts along dimension 0, may hold values from -30 to 30
- key_rows: bfloat16 [65536, 512], P(('dp', 'seq')), parts along dimension 0, may hold values from -4 to 4
- value_rows: bfloat16 [65536, 512], P(('dp', 'seq')), parts along dimension 0, may hold values from -6 to 6
Outputs:
- ssd_out: bfloat16 [65536, 4096], P(('dp', 'seq')), parts along dimension 0
- attn_out: bfloat16 [65536, 2048], P(('dp', 'seq')), parts along dimension 0
There are 16 independent parts, one for each index of `dp`. A program takes and returns all parts, laid end to end along the dimension named above; an argument that names none is the same for every part. Nothing has to cross between parts.
Inputs may be any that keep to these rules, and one draw needn't show every extreme that they name: `step_size`: positive everywhere. Rates exp(decay_log) lie between 30 / 4096 and about 3.4.
All inputs are finite; a program needn't handle non-finite values.
Results may differ from a plain program's by a relative error of at most 0.0059.
Values may be sent and summed in bfloat16 or wider, within the bound.
No kernel may reach another device: no remote copies, remote signals or barrier semaphores. Data moves between devices by JAX's collectives and lax.ppermute only.
A program may use at most 192 MiB of HBM per device.

v0:
```python
import math

import jax
import jax.numpy as jnp
from jax import lax
from jax.sharding import PartitionSpec as P

SSD_HEADS = 32
HEAD_DIM = 128
STATE = 128
GROUPS = 4
SPAN = 128
Q_HEADS = 16
KV_HEADS = 4
ATT_DIM = 128


def entering(value, axis, join, neutral):
    count, mine = (lax.axis_size(axis), lax.axis_index(axis))
    pieces = jax.tree.map(lambda part: lax.all_gather(part, axis), value)
    total = jax.tree.map(
        lambda part, zero: jnp.full_like(part, 0) + jnp.asarray(zero, part.dtype), value, neutral
    )

    def turn(position, total):
        longer = join(total, jax.tree.map(lambda part: part[position], pieces))
        return jax.tree.map(lambda new, old: jnp.where(position < mine, new, old), longer, total)

    return lax.fori_loop(0, count - 1, turn, total)


def gated_norm(mixed_out, gate_input, norm_gain):
    row_count = mixed_out.shape[0]
    gated_y = mixed_out * jax.nn.silu(gate_input.astype(jnp.float32))
    grouped = gated_y.reshape(row_count, GROUPS, -1)
    inverse = lax.rsqrt(jnp.mean(grouped * grouped, axis=-1, keepdims=True) + 1e-05)
    normed = (grouped * inverse).reshape(row_count, -1)
    return (normed * norm_gain.astype(jnp.float32)).astype(jnp.bfloat16)


def chain_join(earlier, later_part):
    return (
        earlier[0] + later_part[0],
        jnp.exp(later_part[0])[..., None, None] * earlier[1] + later_part[1],
    )


def ssd_local(ssd_input, write_map, read_map, step_size, decay_log, skip_gain):
    row_count = ssd_input.shape[0]
    n_spans = row_count // SPAN
    per_group = SSD_HEADS // GROUPS
    decay_rate = (-jnp.exp(decay_log)).reshape(GROUPS, per_group)
    inputs_x = ssd_input.reshape(n_spans, SPAN, GROUPS, per_group, HEAD_DIM)
    write_vals = write_map.reshape(n_spans, SPAN, GROUPS, STATE)
    read_vals = read_map.reshape(n_spans, SPAN, GROUPS, STATE)
    steps_dt = step_size.reshape(n_spans, SPAN, GROUPS, per_group)
    cumulative = jnp.cumsum(steps_dt * decay_rate, axis=1)
    causal = jnp.tril(jnp.ones((SPAN, SPAN), dtype=bool))
    log_gap = cumulative[:, :, None] - cumulative[:, None]
    decay_mat = jnp.where(causal[None, :, :, None, None], jnp.exp(jnp.minimum(log_gap, 0.0)), 0.0)
    intersection = jnp.einsum(
        "ctgn,csgn->ctsg", read_vals, write_vals, preferred_element_type=jnp.float32
    )
    weights = (intersection[..., None] * decay_mat * steps_dt[:, None]).astype(jnp.bfloat16)
    local_y = jnp.einsum(
        "ctsgj,csgjp->ctgjp", weights, inputs_x, preferred_element_type=jnp.float32
    )
    to_end = jnp.exp(cumulative[:, -1:] - cumulative) * steps_dt
    scaled = (to_end[..., None] * inputs_x).astype(jnp.bfloat16)
    span_states = jnp.einsum(
        "csgn,csgjp->cgjnp", write_vals, scaled, preferred_element_type=jnp.float32
    )
    span_decay = cumulative[:, -1]

    def advance(carry_state, pieces):
        piece_state, piece_decay = pieces
        return (jnp.exp(piece_decay)[..., None, None] * carry_state + piece_state, carry_state)

    zero_state = jnp.zeros((GROUPS, per_group, STATE, HEAD_DIM), jnp.float32)
    local_final, local_starts = lax.scan(advance, zero_state, (span_states, span_decay))
    device_decay = jnp.sum(span_decay, axis=0)
    prefix = entering(
        (device_decay, local_final),
        "seq",
        chain_join,
        (jnp.zeros_like(device_decay), jnp.zeros_like(local_final)),
    )
    incoming = prefix[1]
    before = jnp.cumsum(span_decay, axis=0) - span_decay
    starts = (local_starts + jnp.exp(before)[..., None, None] * incoming[None]).astype(jnp.bfloat16)
    carried = (
        jnp.einsum("ctgn,cgjnp->ctgjp", read_vals, starts, preferred_element_type=jnp.float32)
        * jnp.exp(cumulative)[..., None]
    )
    skip_heads = skip_gain.reshape(GROUPS, per_group)
    mixed_out = local_y + carried + skip_heads[:, :, None] * inputs_x
    return mixed_out.reshape(row_count, SSD_HEADS * HEAD_DIM)


def score_block(query_part, part_pos, key_block, value_block, k_pos, current):
    running, weight_sum, context_sum = current
    score_scale = ATT_DIM ** (-0.5)
    scores = (
        jnp.einsum("rhgd,khd->hgrk", query_part, key_block, preferred_element_type=jnp.float32)
        * score_scale
    )
    visible = k_pos[None, :] <= part_pos[:, None]
    scores = jnp.where(visible, scores, -1e30)
    newmax = jnp.maximum(running, jnp.max(scores, axis=-1))
    factor = jnp.exp(running - newmax)
    exps = jnp.where(visible, jnp.exp(scores - newmax[..., None]), 0.0)
    weight_sum = weight_sum * factor + jnp.sum(exps, axis=-1)
    update = jnp.einsum(
        "hgrk,khd->rhgd", exps.astype(jnp.bfloat16), value_block, preferred_element_type=jnp.float32
    )
    context_sum = context_sum * jnp.transpose(factor, (2, 0, 1))[..., None] + update
    return (newmax, weight_sum, context_sum)


def attend(local_q, q_pos, key_rows, value_rows):
    row_count = local_q.shape[0]
    group_size = Q_HEADS // KV_HEADS
    queries = local_q.reshape(row_count, KV_HEADS, group_size, ATT_DIM)
    quarter = row_count // 4
    query_parts = [queries[index_q * quarter : (index_q + 1) * quarter] for index_q in range(4)]
    part_positions = [q_pos[index_q * quarter : (index_q + 1) * quarter] for index_q in range(4)]
    part_last = [jnp.max(element_indices) for element_indices in part_positions]

    def fresh_state():
        return (
            jnp.full((KV_HEADS, group_size, quarter), -1e30, jnp.float32),
            jnp.zeros((KV_HEADS, group_size, quarter), jnp.float32),
            jnp.zeros((quarter, KV_HEADS, group_size, ATT_DIM), jnp.float32),
        )

    initial = (fresh_state(), fresh_state(), fresh_state(), fresh_state())
    key_piece = lax.all_gather(key_rows, "seq", axis=0, tiled=True)
    value_piece = lax.all_gather(value_rows, "seq", axis=0, tiled=True)
    piece_rows = key_piece.shape[0]
    block_rows = math.gcd(piece_rows, 512)
    key_all = key_piece.reshape(piece_rows, KV_HEADS, ATT_DIM)
    value_all = value_piece.reshape(piece_rows, KV_HEADS, ATT_DIM)

    def one_block(index_b, states):
        offset = index_b * block_rows
        key_block = lax.dynamic_slice_in_dim(key_all, offset, block_rows, 0)
        value_block = lax.dynamic_slice_in_dim(value_all, offset, block_rows, 0)
        k_pos = offset + jnp.arange(block_rows, dtype=jnp.int32)
        updated = []
        for index_q in range(4):
            compute = partial_block(
                query_parts[index_q], part_positions[index_q], key_block, value_block, k_pos
            )
            updated.append(
                lax.cond(
                    offset > part_last[index_q], lambda current: current, compute, states[index_q]
                )
            )
        return tuple(updated)

    result = lax.fori_loop(0, piece_rows // block_rows, one_block, initial)
    contexts = [state[2] / jnp.transpose(state[1], (2, 0, 1))[..., None] for state in result]
    context = jnp.concatenate(contexts, axis=0)
    return context.reshape(row_count, Q_HEADS * ATT_DIM).astype(jnp.bfloat16)


def partial_block(query_part, part_pos, key_block, value_block, k_pos):

    def compute(current):
        return score_block(query_part, part_pos, key_block, value_block, k_pos, current)

    return compute


def local(
    ssd_input,
    gate_input,
    write_map,
    read_map,
    step_size,
    decay_log,
    skip_gain,
    norm_gain,
    query_rows,
    key_rows,
    value_rows,
):
    mixed_out = ssd_local(ssd_input, write_map, read_map, step_size, decay_log, skip_gain)
    ssd_out = gated_norm(mixed_out, gate_input, norm_gain)
    row_count = query_rows.shape[0]
    my_index = lax.axis_index("seq")
    local_idx = jnp.arange(row_count, dtype=jnp.int32)
    q_pos = my_index * row_count + local_idx
    context = attend(query_rows, q_pos, key_rows, value_rows)
    return (ssd_out, context)


def solution(mesh):
    in_specs = (
        P(("dp", "seq"), None),
        P(("dp", "seq"), None),
        P(("dp", "seq"), None),
        P(("dp", "seq"), None),
        P(("dp", "seq"), None),
        P(),
        P(),
        P(),
        P(("dp", "seq"), None),
        P(("dp", "seq"), None),
        P(("dp", "seq"), None),
    )
    out_specs = (P(("dp", "seq"), None), P(("dp", "seq"), None))
    return jax.shard_map(local, mesh=mesh, in_specs=in_specs, out_specs=out_specs, check_vma=False)
```

profile of v0, /device:TPU:64, one launch (start us, length us, event | category | flops | bytes accessed | tf_op | source)
XLA Modules:
  0.0 428.2 jit_solution(18411172037231461270)
XLA Ops:
  7.2 1.8 copy.129
  9.1 1.8 copy.130
  14.0 2.1 fusion.93
  16.3 3.5 copy.158
  19.8 5.4 %convolution_bitcast_fusion.4 = f32[2,4,8,128,128]{3,4,2,1,0:T(8,128)} fusion(f32[2,128,4,8]{1,3,2,0:T(8,128)S(1)} %copy.117, bf16[2,128,4,8,128]{4,3,2,1,0:T(8,128)(2,1)} %bitcast.197, bf16[2,128,4,128,1]{3,2,1,0,4:T(4,128)(2,1)S(1)} %bitcast.208), kind=kOutput, calls=%fused_computation.109 | convolution fusion | flops 271581184 | bytes 6586368 | tf_op jit(solution)/shard_map/csgn,csgjp->cgjnp/dot_general | solution.py:70
  25.2 18.8 %while.63 = (s32[]{:T(128)}, f32[4,8,128,128]{3,2,1,0:T(8,128)S(1)}, f32[2,4,8,128,128]{4,3,2,1,0:T(8,128)}, f32[2,4,8]{2,1,0:T(4,128)S(1)}, f32[2,4,8,128,128]{3,4,2,1,0:T(8,128)}, /*index=5*/s32[]{:T(128)}, s32[]{:T(128)}) while((s32[]{:T(128)}, f32[4,8,128,128]{3,2,1,0:T(8,128)S(1)}, f32[2,4,8,128,128]{4,3,2,1,0:T(8,128)}, ...), condition=%wide.region_2.3_spmd.clone, body=%wide.region_1.2_spmd.clone.sunk | while | flops 2097155 | bytes 35652600 | solution.py:80
  25.2 1.5 bitcast_dynamic-update-slice_fusion.2
  26.7 1.5 copy-done.1
  28.2 1.5 constant_dynamic-slice_fusion.6
  29.7 2.9 copy.181
  32.6 2.0 bitcast_add_fusion.3
  36.1 1.5 copy-done.1
  37.6 1.5 constant_dynamic-slice_fusion.6
  39.1 2.9 copy.181
  42.0 2.0 bitcast_add_fusion.3
  45.5 2.1 fusion.92
  57.0 2.1 copy.110
  59.1 25.5 %all-gather.2 = f32[16,4,8]{2,1,0:T(4,128)} all-gather(f32[1,4,8]{2,1,0:T(4,128)S(1)} %bitcast.232), channel_id=2, replica_groups=mesh['dp'=16,'seq'=16] {'seq'}, dimensions={0}, use_global_device_ids=true | all-gather | bytes 2176 | tf_op jit(solution)/shard_map/all_gather | solution.py:20
  86.1 4.6 %fusion.72 = f32[2,4,8,128,128]{4,3,2,1,0:T(8,128)} fusion(f32[2,128,4,8]{1,3,2,0:T(8,128)S(1)} %copy.114, f32[2,128,4,8]{1,3,2,0:T(8,128)S(1)} %copy.112, f32[2,128,128,4]{2,1,3,0:T(8,128)} %copy.110, pred[128,128]{1,0:T(8,128)(4,1)S(1)} %iota_compare_fusion, bf16[2,128,4,8,128]{4,3,2,1,0:T(8,128)(2,1)} %bitcast.198), kind=kOutput, calls=%fused_computation.110 | convolution fusion | flops 274726912 | bytes 6897664 | tf_op jit(solution)/shard_map/ctsgj,csgjp->ctgjp/dot_general | solution.py:65
  90.7 49.0 %all-gather.9.cloned.1.call-done = bf16[4096,512]{0,1:T(8,128)(2,1)} async-done(((bf16[256,512]{0,1:T(8,128)(2,1)}), bf16[4096,512]{0,1:T(8,128)(2,1)}) %all-gather.9.cloned.1.call-update) | async-done | bytes 4194320 | tf_op jit(solution)/shard_map/all_gather | solution.py:138
  143.2 74.1 %while.62 = (s32[]{:T(128)}, f32[4,4,64]{2,1,0:T(4,128)S(1)}, f32[4,4,64]{2,1,0:T(4,128)S(1)}, f32[64,4,4,128]{3,0,2,1:T(8,128)}, f32[4,4,64]{2,1,0:T(4,128)S(1)...) while((s32[]{:T(128)}, f32[4,4,64]{2,1,0:T(4,128)S(1)}, ...), condition=%wide.region_29.30_spmd, body=%wide.region_12.29_spmd.sunk | while | flops 1102197248 | bytes 64761988 | solution.py:161
  143.2 2.1 constant_dynamic-slice_fusion.5
  148.4 4.2 conditional.10
  148.5 1.6 fusion.32
  153.2 4.2 conditional.11
  153.3 1.6 fusion.48
  158.0 4.2 conditional.9
  158.2 1.6 fusion.16
  162.8 3.1 conditional.8
  166.0 2.1 constant_dynamic-slice_fusion.5
  173.2 2.1 constant_dynamic-slice_fusion.5
  180.6 2.2 constant_dynamic-slice_fusion.5
  187.9 2.1 constant_dynamic-slice_fusion.5
  195.2 2.1 constant_dynamic-slice_fusion.5
  202.5 2.1 constant_dynamic-slice_fusion.5
  209.8 2.4 constant_dynamic-slice_fusion.5
  217.3 1.5 divide_convert_fusion
  218.9 1.5 divide_convert_fusion.2
  221.3 1.6 convert_element_type.73
  222.9 120.8 %all-gather.11.cloned.1.call-done = f32[64,8,128,128]{3,2,1,0:T(8,128)} async-done(((f32[4,8,128,128]{3,2,1,0:T(8,128)}), f32[64,8,128,128]{3,2,1,0:T(8,128)}) %all-gather.11.cloned.1.call-update) | async-done | bytes 33554448 | tf_op jit(solution)/shard_map/all_gather | solution.py:20
  343.7 41.7 %while.64 = (s32[]{:T(128)}, f32[4,8,128,128]{3,2,1,0:T(8,128)S(1)}, s32[]{:T(128)}, f32[16,4,8]{2,1,0:T(4,128)}, f32[16,4,8,128,128]{4,3,2,1,0:T(8,128)}, /*index=5*/s32[]{:T(128)}, s32[]{:T(128)}) while((s32[]{:T(128)}, f32[4,8,128,128]{3,2,1,0:T(8,128)S(1)}, s32[]{:T(128)}, f32[16,4,8]{2,1,0:T(4,128)}, ...), condition=%wide.region_6.7_spmd.clone, body=%wide.region_5.6_spmd.clone.sunk | while | flops 2097156 | bytes 6291945 | solution.py:29
  344.4 2.1 fusion.101
  347.2 2.1 fusion.101
  350.0 2.1 fusion.101
  352.8 2.1 fusion.101
  355.6 2.1 fusion.101
  358.3 2.1 fusion.101
  361.1 2.1 fusion.101
  363.9 2.1 fusion.101
  366.6 2.1 fusion.101
  369.4 2.1 fusion.101
  372.2 2.1 fusion.101
  375.0 2.1 fusion.101
  377.8 2.1 fusion.101
  380.6 2.1 fusion.101
  383.4 2.1 fusion.101
  385.5 5.2 %fusion.66 = f32[2,128,4,8,128]{4,1,3,2,0:T(8,128)S(1)} fusion(f32[2,4,8,128,128]{4,3,2,1,0:T(8,128)} %fusion.72, f32[2,4,8,128,128]{4,3,2,1,0:T(8,128)} %get-tuple-element.711, f32[4,8]{1,0:T(4,128)S(1)} %mul.227, f32[2,128,4,8]{1,3,2,0:T(8,128)S(1)} %copy.125, f32[4,8,128,128]{3,2,1,0:T(8,128)S(1)} %get-tuple-element.713, f32[2,4,8]{2,1,0:T(4,128)S(1)} %copy-done.19, ...), kind=kOutput, calls=%fused_computation.99 | convolution fusion | flops 276824064 | bytes 17072512 | tf_op jit(solution)/shard_map/ctgn,cgjnp->ctgjp/dot_general | solution.py:92
  390.7 4.4 %copy.126 = f32[2,128,4,8,128]{4,3,2,1,0:T(8,128)} copy(f32[2,128,4,8,128]{4,1,3,2,0:T(8,128)S(1)} %fusion.66) | data formatting | bytes 8388608 | tf_op jit(solution)/shard_map/add | solution.py:96
  395.1 5.1 %reshape.122 = f32[256,4096]{1,0:T(8,128)} reshape(f32[2,128,4,8,128]{4,3,2,1,0:T(8,128)} %copy.126) | data formatting | bytes 8388608 | tf_op jit(solution)/shard_map/reshape | solution.py:97
  400.2 5.3 %fusion.91 = f32[256,4096]{1,0:T(8,128)} fusion(f32[256,4096]{1,0:T(8,128)} %reshape.122, bf16[256,4096]{1,0:T(8,128)(2,1)S(1)} %copy-done.7), kind=kLoop, calls=%fused_computation.147 | loop fusion | flops 7340032 | bytes 10485760 | tf_op jit(solution)/shard_map/mul | solution.py:36
  405.5 6.0 %mul.233 = f32[256,4,1024]{2,1,0:T(4,128)} reshape(f32[256,4096]{1,0:T(8,128)} %fusion.91) | data formatting | bytes 8388608 | tf_op jit(solution)/shard_map/mul | solution.py:36
  411.6 2.8 reduce_sum.55
  415.0 3.9 copy.159
  418.9 2.8 multiply_convert_fusion
  (250 shorter events, 62.5 us)
Async XLA Ops:
  7.2 83.6 %all-gather.7.cloned.1.call-start = ((), (), s32[]{:S(2)}) async-start(), calls=%async_computation | async-start | bytes 4456448 | tf_op jit(solution)/shard_map/all_gather | solution.py:137
  9.0 130.7 %all-gather.9.cloned.1.call-start = ((), (), s32[]{:S(2)}) async-start(), calls=%async_computation.1 | async-start | bytes 4456448 | tf_op jit(solution)/shard_map/all_gather | solution.py:138
  10.9 332.9 %all-gather.11.cloned.1.call-start = ((), (), s32[]{:S(2)}) async-start(), calls=%async_computation.2 | async-start | bytes 35651584 | tf_op jit(solution)/shard_map/all_gather | solution.py:20
  16.3 3.5 copy-start.18
  25.2 3.0 copy-start.1
  34.6 3.0 copy-start.1
  44.0 1.3 copy-start
  51.7 7.3 %copy-start.21 = (f32[32]{0:T(128)S(1)}, f32[32]{0:T(128)}, u32[]{:S(2)}) copy-start(f32[32]{0:T(128)} %param.31) | copy-start | bytes 388
  51.7 7.4 %copy-start.20 = (bf16[4096]{0:T(1024)(128)(2,1)S(1)}, bf16[4096]{0:T(1024)(128)(2,1)}, u32[]{:S(2)}) copy-start(bf16[4096]{0:T(1024)(128)(2,1)} %param.32) | copy-start | bytes 24580
  55.9 34.9 %copy-start.8 = (bf16[2,128,4,128]{3,2,1,0:T(4,128)(2,1)}, bf16[2,128,4,128]{3,2,1,0:T(4,128)(2,1)S(1)}, u32[]{:S(2)}) copy-start(bf16[2,128,4,128]{3,2,1,0:T(4,128)(2,1)S(1)} %reshape.119) | copy-start | bytes 786436
  148.5 2.3 copy-start.3
  148.5 2.3 copy-start.14
  151.7 0.8 copy-start.15
  153.3 2.4 copy-start.4
  153.3 2.4 copy-start.16
  156.5 0.8 copy-start.17
  158.1 2.4 copy-start.5
  158.1 2.4 copy-start.12
  161.4 0.8 copy-start.13
  162.9 1.3 copy-start.6
  163.0 1.3 copy-start.10
  165.2 0.8 copy-start.11
  343.7 41.7 %copy-start.9 = (bf16[2,128,4,128]{3,2,1,0:T(4,128)(2,1)S(1)}, bf16[2,128,4,128]{3,2,1,0:T(4,128)(2,1)}, u32[]{:S(2)}) copy-start(bf16[2,128,4,128]{3,2,1,0:T(4,128)(2,1)} %copy-done.8) | copy-start | bytes 786436
  343.7 41.7 %copy-start.19 = (f32[2,4,8]{2,1,0:T(4,128)S(1)}, f32[2,4,8]{2,1,0:T(4,128)}, u32[]{:S(2)}) copy-start(f32[2,4,8]{2,1,0:T(4,128)} %fusion.85) | copy-start | bytes 772
  395.1 5.1 %copy-start.7 = (bf16[256,4096]{1,0:T(8,128)(2,1)S(1)}, bf16[256,4096]{1,0:T(8,128)(2,1)}, u32[]{:S(2)}) copy-start(bf16[256,4096]{1,0:T(8,128)(2,1)} %param.26) | copy-start | bytes 6291460
  415.0 3.9 copy-start.2
Sparse Core Ops, SparseCore 0:
  10.4 64.8 all-gather.6
  77.7 61.9 all-gather.8
  142.2 201.5 all-gather.10
where the time goes:
time: 433 us; the launch traced here: 428 us
  waiting for transfers between devices  170 us (39%)
  local copies, waits for them, and re-layouts  111 us (26%)
  other arithmetic  60.3 us (14%)
  blocking collectives  25.5 us (6%)
  matrix products  25.2 us (6%)
  loops' own time  22.7 us (5%)
  between operations  14 us (3%)
    all_gather x1, waiting for transfers between devices, entering(): pieces = jax.tree.map(lambda part: lax.all_gather(part, axis), value)  121 us
    all_gather x1, waiting for transfers between devices, attend(): value_piece = lax.all_gather(value_rows, 'seq', axis=0, tiled=True)  49 us
    select_n x15, other arithmetic, turn(): jnp.where(position < mine, new, old)  31.4 us
    dynamic_slice x16, local copies, waits for them, and re-layouts, one_block(): value_block = lax.dynamic_slice_in_dim(value_all, offset, block_rows, 0)  25.7 us
    all_gather x1, blocking collectives, entering(): pieces = jax.tree.map(lambda part: lax.all_gather(part, axis), value)  25.5 us
    another operation x1, loops' own time, attend(): result = lax.fori_loop(0, piece_rows // block_rows, one_block, initial)  21.3 us
    unnamed x22, local copies, waits for them, and re-layouts  12.2 us
    dynamic_slice x8, local copies, waits for them, and re-layouts, one_block(): key_block = lax.dynamic_slice_in_dim(key_all, offset, block_rows, 0)  10.5 us
  transfers between devices with their start and end apart: 3, of which 2 were waited for; matrix products, arithmetic and copies ran while one was open for 25% of the time, Pallas kernels for 0%

commit v1 on v0

v1 whole, which is shorter than its diff:
```python
import math

import jax
import jax.numpy as jnp
import numpy as np
from jax import lax
from jax.experimental import pallas as pl
from jax.experimental.pallas import tpu as pltpu
from jax.sharding import Mesh, PartitionSpec as P

SSD_HEADS = 32
GROUPS = 4
PER = SSD_HEADS // GROUPS
D = 128
NQ = 4
KV_HEADS = 4
SIDE = 4
SCALE = (D**-0.5) * math.log2(math.e)
LOG2E = math.log2(math.e)
BF = jnp.bfloat16
F32 = jnp.float32
NEG = -1e30
EXTRA = 8


def params(mib=48):
    return pltpu.CompilerParams(vmem_limit_bytes=mib << 20)


def pack_body(at_ref, *refs):
    ins, outs = refs[:8], refs[8:]
    for s in range(SIDE):
        outs[s][:, :D] = ins[s][...]
        outs[s][:, D:] = ins[SIDE + s][...]


def pack_kv(at, k, v):
    rows = k.shape[0]

    def spec(s):
        return pl.BlockSpec((rows, D), lambda g, at: (0, lax.rem(at[0] + s, SIDE)))

    whole = pl.BlockSpec((rows, 2 * D), lambda g, at: (0, 0))
    return pl.pallas_call(
        pack_body,
        grid_spec=pltpu.PrefetchScalarGridSpec(
            num_scalar_prefetch=1,
            grid=(1,),
            in_specs=[spec(s) for s in range(SIDE)] * 2,
            out_specs=[whole] * SIDE,
        ),
        out_shape=[jax.ShapeDtypeStruct((rows, 2 * D), BF)] * SIDE,
        name="pack_kv",
    )(at, *([k] * SIDE), *([v] * SIDE))


def pack_q_body(at_ref, *refs):
    for s in range(SIDE):
        refs[SIDE + s][...] = refs[s][...]


def pack_q(at, q):
    rows, cols = q.shape
    width = cols // SIDE

    def spec(s):
        return pl.BlockSpec((rows, width), lambda g, at: (0, lax.rem(at[0] + s, SIDE)))

    whole = pl.BlockSpec((rows, width), lambda g, at: (0, 0))
    return pl.pallas_call(
        pack_q_body,
        grid_spec=pltpu.PrefetchScalarGridSpec(
            num_scalar_prefetch=1,
            grid=(1,),
            in_specs=[spec(s) for s in range(SIDE)],
            out_specs=[whole] * SIDE,
        ),
        out_shape=[jax.ShapeDtypeStruct((rows, width), BF)] * SIDE,
        name="pack_q",
    )(at, *([q] * SIDE))


def span_sums(log_decay, span):
    row = lax.rem(lax.broadcasted_iota(jnp.int32, log_decay.shape, 0), span)
    step = 1
    while step < span:
        moved = pltpu.roll(log_decay, step, 0)
        log_decay = log_decay + jnp.where(row >= step, moved, 0.0)
        step *= 2
    return log_decay


def state_body(at_ref, x_ref, w_ref, dt_ref, rate_ref, *rest):
    outs, first_ref, (to_end, total) = rest[:SIDE], rest[SIDE], rest[SIDE + 1 :]
    s = pl.program_id(0)
    rows = dt_ref.shape[0]
    half = rows // 2
    group = lax.rem(at_ref[1] + s, SIDE)

    @pl.when(s == 0)
    def _():
        dt = dt_ref[...]
        sums = span_sums(dt * (-jnp.exp(rate_ref[...])), half)
        ends = jnp.concatenate(
            [jnp.broadcast_to(sums[half * c + half - 1 : half * c + half], (half, SSD_HEADS)) for c in range(2)],
            axis=0,
        )
        to_end[...] = jnp.exp(ends - sums) * dt
        total[0:8, :] = ends[half : half + 8]
        total[8:16, :] = ends[:8] + ends[half : half + 8]

    for g in range(GROUPS):

        @pl.when(group == g)
        def _():
            scaled, last, decays = [], [], []
            for j in range(PER):
                h = g * PER + j
                scaled.append(
                    (to_end[:, h : h + 1] * x_ref[:, j * D : (j + 1) * D].astype(F32)).astype(BF)
                )
                last.append(jnp.broadcast_to(total[0:1, h : h + 1], (1, D)))
                decays.append(jnp.broadcast_to(total[8:16, h : h + 1], (8, D)))
            scaled = jnp.concatenate(scaled, axis=1)
            first, second = [
                lax.dot_general(
                    w_ref[c * half : (c + 1) * half, :],
                    scaled[c * half : (c + 1) * half],
                    (((0,), (0,)), ((), ())),
                    preferred_element_type=F32,
                )
                for c in range(2)
            ]
            first_ref[0] = first
            state = jnp.exp(jnp.concatenate(last, axis=1)) * first + second
            decay = jnp.concatenate(decays, axis=1)
            for t in range(SIDE):

                @pl.when(s == t)
                def _():
                    outs[t][:D, :] = state
                    outs[t][D:, :] = decay


def local_states(at, x, w, dt, rate):
    rows = x.shape[0]
    width = PER * D
    return pl.pallas_call(
        state_body,
        grid_spec=pltpu.PrefetchScalarGridSpec(
            num_scalar_prefetch=1,
            grid=(SIDE,),
            in_specs=[
                pl.BlockSpec((rows, width), lambda s, at: (0, lax.rem(at[1] + s, SIDE))),
                pl.BlockSpec((rows, D), lambda s, at: (0, lax.rem(at[1] + s, SIDE))),
                pl.BlockSpec((rows, SSD_HEADS), lambda s, at: (0, 0)),
                pl.BlockSpec((1, SSD_HEADS), lambda s, at: (0, 0)),
            ],
            out_specs=[pl.BlockSpec((D + EXTRA, width), lambda s, at: (0, 0))] * SIDE
            + [pl.BlockSpec((1, D, width), lambda s, at: (s, 0, 0))],
            scratch_shapes=[pltpu.VMEM((rows, SSD_HEADS), F32), pltpu.VMEM((16, SSD_HEADS), F32)],
        ),
        out_shape=[jax.ShapeDtypeStruct((D + EXTRA, width), F32)] * SIDE
        + [jax.ShapeDtypeStruct((SIDE, D, width), F32)],
        compiler_params=params(),
        name="local_states",
    )(at, x, w, dt, rate)


def flag(condition):
    return jnp.where(condition, 1.0, 0.0).astype(F32)


def row_total_body(at_ref, *refs):
    ins, outs, total = refs[:SIDE], refs[SIDE : 2 * SIDE], refs[2 * SIDE]
    x, y = at_ref[0], at_ref[1]
    place = [lax.rem(y - s + SIDE, SIDE) for s in range(SIDE)]
    logs = [ref[D : D + 1, :] for ref in ins]
    value = None
    for s in range(SIDE):
        later = sum(flag(place[u] > place[s]) * logs[u] for u in range(SIDE) if u != s)
        term = ins[s][:D, :] * jnp.exp(later)
        value = term if value is None else value + term
    total[:D, :] = value
    total[D:, :] = jnp.broadcast_to(logs[0] + logs[1] + logs[2] + logs[3], (EXTRA, value.shape[1]))
    width = value.shape[1] // SIDE
    for s in range(SIDE):
        begin = pl.multiple_of(lax.rem(x + s, SIDE) * width, width)
        outs[s][...] = total[:, pl.ds(begin, width)]


def row_total(at, states):
    rows, width = states[0].shape
    return pl.pallas_call(
        row_total_body,
        in_specs=[pl.BlockSpec(memory_space=pltpu.SMEM)] + [pl.BlockSpec(memory_space=pltpu.VMEM)] * SIDE,
        out_specs=[pl.BlockSpec(memory_space=pltpu.VMEM)] * SIDE,
        out_shape=[jax.ShapeDtypeStruct((rows, width // SIDE), F32)] * SIDE,
        scratch_shapes=[pltpu.VMEM((rows, width), F32)],
        compiler_params=params(),
        name="row_total",
    )(at, *states)


def entering_body(at_ref, *refs):
    ins, outs = refs[:SIDE], refs[SIDE:]
    prefixes(at_ref[0], ins, outs, None)


def prefixes(mine, ins, outs, entering):
    place = [lax.rem(mine - s + SIDE, SIDE) for s in range(SIDE)]
    logs = [ref[D : D + 1, :] for ref in ins]
    for t in range(SIDE):
        if entering is None:
            state = jnp.zeros((D, ins[0].shape[1]), F32)
        else:
            before = sum(flag(place[u] < place[t]) * logs[u] for u in range(SIDE) if u != t)
            state = jnp.exp(before) * entering
        for s in range(SIDE):
            if s == t:
                continue
            gap = sum(
                flag((place[u] > place[s]) & (place[u] < place[t])) * logs[u]
                for u in range(SIDE)
                if u != t and u != s
            )
            state = state + (flag(place[s] < place[t]) * jnp.exp(gap)) * ins[s][:D, :]
        outs[t][...] = state


def entering_rows(at, totals):
    width = totals[0].shape[1]
    return pl.pallas_call(
        entering_body,
        in_specs=[pl.BlockSpec(memory_space=pltpu.SMEM)] + [pl.BlockSpec(memory_space=pltpu.VMEM)] * SIDE,
        out_specs=[pl.BlockSpec(memory_space=pltpu.VMEM)] * SIDE,
        out_shape=[jax.ShapeDtypeStruct((D, width), F32)] * SIDE,
        compiler_params=params(),
        name="entering_rows",
    )(at, *totals)


def starts_body(at_ref, *refs):
    ins, pieces = refs[:SIDE], refs[SIDE : 2 * SIDE]
    outs, whole = refs[2 * SIDE : 3 * SIDE], refs[3 * SIDE]
    width = pieces[0].shape[1]
    for s in range(SIDE):
        begin = pl.multiple_of(lax.rem(at_ref[0] + s, SIDE) * width, width)
        whole[:, pl.ds(begin, width)] = pieces[s][...]
    prefixes(at_ref[1], ins, outs, whole[...])


def start_states(at, states, entering):
    width = states[0].shape[1]
    return pl.pallas_call(
        starts_body,
        in_specs=[pl.BlockSpec(memory_space=pltpu.SMEM)]
        + [pl.BlockSpec(memory_space=pltpu.VMEM)] * (2 * SIDE),
        out_specs=[pl.BlockSpec(memory_space=pltpu.VMEM)] * SIDE,
        out_shape=[jax.ShapeDtypeStruct((D, width), F32)] * SIDE,
        scratch_shapes=[pltpu.VMEM((D, width), F32)],
        compiler_params=params(),
        name="start_states",
    )(at, *states, *entering)


def ssd_body(
    at_ref, x_ref, gate_ref, w_ref, r_ref, dt_ref, rate_ref, skip_ref, gain_ref, first_ref, *rest
):
    starts, out_ref, (cum, cum_t, ends, gated) = rest[:SIDE], rest[SIDE], rest[SIDE + 1 :]
    s = pl.program_id(0)
    rows = dt_ref.shape[0]
    half = rows // 2
    group = lax.rem(at_ref[1] + s, SIDE)

    @pl.when(s == 0)
    def _():
        dt = dt_ref[...]
        sums = span_sums(dt * (-jnp.exp(rate_ref[...])), half)
        cum[...] = sums * LOG2E
        cum_t[...] = jnp.transpose((sums - jnp.log(dt)) * LOG2E)
        ends[...] = jnp.broadcast_to(sums[half - 1 : half], ends.shape)

    row = lax.broadcasted_iota(jnp.int32, (half, half), 0)
    col = lax.broadcasted_iota(jnp.int32, (half, half), 1)
    causal = col <= row
    spans = [slice(c * half, (c + 1) * half) for c in range(2)]
    pairs = [
        lax.dot_general(
            r_ref[span, :], w_ref[span, :], (((1,), (1,)), ((), ())), preferred_element_type=F32
        )
        for span in spans
    ]

    for g in range(GROUPS):

        @pl.when(group == g)
        def _():
            decay = jnp.exp(
                jnp.concatenate(
                    [
                        jnp.broadcast_to(ends[0:1, g * PER + j : g * PER + j + 1], (1, D))
                        for j in range(PER)
                    ],
                    axis=1,
                )
            )
            for t in range(SIDE):

                @pl.when(s == t)
                def _():
                    start = starts[t][...]
                    gated[spans[0], :] = jnp.dot(
                        r_ref[spans[0], :], start.astype(BF), preferred_element_type=F32
                    )
                    gated[spans[1], :] = jnp.dot(
                        r_ref[spans[1], :],
                        (decay * start + first_ref[0]).astype(BF),
                        preferred_element_type=F32,
                    )

            square = jnp.zeros((rows, D), F32)
            for j in range(PER):
                h = g * PER + j
                lanes = slice(j * D, (j + 1) * D)
                down = jnp.broadcast_to(cum[:, h : h + 1], (rows, D))
                x = x_ref[:, lanes]
                mixed = []
                for c, span in enumerate(spans):
                    weights = pairs[c] * jnp.exp2(down[span] - cum_t[h : h + 1, span])
                    weights = jnp.where(causal, weights, 0.0).astype(BF)
                    mixed.append(jnp.dot(weights, x[span], preferred_element_type=F32))
                mixed = jnp.concatenate(mixed, axis=0)
                mixed = mixed + jnp.exp2(down) * gated[:, lanes] + skip_ref[0, h] * x.astype(F32)
                gate = gate_ref[:, lanes].astype(F32)
                value = mixed * (gate * (0.5 + 0.5 * jnp.tanh(0.5 * gate)))
                gated[:, lanes] = value
                square = square + value * value
            mean = jnp.sum(square, axis=1, keepdims=True) * (1.0 / (PER * D))
            inverse = lax.rsqrt(mean + 1e-05)
            for j in range(PER):
                lanes = slice(j * D, (j + 1) * D)
                out_ref[:, lanes] = (
                    gated[:, lanes] * inverse * gain_ref[:, lanes].astype(F32)
                ).astype(BF)


def ssd_out_of(at, x, gate, w, r, dt, rate, skip, gain, first, starts):
    rows = x.shape[0]
    width = PER * D

    def turned(s, at):
        return (0, lax.rem(at[1] + s, SIDE))

    def fixed(s, at):
        return (0, 0)

    return pl.pallas_call(
        ssd_body,
        grid_spec=pltpu.PrefetchScalarGridSpec(
            num_scalar_prefetch=1,
            grid=(SIDE,),
            in_specs=[
                pl.BlockSpec((rows, width), turned),
                pl.BlockSpec((rows, width), turned),
                pl.BlockSpec((rows, D), turned),
                pl.BlockSpec((rows, D), turned),
                pl.BlockSpec((rows, SSD_HEADS), fixed),
                pl.BlockSpec((1, SSD_HEADS), fixed),
                pl.BlockSpec(memory_space=pltpu.SMEM),
                pl.BlockSpec((1, width), turned),
                pl.BlockSpec((1, D, width), lambda s, at: (s, 0, 0)),
            ]
            + [pl.BlockSpec((D, width), fixed)] * SIDE,
            out_specs=pl.BlockSpec((rows, width), turned),
            scratch_shapes=[
                pltpu.VMEM((rows, SSD_HEADS), F32),
                pltpu.VMEM((SSD_HEADS, rows), F32),
                pltpu.VMEM((8, SSD_HEADS), F32),
                pltpu.VMEM((rows, width), F32),
            ],
        ),
        out_shape=jax.ShapeDtypeStruct(x.shape, BF),
        compiler_params=params(),
        name="ssd_out",
    )(at, x, gate, w, r, dt, rate, skip, gain, first, *starts)


def attn_body(qi_ref, ci_ref, at_ref, q_ref, *rest):
    parts, o_ref, (qs, kk, va, acc, top) = rest[:SIDE], rest[SIDE], rest[SIDE + 1 :]
    step = pl.program_id(0)
    qi = qi_ref[step]
    ci = ci_ref[step]
    x = at_ref[0]
    y = at_ref[1]
    rows = q_ref.shape[0]
    keys = SIDE * rows

    @pl.when(step == 0)
    def _():
        for u in range(SIDE):
            for c in range(SIDE):
                source = slice(c * rows, (c + 1) * rows)
                to = slice(c * keys + u * rows, c * keys + (u + 1) * rows)
                kk[to, :D] = parts[u][source, :D]
                kk[to, D:] = parts[u][source, :D]
                va[to, :D] = parts[u][source, D:]
        va[:, D:] = jnp.ones((SIDE * keys, D), BF)

    @pl.when(ci == 0)
    def _():
        for h in range(NQ):
            q = q_ref[:, h * D : (h + 1) * D].astype(F32) * SCALE
            hi = q.astype(BF)
            qs[h * rows : (h + 1) * rows, :D] = hi
            qs[h * rows : (h + 1) * rows, D:] = (q - hi.astype(F32)).astype(BF)
        acc[...] = jnp.zeros_like(acc)
        top[...] = jnp.full_like(top, NEG)

    slot = lax.rem(x - ci + SIDE, SIDE)
    where = pl.ds(pl.multiple_of(slot * keys, keys), keys)

    def run(masked):
        kc = kk.at[where, :]
        vc = va.at[where, :]
        if masked:
            key = lax.broadcasted_iota(jnp.int32, (rows, rows), 1)
            query = lax.broadcasted_iota(jnp.int32, (rows, rows), 0)
            ahead = key - query

        def scores(h):
            mine = qs[h * rows : (h + 1) * rows, :]
            pieces = []
            for u in range(SIDE):
                piece = lax.dot_general(
                    mine,
                    kc[u * rows : (u + 1) * rows, :],
                    (((1,), (1,)), ((), ())),
                    preferred_element_type=F32,
                )
                if masked:
                    behind = (y - lax.rem(y - u + SIDE, SIDE)) * rows
                    piece = jnp.where(ahead <= behind, piece, NEG)
                pieces.append(piece)
            return jnp.concatenate(pieces, axis=1)

        now = scores(0)
        for h in range(NQ):
            following = scores(h + 1) if h + 1 < NQ else None
            mine = slice(h * rows, (h + 1) * rows)
            old = top[mine, :]
            new = jnp.maximum(old, jnp.max(now, axis=1, keepdims=True))
            factor = jnp.exp2(old - new)
            weights = jnp.exp2(now - new[:, :1]).astype(BF)
            top[mine, :] = new
            out = acc[mine, :] * jnp.concatenate([factor, factor], axis=1)
            for u in range(SIDE):
                out = out + jnp.dot(
                    weights[:, u * rows : (u + 1) * rows],
                    vc[u * rows : (u + 1) * rows, :],
                    preferred_element_type=F32,
                )
            acc[mine, :] = out
            now = following

    @pl.when(ci < qi)
    def _():
        run(False)

    @pl.when(ci == qi)
    def _():
        run(True)
        for h in range(NQ):
            mine = slice(h * rows, (h + 1) * rows)
            o_ref[:, h * D : (h + 1) * D] = (acc[mine, :D] / acc[mine, D:]).astype(BF)


def attention(at, q, parts):
    rows = q.shape[0] // SIDE
    width = q.shape[1]
    keys = parts[0].shape[0]
    order = [(a, c) for a in range(SIDE) for c in range(a + 1)]
    qi = np.array([a for a, _ in order], np.int32)
    ci = np.array([c for _, c in order], np.int32)

    def turned(step, qi, ci, at):
        return (lax.rem(at[0] - qi[step] + SIDE, SIDE), 0)

    return pl.pallas_call(
        attn_body,
        grid_spec=pltpu.PrefetchScalarGridSpec(
            num_scalar_prefetch=3,
            grid=(len(order),),
            in_specs=[pl.BlockSpec((rows, width), turned)]
            + [pl.BlockSpec((keys, 2 * D), lambda step, qi, ci, at: (0, 0))] * SIDE,
            out_specs=pl.BlockSpec((rows, width), turned),
            scratch_shapes=[
                pltpu.VMEM((NQ * rows, 2 * D), BF),
                pltpu.VMEM((SIDE * keys, 2 * D), BF),
                pltpu.VMEM((SIDE * keys, 2 * D), BF),
                pltpu.VMEM((NQ * rows, 2 * D), F32),
                pltpu.VMEM((NQ * rows, D), F32),
            ],
        ),
        out_shape=jax.ShapeDtypeStruct(q.shape, BF),
        compiler_params=params(),
        name="attention",
    )(jnp.asarray(qi), jnp.asarray(ci), at, q, *parts)


def unpack_body(at_ref, *refs):
    ins, out = refs[:SIDE], refs[SIDE]
    s = pl.program_id(0)
    for t in range(SIDE):

        @pl.when(s == t)
        def _():
            out[...] = ins[t][...]


def unpack(at, pieces):
    rows, width = pieces[0].shape
    return pl.pallas_call(
        unpack_body,
        grid_spec=pltpu.PrefetchScalarGridSpec(
            num_scalar_prefetch=1,
            grid=(SIDE,),
            in_specs=[pl.BlockSpec((rows, width), lambda s, at: (0, 0))] * SIDE,
            out_specs=pl.BlockSpec((rows, width), lambda s, at: (0, lax.rem(at[0] + s, SIDE))),
        ),
        out_shape=jax.ShapeDtypeStruct((rows, SIDE * width), BF),
        name="unpack",
    )(at, *pieces)


def shifted(value, axis, by):
    return lax.ppermute(value, axis, [(i, (i + by) % SIDE) for i in range(SIDE)])


def exchange(pieces, axis, sign):
    return [pieces[0]] + [shifted(pieces[s], axis, sign * s) for s in range(1, SIDE)]


def gather_ring(own, axis):
    middle = own.shape[0] // 2
    before = shifted(own, axis, 1)
    after = shifted(own, axis, -1)
    top = shifted(before[:middle], axis, 1)
    bottom = shifted(after[middle:], axis, -1)
    return [own, before, jnp.concatenate([top, bottom], axis=0), after]


def local(
    ssd_input, gate_input, write_map, read_map, step_size, decay_log, skip_gain, norm_gain,
    query_rows, key_rows, value_rows,
):
    at = jnp.stack([lax.axis_index("x"), lax.axis_index("y")]).astype(jnp.int32)
    rate = decay_log.reshape(1, -1)
    skip = skip_gain.reshape(1, -1)
    gain = norm_gain.reshape(1, -1)
    kv = exchange(pack_kv(at, key_rows, value_rows), "x", 1)
    *states, first = local_states(at, ssd_input, write_map, step_size, rate)
    states = exchange(states, "y", 1)
    queries = exchange(pack_q(at, query_rows), "x", 1)
    own = jnp.concatenate(kv, axis=0)
    parts = gather_ring(own, "y")
    totals = exchange(row_total(at, states), "x", 1)
    entering = exchange(entering_rows(at, totals), "x", -1)
    starts = exchange(start_states(at, states, entering), "y", -1)
    q_all = jnp.concatenate(queries, axis=0)
    attended = attention(at, q_all, parts)
    rows = query_rows.shape[0]
    back = exchange([attended[s * rows : (s + 1) * rows] for s in range(SIDE)], "x", -1)
    ssd = ssd_out_of(
        at, ssd_input, gate_input, write_map, read_map, step_size, rate, skip, gain, first, starts
    )
    return (ssd, unpack(at, back))


def solution(mesh):
    grid = Mesh(mesh.devices.reshape(-1, SIDE, SIDE), ("dp", "x", "y"))
    split = P(("dp", "x", "y"), None)
    in_specs = (split,) * 5 + (P(), P(), P()) + (split,) * 3
    return jax.shard_map(
        local, mesh=grid, in_specs=in_specs, out_specs=(split, split), check_vma=False
    )
```

time: 433 us -> 140 us (0.32)
  waiting for transfers between devices: 170 us -> 35 us
  local copies, waits for them, and re-layouts: 111 us -> 7.45 us
  other arithmetic: 60.3 us -> 0.75 us
  Pallas kernels: 0 us -> 50.2 us
  starting transfers between devices: 0.12 us -> 45 us
  blocking collectives: 25.5 us -> 0 us
  matrix products: 25.2 us -> 0 us
  loops' own time: 22.7 us -> 0 us
  between operations: 14 us -> 0.96 us
    all_gather x3 -> x0, waiting for transfers between devices: 170 us -> none  [the longest x1 121 us: entering(): pieces = jax.tree.map(lambda part: lax.all_gather(part, axis), value)]
    pallas_call x0 -> x9, Pallas kernels: none -> 50.2 us  [the longest x1 21 us: attention(): pl.pallas_call(attn_body, grid_spec=pltpu.PrefetchScalarGridSpec(num_scal...]
    ppermute x0 -> x25, starting transfers between devices: none -> 45 us  [shifted(): lax.ppermute(value, axis, [(i, (i + by) % SIDE) for i in range(SIDE)])]
    dynamic_slice x28 -> x0, local copies, waits for them, and re-layouts: 45 us -> none  [the longest x16 25.7 us: one_block(): value_block = lax.dynamic_slice_in_dim(value_all, offset, block_rows, 0)]
    ppermute x0 -> x25, waiting for transfers between devices: none -> 35 us  [shifted(): lax.ppermute(value, axis, [(i, (i + by) % SIDE) for i in range(SIDE)])]
    select_n x15 -> x0, other arithmetic: 31.4 us -> none  [turn(): jnp.where(position < mine, new, old)]
    all_gather x1 -> x0, blocking collectives: 25.5 us -> none  [entering(): pieces = jax.tree.map(lambda part: lax.all_gather(part, axis), value)]
    dot_general x12 -> x0, matrix products: 25.2 us -> none  [the longest x1 5.42 us: ssd_local(): jnp.einsum('csgn,csgjp->cgjnp', write_vals, scaled, preferred_element_typ...]
  transfers between devices with their start and end apart: 3 -> 25, of which waited for: 2 -> 10; matrix products, arithmetic and copies ran while one was open for 25% -> 3% of each run, Pallas kernels for 0% -> 27%
where the time goes in v1:
time: 140 us; the launch traced here: 139 us
  Pallas kernels  50.2 us (36%)
  starting transfers between devices  45 us (32%)
  waiting for transfers between devices  35 us (25%)
  local copies, waits for them, and re-layouts  7.45 us (5%)
    ppermute x25, starting transfers between devices, shifted(): lax.ppermute(value, axis, [(i, (i + by) % SIDE) for i in range(SIDE)])  45 us
    ppermute x25, waiting for transfers between devices, shifted(): lax.ppermute(value, axis, [(i, (i + by) % SIDE) for i in range(SIDE)])  35 us
    pallas_call x1, Pallas kernels, attention(): pl.pallas_call(attn_body, grid_spec=pltpu.PrefetchScalarGridSpec(num_scal...  21 us
    pallas_call x1, Pallas kernels, ssd_out_of(): pl.pallas_call(ssd_body, grid_spec=pltpu.PrefetchScalarGridSpec(num_scala...  9.94 us
    pallas_call x1, Pallas kernels, local_states(): pl.pallas_call(state_body, grid_spec=pltpu.PrefetchScalarGridSpec(num_sca...  6.09 us
    unnamed x54, local copies, waits for them, and re-layouts  5.02 us
    pallas_call x1, Pallas kernels, unpack(): pl.pallas_call(unpack_body, grid_spec=pltpu.PrefetchScalarGridSpec(num_sc...  3.43 us
    pallas_call x1, Pallas kernels, pack_q(): pl.pallas_call(pack_q_body, grid_spec=pltpu.PrefetchScalarGridSpec(num_sc...  2.88 us
  transfers between devices with their start and end apart: 25, of which 10 were waited for; matrix products, arithmetic and copies ran while one was open for 3% of the time, Pallas kernels for 27%

profile of v1, /device:TPU:64, one launch (start us, length us, event | category | flops | bytes accessed | tf_op | source)
XLA Modules:
  0.0 139.4 jit_solution(4982284429263365773)
XLA Ops:
  0.6 0.0 copy-start.6
  0.7 0.7 pad_add_fusion.at_ref
  1.3 2.8 %pack_kv.1 = (bf16[256,256]{1,0:T(8,128)(2,1)}, bf16[256,256]{1,0:T(8,128)(2,1)}, bf16[256,256]{1,0:T(8,128)(2,1)}, bf16[256,256]{1,0:T(8,128)(2,1)}) custom-call(s32[2]{0:T(128)} %pad_add_fusion.at_ref, bf16[256,512]{1,0:T(8,128)(2,1)} %refs_3_.3, bf16[256,512]{1,0:T(8,128)(2,1)} %refs_3_.3, bf16[256,512]{1,0:T(8,128)(2,1)} %refs_3_.3, ...), custom_call_target="tpu_custom_call" | custom-call | tf_op jit(solution)/shard_map/pack_kv/pallas_call | solution.py:44
  4.1 1.6 %collective-permute-start.15 = (bf16[256,256]{1,0:T(8,128)(2,1)}, bf16[256,256]{1,0:T(8,128)(2,1)S(1)}, u32[]{:S(2)}, u32[]{:S(2)}) collective-permute-start(bf16[256,256]{1,0:T(8,128)(2,1)} %get-tuple-element.49), channel_id=1, source_target_pairs={{0,4},{4,8},{8,12},{12,0},{1,5},{5,9},{9,13},{13,1},{2,6},{6,10},{... | collective-permute-start | bytes 393224 | tf_op jit(solution)/shard_map/ppermute | solution.py:537
  5.7 0.1 copy.16.dt_ref
  5.8 6.1 %local_states.1 = (f32[136,1024]{1,0:T(8,128)S(1)}, f32[136,1024]{1,0:T(8,128)}, f32[136,1024]{1,0:T(8,128)}, f32[136,1024]{1,0:T(8,128)}, f32[4,128,1024]{2,1,0:T(8,128)S(1)}) custom-call(s32[2]{0:T(128)S(1)} %copy-done.11, bf16[256,4096]{1,0:T(8,128)(2,1)} %x_ref.3, bf16[256,512]{1,0:T(8,128)(2,1)S(1)} %copy-done.6, f32[256,32]{1,0:T(8,128)S(1)} %copy.16.dt_ref, ...), custom_call_target="tpu_custom_call" | custom-call | tf_op jit(solution)/shard_map/local_states/pallas_call | solution.py:148
  11.9 1.3 copy-done.5
  13.2 1.6 %collective-permute-start = (f32[136,1024]{1,0:T(8,128)}, f32[136,1024]{1,0:T(8,128)S(1)}, u32[]{:S(2)}, u32[]{:S(2)}) collective-permute-start(f32[136,1024]{1,0:T(8,128)} %get-tuple-element.29), channel_id=1, source_target_pairs={{0,1},{1,2},{2,3},{3,0},{4,5},{5,6},{6,7},{7,4},{8,9},{9,10},{10,1... | collective-permute-start | bytes 1671176 | tf_op jit(solution)/shard_map/ppermute | solution.py:537
  14.8 2.7 %collective-permute-start.16 = (bf16[256,256]{1,0:T(8,128)(2,1)S(1)}, bf16[256,256]{1,0:T(8,128)(2,1)S(1)}, u32[]{:S(2)}, u32[]{:S(2)}) collective-permute-start(bf16[256,256]{1,0:T(8,128)(2,1)S(1)} %copy-done.24), channel_id=1, source_target_pairs={{0,8},{4,12},{8,0},{12,4},{1,9},{5,13},{9,1},{13,5},{2,10},{6,14},... | collective-permute-start | bytes 393224 | tf_op jit(solution)/shard_map/ppermute | solution.py:537
  17.6 1.4 %collective-permute-start.17 = (bf16[256,256]{1,0:T(8,128)(2,1)S(1)}, bf16[256,256]{1,0:T(8,128)(2,1)S(1)}, u32[]{:S(2)}, u32[]{:S(2)}) collective-permute-start(bf16[256,256]{1,0:T(8,128)(2,1)S(1)} %copy-done.23), channel_id=1, source_target_pairs={{0,12},{4,0},{8,4},{12,8},{1,13},{5,1},{9,5},{13,9},{2,14},{6,2},{... | collective-permute-start | bytes 393224 | tf_op jit(solution)/shard_map/ppermute | solution.py:537
  19.0 0.7 constant_dynamic-update-slice_fusion.3
  19.7 0.7 constant_dynamic-update-slice_fusion.2
  20.3 1.0 collective-permute-done.16
  21.3 0.6 constant_dynamic-update-slice_fusion.1
  22.0 1.2 collective-permute-done.17
  23.2 0.7 constant_dynamic-update-slice_fusion.rest_0_
  23.9 1.6 %collective-permute-start.18 = (bf16[1024,256]{1,0:T(8,128)(2,1)}, bf16[1024,256]{1,0:T(8,128)(2,1)S(1)}, u32[]{:S(2)}, u32[]{:S(2)}) collective-permute-start(bf16[1024,256]{1,0:T(8,128)(2,1)} %constant_dynamic-update-slice_fusion.rest_0_), channel_id=1, source_target_pairs={{0,1},{1,2},{2,3},{3,0},{4,5},{5,6},{6,7},{7,4},{8,9},{9,10},{10,1... | collective-permute-start | bytes 1572872 | tf_op jit(solution)/shard_map/ppermute | solution.py:537
  25.4 1.7 %collective-permute-start.20 = (bf16[1024,256]{1,0:T(8,128)(2,1)}, bf16[1024,256]{1,0:T(8,128)(2,1)}, u32[]{:S(2)}, u32[]{:S(2)}) collective-permute-start(bf16[1024,256]{1,0:T(8,128)(2,1)} %constant_dynamic-update-slice_fusion.rest_0_), channel_id=1, source_target_pairs={{0,3},{1,0},{2,1},{3,2},{4,7},{5,4},{6,5},{7,6},{8,11},{9,8},{10,9... | collective-permute-start | bytes 1572872 | tf_op jit(solution)/shard_map/ppermute | solution.py:537
  27.1 1.7 %collective-permute-start.1 = (f32[136,1024]{1,0:T(8,128)}, f32[136,1024]{1,0:T(8,128)S(1)}, u32[]{:S(2)}, u32[]{:S(2)}) collective-permute-start(f32[136,1024]{1,0:T(8,128)} %get-tuple-element.30), channel_id=1, source_target_pairs={{0,2},{1,3},{2,0},{3,1},{4,6},{5,7},{6,4},{7,5},{8,10},{9,11},{10,... | collective-permute-start | bytes 1671176 | tf_op jit(solution)/shard_map/ppermute | solution.py:537
  28.8 1.4 collective-permute-start.2
  30.1 2.9 %pack_q.1 = (bf16[256,512]{1,0:T(8,128)(2,1)}, bf16[256,512]{1,0:T(8,128)(2,1)}, bf16[256,512]{1,0:T(8,128)(2,1)}, bf16[256,512]{1,0:T(8,128)(2,1)}) custom-call(s32[2]{0:T(128)} %pad_add_fusion.at_ref, bf16[256,2048]{1,0:T(8,128)(2,1)} %refs_3_.2, bf16[256,2048]{1,0:T(8,128)(2,1)} %refs_3_.2, bf16[256,2048]{1,0:T(8,128)(2,1)} %refs_3_.2, ...), custom_call_target="tpu_custom_call" | custom-call | tf_op jit(solution)/shard_map/pack_q/pallas_call | solution.py:70
  33.0 0.0 collective-permute-done.refs_1_
  33.0 2.7 %collective-permute-start.14 = (bf16[256,512]{1,0:T(8,128)(2,1)}, bf16[256,512]{1,0:T(8,128)(2,1)S(1)}, u32[]{:S(2)}, u32[]{:S(2)}) collective-permute-start(bf16[256,512]{1,0:T(8,128)(2,1)} %get-tuple-element.47), channel_id=1, source_target_pairs={{0,12},{4,0},{8,4},{12,8},{1,13},{5,1},{9,5},{13,9},{2,14},{6,2},{... | collective-permute-start | bytes 786440 | tf_op jit(solution)/shard_map/ppermute | solution.py:537
  35.8 4.6 %collective-permute-done.18.rest_1_ = bf16[1024,256]{1,0:T(8,128)(2,1)S(1)} collective-permute-done((bf16[1024,256]{1,0:T(8,128)(2,1)}, bf16[1024,256]{1,0:T(8,128)(2,1)S(1)}, u32[]{:S(2)}, u32[]{:S(2)}) %collective-permute-start.18) | collective-permute-done | bytes 524320 | tf_op jit(solution)/shard_map/ppermute | solution.py:537
  40.3 2.7 %collective-permute-start.13 = (bf16[256,512]{1,0:T(8,128)(2,1)}, bf16[256,512]{1,0:T(8,128)(2,1)S(1)}, u32[]{:S(2)}, u32[]{:S(2)}) collective-permute-start(bf16[256,512]{1,0:T(8,128)(2,1)} %get-tuple-element.46), channel_id=1, source_target_pairs={{0,8},{4,12},{8,0},{12,4},{1,9},{5,13},{9,1},{13,5},{2,10},{6,14},... | collective-permute-start | bytes 786440 | tf_op jit(solution)/shard_map/ppermute | solution.py:537
  43.1 8.3 %collective-permute-done.20.rest_3_ = bf16[1024,256]{1,0:T(8,128)(2,1)} collective-permute-done((bf16[1024,256]{1,0:T(8,128)(2,1)}, bf16[1024,256]{1,0:T(8,128)(2,1)}, u32[]{:S(2)}, u32[]{:S(2)}) %collective-permute-start.20) | collective-permute-done | bytes 524320 | tf_op jit(solution)/shard_map/ppermute | solution.py:537
  51.4 1.5 %collective-permute-start.12 = (bf16[256,512]{1,0:T(8,128)(2,1)}, bf16[256,512]{1,0:T(8,128)(2,1)S(1)}, u32[]{:S(2)}, u32[]{:S(2)}) collective-permute-start(bf16[256,512]{1,0:T(8,128)(2,1)} %get-tuple-element.45), channel_id=1, source_target_pairs={{0,4},{4,8},{8,12},{12,0},{1,5},{5,9},{9,13},{13,1},{2,6},{6,10},{... | collective-permute-start | bytes 786440 | tf_op jit(solution)/shard_map/ppermute | solution.py:537
  52.8 1.0 slice.25
  53.8 0.0 copy-start.1
  53.9 4.1 %collective-permute-start.21 = (bf16[512,256]{1,0:T(8,128)(2,1)S(1)}, bf16[512,256]{1,0:T(8,128)(2,1)S(1)}, u32[]{:S(2)}, u32[]{:S(2)}) collective-permute-start(bf16[512,256]{1,0:T(8,128)(2,1)S(1)} %slice.25), channel_id=1, source_target_pairs={{0,3},{1,0},{2,1},{3,2},{4,7},{5,4},{6,5},{7,6},{8,11},{9,8},{10,9... | collective-permute-start | bytes 786440 | tf_op jit(solution)/shard_map/ppermute | solution.py:537
  58.0 6.4 %collective-permute-done.2.refs_3_ = f32[136,1024]{1,0:T(8,128)S(1)} collective-permute-done((f32[136,1024]{1,0:T(8,128)}, f32[136,1024]{1,0:T(8,128)S(1)}, u32[]{:S(2)}, u32[]{:S(2)}) %collective-permute-start.2) | collective-permute-done | bytes 557088 | tf_op jit(solution)/shard_map/ppermute | solution.py:537
  64.4 1.2 collective-permute-start.19
  65.7 0.9 row_total.1
  66.5 0.0 copy-start.16
  66.6 0.0 copy-start.17
  66.6 1.5 %collective-permute-start.3 = (f32[136,256]{1,0:T(8,128)S(1)}, f32[136,256]{1,0:T(8,128)S(1)}, u32[]{:S(2)}, u32[]{:S(2)}) collective-permute-start(f32[136,256]{1,0:T(8,128)S(1)} %get-tuple-element.33), channel_id=1, source_target_pairs={{0,4},{4,8},{8,12},{12,0},{1,5},{5,9},{9,13},{13,1},{2,6},{6,10},{... | collective-permute-start | bytes 417800 | tf_op jit(solution)/shard_map/ppermute | solution.py:537
  68.1 2.7 %collective-permute-start.4 = (f32[136,256]{1,0:T(8,128)S(1)}, f32[136,256]{1,0:T(8,128)S(1)}, u32[]{:S(2)}, u32[]{:S(2)}) collective-permute-start(f32[136,256]{1,0:T(8,128)S(1)} %get-tuple-element.34), channel_id=1, source_target_pairs={{0,8},{4,12},{8,0},{12,4},{1,9},{5,13},{9,1},{13,5},{2,10},{6,14},... | collective-permute-start | bytes 417800 | tf_op jit(solution)/shard_map/ppermute | solution.py:537
  70.8 1.2 collective-permute-start.5
  72.0 0.1 pad_maximum_fusion.q_ref
  72.1 0.8 collective-permute-done.3.refs_1_
  72.9 2.4 %collective-permute-done.4.refs_2_ = f32[136,256]{1,0:T(8,128)S(1)} collective-permute-done((f32[136,256]{1,0:T(8,128)S(1)}, f32[136,256]{1,0:T(8,128)S(1)}, u32[]{:S(2)}, u32[]{:S(2)}) %collective-permute-start.4) | collective-permute-done | bytes 139296 | tf_op jit(solution)/shard_map/ppermute | solution.py:537
  75.3 2.2 %collective-permute-done.5.refs_3_ = f32[136,256]{1,0:T(8,128)S(1)} collective-permute-done((f32[136,256]{1,0:T(8,128)S(1)}, f32[136,256]{1,0:T(8,128)S(1)}, u32[]{:S(2)}, u32[]{:S(2)}) %collective-permute-start.5) | collective-permute-done | bytes 139296 | tf_op jit(solution)/shard_map/ppermute | solution.py:537
  77.5 0.7 entering_rows.1
  78.2 3.7 %collective-permute-start.6 = (f32[128,256]{1,0:T(8,128)S(1)}, f32[128,256]{1,0:T(8,128)S(1)}, u32[]{:S(2)}, u32[]{:S(2)}) collective-permute-start(f32[128,256]{1,0:T(8,128)S(1)} %get-tuple-element.37), channel_id=1, source_target_pairs={{0,12},{4,0},{8,4},{12,8},{1,13},{5,1},{9,5},{13,9},{2,14},{6,2},{... | collective-permute-start | bytes 393224 | tf_op jit(solution)/shard_map/ppermute | solution.py:537
  81.9 1.1 collective-permute-start.8
  83.0 21.0 %attention.1 = bf16[1024,512]{1,0:T(8,128)(2,1)S(1)} custom-call(s32[10]{0:T(128)S(1)} %copy-done.16, s32[10]{0:T(128)S(1)} %copy-done.17, s32[2]{0:T(128)S(1)} %copy-done.12, bf16[1024,512]{1,0:T(8,128)(2,1)S(1)} %pad_maximum_fusion.q_ref, bf16[1024,256]{1,0:T(8,128)(2,1)} %constant_dynamic-update-slice_fusion.rest_0_, ...), custom_call_target="tpu_custom_call" | custom-call | tf_op jit(solution)/shard_map/attention/pallas_call | solution.py:489
  104.1 0.0 copy-start.2
  104.1 0.0 copy-start.4
  104.1 0.0 copy-start.22
  104.1 0.8 fusion
  104.9 2.2 %collective-permute-start.22 = (bf16[256,512]{1,0:T(8,128)(2,1)S(1)}, bf16[256,512]{1,0:T(8,128)(2,1)S(1)}, u32[]{:S(2)}, u32[]{:S(2)}) collective-permute-start(bf16[256,512]{1,0:T(8,128)(2,1)S(1)} %get-tuple-element.54), channel_id=1, source_target_pairs={{0,12},{4,0},{8,4},{12,8},{1,13},{5,1},{9,5},{13,9},{2,14},{6,2},{... | collective-permute-start | bytes 786440 | tf_op jit(solution)/shard_map/ppermute | solution.py:537
  107.1 0.0 copy-start
  107.1 0.0 copy-start.15
  107.1 2.5 %start_states.1 = (f32[128,1024]{1,0:T(8,128)S(1)}, f32[128,1024]{1,0:T(8,128)}, f32[128,1024]{1,0:T(8,128)}, f32[128,1024]{1,0:T(8,128)}) custom-call(s32[2]{0:T(128)S(1)} %copy-done.12, f32[136,1024]{1,0:T(8,128)S(1)} %get-tuple-element.28.refs_0_, f32[136,1024]{1,0:T(8,128)S(1)} %collective-permute-done.refs_1_, f32[136,1024]{1,0:T(8,128)S(1)} %copy-done.2, ...), custom_call_target="tpu_custom_call" | custom-call | tf_op jit(solution)/shard_map/start_states/pallas_call | solution.py:255
  109.6 0.8 copy-done.8
  110.4 1.9 %collective-permute-start.9 = (f32[128,1024]{1,0:T(8,128)}, f32[128,1024]{1,0:T(8,128)}, u32[]{:S(2)}, u32[]{:S(2)}) collective-permute-start(f32[128,1024]{1,0:T(8,128)} %get-tuple-element.41), channel_id=1, source_target_pairs={{0,3},{1,0},{2,1},{3,2},{4,7},{5,4},{6,5},{7,6},{8,11},{9,8},{10,9... | collective-permute-start | bytes 1572872 | tf_op jit(solution)/shard_map/ppermute | solution.py:537
  112.3 1.6 %collective-permute-start.10 = (f32[128,1024]{1,0:T(8,128)}, f32[128,1024]{1,0:T(8,128)}, u32[]{:S(2)}, u32[]{:S(2)}) collective-permute-start(f32[128,1024]{1,0:T(8,128)} %get-tuple-element.42), channel_id=1, source_target_pairs={{0,2},{1,3},{2,0},{3,1},{4,6},{5,7},{6,4},{7,5},{8,10},{9,11},{10,... | collective-permute-start | bytes 1572872 | tf_op jit(solution)/shard_map/ppermute | solution.py:537
  113.9 1.3 collective-permute-start.11
  115.2 2.0 %collective-permute-start.23 = (bf16[256,512]{1,0:T(8,128)(2,1)S(1)}, bf16[256,512]{1,0:T(8,128)(2,1)}, u32[]{:S(2)}, u32[]{:S(2)}) collective-permute-start(bf16[256,512]{1,0:T(8,128)(2,1)S(1)} %get-tuple-element.53), channel_id=1, source_target_pairs={{0,8},{4,12},{8,0},{12,4},{1,9},{5,13},{9,1},{13,5},{2,10},{6,14},... | collective-permute-start | bytes 786440 | tf_op jit(solution)/shard_map/ppermute | solution.py:537
  117.2 0.7 copy-done.18
  117.9 5.3 %collective-permute-done.23.refs_2_ = bf16[256,512]{1,0:T(8,128)(2,1)} collective-permute-done((bf16[256,512]{1,0:T(8,128)(2,1)S(1)}, bf16[256,512]{1,0:T(8,128)(2,1)}, u32[]{:S(2)}, u32[]{:S(2)}) %collective-permute-start.23) | collective-permute-done | bytes 262176 | tf_op jit(solution)/shard_map/ppermute | solution.py:537
  123.2 2.8 %collective-permute-done.24.refs_3_ = bf16[256,512]{1,0:T(8,128)(2,1)} collective-permute-done((bf16[256,512]{1,0:T(8,128)(2,1)S(1)}, bf16[256,512]{1,0:T(8,128)(2,1)}, u32[]{:S(2)}, u32[]{:S(2)}) %collective-permute-start.24) | collective-permute-done | bytes 262176 | tf_op jit(solution)/shard_map/ppermute | solution.py:537
  126.0 3.4 %unpack.1 = bf16[256,2048]{1,0:T(8,128)(2,1)} custom-call(s32[2]{0:T(128)} %pad_add_fusion.at_ref, bf16[256,512]{1,0:T(8,128)(2,1)} %get-tuple-element.55.refs_0_, bf16[256,512]{1,0:T(8,128)(2,1)} %copy-done.18, bf16[256,512]{1,0:T(8,128)(2,1)} %collective-permute-done.23.refs_2_, bf16[256,512]{1,0:T(8,128)(2,1)} %collective-permute-done.24.refs_3_), custom_call_target="tpu_custom_call" | custom-call | tf_op jit(solution)/shard_map/unpack/pallas_call | solution.py:523
  129.5 9.9 %ssd_out.1 = bf16[256,4096]{1,0:T(8,128)(2,1)} custom-call(s32[2]{0:T(128)S(1)} %copy-done.13, bf16[256,4096]{1,0:T(8,128)(2,1)S(1)} %copy-done, bf16[256,4096]{1,0:T(8,128)(2,1)} %gate_ref.1, bf16[256,512]{1,0:T(8,128)(2,1)S(1)} %copy-done.7, bf16[256,512]{1,0:T(8,128)(2,1)S(1)} %copy-done.10, f32[256,32]{1,0:T(8,128)S(1)} %copy.16.dt_ref, ...), custom_call_target="tpu_custom_call" | custom-call | tf_op jit(solution)/shard_map/ssd_out/pallas_call | solution.py:358
  (57 shorter events, 0.2 us)
Async XLA Ops:
  0.6 5.0 %copy-start.21 = (f32[256,32]{0,1:T(8,128)S(1)}, f32[256,32]{0,1:T(8,128)}, u32[]{:S(2)}) copy-start(f32[256,32]{0,1:T(8,128)} %param.17) | copy-start | bytes 98308
  0.6 5.1 %copy-start.6 = (bf16[256,512]{1,0:T(8,128)(2,1)S(1)}, bf16[256,512]{1,0:T(8,128)(2,1)}, u32[]{:S(2)}) copy-start(bf16[256,512]{1,0:T(8,128)(2,1)} %w_ref.3) | copy-start | bytes 786436
  0.7 5.1 %copy-start.14 = (f32[32]{0:T(128)S(1)}, f32[32]{0:T(128)}, u32[]{:S(2)}) copy-start(f32[32]{0:T(128)} %param.18) | copy-start | bytes 388
  1.3 4.5 %copy-start.11 = (s32[2]{0:T(128)S(1)}, s32[2]{0:T(128)}, u32[]{:S(2)}) copy-start(s32[2]{0:T(128)} %pad_add_fusion.at_ref) | copy-start | bytes 28
  4.1 10.7 %copy-start.24 = (bf16[256,256]{1,0:T(8,128)(2,1)S(1)}, bf16[256,256]{1,0:T(8,128)(2,1)}, u32[]{:S(2)}) copy-start(bf16[256,256]{1,0:T(8,128)(2,1)} %get-tuple-element.50) | copy-start | bytes 393220
  4.1 13.5 %copy-start.23 = (bf16[256,256]{1,0:T(8,128)(2,1)S(1)}, bf16[256,256]{1,0:T(8,128)(2,1)}, u32[]{:S(2)}) copy-start(bf16[256,256]{1,0:T(8,128)(2,1)} %get-tuple-element.51) | copy-start | bytes 393220
  4.1 14.9 %copy-start.20 = (bf16[256,256]{1,0:T(8,128)(2,1)S(1)}, bf16[256,256]{1,0:T(8,128)(2,1)}, u32[]{:S(2)}) copy-start(bf16[256,256]{1,0:T(8,128)(2,1)} %get-tuple-element.48) | copy-start | bytes 393220
  4.1 15.6 %collective-permute-start.15 = (bf16[256,256]{1,0:T(8,128)(2,1)}, bf16[256,256]{1,0:T(8,128)(2,1)S(1)}, u32[]{:S(2)}, u32[]{:S(2)}) collective-permute-start(bf16[256,256]{1,0:T(8,128)(2,1)} %get-tuple-element.49), channel_id=1, source_target_pairs={{0,4},{4,8},{8,12},{12,0},{1,5},{5,9},{9,13},{13,1},{2,6},{6,10},{... | collective-permute-start | bytes 393224 | tf_op jit(solution)/shard_map/ppermute | solution.py:537
  11.9 1.4 copy-start.5
  13.2 19.8 %collective-permute-start = (f32[136,1024]{1,0:T(8,128)}, f32[136,1024]{1,0:T(8,128)S(1)}, u32[]{:S(2)}, u32[]{:S(2)}) collective-permute-start(f32[136,1024]{1,0:T(8,128)} %get-tuple-element.29), channel_id=1, source_target_pairs={{0,1},{1,2},{2,3},{3,0},{4,5},{5,6},{6,7},{7,4},{8,9},{9,10},{10,1... | collective-permute-start | bytes 1671176 | tf_op jit(solution)/shard_map/ppermute | solution.py:537
  14.8 6.5 %collective-permute-start.16 = (bf16[256,256]{1,0:T(8,128)(2,1)S(1)}, bf16[256,256]{1,0:T(8,128)(2,1)S(1)}, u32[]{:S(2)}, u32[]{:S(2)}) collective-permute-start(bf16[256,256]{1,0:T(8,128)(2,1)S(1)} %copy-done.24), channel_id=1, source_target_pairs={{0,8},{4,12},{8,0},{12,4},{1,9},{5,13},{9,1},{13,5},{2,10},{6,14},... | collective-permute-start | bytes 393224 | tf_op jit(solution)/shard_map/ppermute | solution.py:537
  17.6 5.6 %collective-permute-start.17 = (bf16[256,256]{1,0:T(8,128)(2,1)S(1)}, bf16[256,256]{1,0:T(8,128)(2,1)S(1)}, u32[]{:S(2)}, u32[]{:S(2)}) collective-permute-start(bf16[256,256]{1,0:T(8,128)(2,1)S(1)} %copy-done.23), channel_id=1, source_target_pairs={{0,12},{4,0},{8,4},{12,8},{1,13},{5,1},{9,5},{13,9},{2,14},{6,2},{... | collective-permute-start | bytes 393224 | tf_op jit(solution)/shard_map/ppermute | solution.py:537
  23.9 16.5 %collective-permute-start.18 = (bf16[1024,256]{1,0:T(8,128)(2,1)}, bf16[1024,256]{1,0:T(8,128)(2,1)S(1)}, u32[]{:S(2)}, u32[]{:S(2)}) collective-permute-start(bf16[1024,256]{1,0:T(8,128)(2,1)} %constant_dynamic-update-slice_fusion.rest_0_), channel_id=1, source_target_pairs={{0,1},{1,2},{2,3},{3,0},{4,5},{5,6},{6,7},{7,4},{8,9},{9,10},{10,1... | collective-permute-start | bytes 1572872 | tf_op jit(solution)/shard_map/ppermute | solution.py:537
  25.4 25.9 %collective-permute-start.20 = (bf16[1024,256]{1,0:T(8,128)(2,1)}, bf16[1024,256]{1,0:T(8,128)(2,1)}, u32[]{:S(2)}, u32[]{:S(2)}) collective-permute-start(bf16[1024,256]{1,0:T(8,128)(2,1)} %constant_dynamic-update-slice_fusion.rest_0_), channel_id=1, source_target_pairs={{0,3},{1,0},{2,1},{3,2},{4,7},{5,4},{6,5},{7,6},{8,11},{9,8},{10,9... | collective-permute-start | bytes 1572872 | tf_op jit(solution)/shard_map/ppermute | solution.py:537
  27.1 26.7 %collective-permute-start.1 = (f32[136,1024]{1,0:T(8,128)}, f32[136,1024]{1,0:T(8,128)S(1)}, u32[]{:S(2)}, u32[]{:S(2)}) collective-permute-start(f32[136,1024]{1,0:T(8,128)} %get-tuple-element.30), channel_id=1, source_target_pairs={{0,2},{1,3},{2,0},{3,1},{4,6},{5,7},{6,4},{7,5},{8,10},{9,11},{10,... | collective-permute-start | bytes 1671176 | tf_op jit(solution)/shard_map/ppermute | solution.py:537
  28.8 36.9 %copy-start.12 = (s32[2]{0:T(128)S(1)}, s32[2]{0:T(128)}, u32[]{:S(2)}) copy-start(s32[2]{0:T(128)} %pad_add_fusion.at_ref) | copy-start | bytes 28
  28.8 35.6 %collective-permute-start.2 = (f32[136,1024]{1,0:T(8,128)}, f32[136,1024]{1,0:T(8,128)S(1)}, u32[]{:S(2)}, u32[]{:S(2)}) collective-permute-start(f32[136,1024]{1,0:T(8,128)} %get-tuple-element.31), channel_id=1, source_target_pairs={{0,3},{1,0},{2,1},{3,2},{4,7},{5,4},{6,5},{7,6},{8,11},{9,8},{10,9... | collective-permute-start | bytes 1671176 | tf_op jit(solution)/shard_map/ppermute | solution.py:537
  33.0 39.0 %copy-start.19 = (bf16[256,512]{1,0:T(8,128)(2,1)S(1)}, bf16[256,512]{1,0:T(8,128)(2,1)}, u32[]{:S(2)}) copy-start(bf16[256,512]{1,0:T(8,128)(2,1)} %get-tuple-element.44) | copy-start | bytes 786436
  33.0 33.6 %collective-permute-start.14 = (bf16[256,512]{1,0:T(8,128)(2,1)}, bf16[256,512]{1,0:T(8,128)(2,1)S(1)}, u32[]{:S(2)}, u32[]{:S(2)}) collective-permute-start(bf16[256,512]{1,0:T(8,128)(2,1)} %get-tuple-element.47), channel_id=1, source_target_pairs={{0,12},{4,0},{8,4},{12,8},{1,13},{5,1},{9,5},{13,9},{2,14},{6,2},{... | collective-permute-start | bytes 786440 | tf_op jit(solution)/shard_map/ppermute | solution.py:537
  40.3 27.8 %collective-permute-start.13 = (bf16[256,512]{1,0:T(8,128)(2,1)}, bf16[256,512]{1,0:T(8,128)(2,1)S(1)}, u32[]{:S(2)}, u32[]{:S(2)}) collective-permute-start(bf16[256,512]{1,0:T(8,128)(2,1)} %get-tuple-element.46), channel_id=1, source_target_pairs={{0,8},{4,12},{8,0},{12,4},{1,9},{5,13},{9,1},{13,5},{2,10},{6,14},... | collective-permute-start | bytes 786440 | tf_op jit(solution)/shard_map/ppermute | solution.py:537
  51.4 19.4 %collective-permute-start.12 = (bf16[256,512]{1,0:T(8,128)(2,1)}, bf16[256,512]{1,0:T(8,128)(2,1)S(1)}, u32[]{:S(2)}, u32[]{:S(2)}) collective-permute-start(bf16[256,512]{1,0:T(8,128)(2,1)} %get-tuple-element.45), channel_id=1, source_target_pairs={{0,4},{4,8},{8,12},{12,0},{1,5},{5,9},{9,13},{13,1},{2,6},{6,10},{... | collective-permute-start | bytes 786440 | tf_op jit(solution)/shard_map/ppermute | solution.py:537
  53.8 18.2 %copy-start.1 = (f32[136,1024]{1,0:T(8,128)}, f32[136,1024]{1,0:T(8,128)S(1)}, u32[]{:S(2)}) copy-start(f32[136,1024]{1,0:T(8,128)S(1)} %collective-permute-done.1.refs_2_) | copy-start | bytes 1671172
  53.9 29.1 %collective-permute-start.21 = (bf16[512,256]{1,0:T(8,128)(2,1)S(1)}, bf16[512,256]{1,0:T(8,128)(2,1)S(1)}, u32[]{:S(2)}, u32[]{:S(2)}) collective-permute-start(bf16[512,256]{1,0:T(8,128)(2,1)S(1)} %slice.25), channel_id=1, source_target_pairs={{0,3},{1,0},{2,1},{3,2},{4,7},{5,4},{6,5},{7,6},{8,11},{9,8},{10,9... | collective-permute-start | bytes 786440 | tf_op jit(solution)/shard_map/ppermute | solution.py:537
  64.4 7.7 %copy-start.3 = (f32[136,1024]{1,0:T(8,128)}, f32[136,1024]{1,0:T(8,128)S(1)}, u32[]{:S(2)}) copy-start(f32[136,1024]{1,0:T(8,128)S(1)} %collective-permute-done.2.refs_3_) | copy-start | bytes 1671172
  64.4 18.6 %collective-permute-start.19 = (bf16[512,256]{1,0:T(8,128)(2,1)S(1)}, bf16[512,256]{1,0:T(8,128)(2,1)S(1)}, u32[]{:S(2)}, u32[]{:S(2)}) collective-permute-start(bf16[512,256]{1,0:T(8,128)(2,1)S(1)} %slice.24), channel_id=1, source_target_pairs={{0,1},{1,2},{2,3},{3,0},{4,5},{5,6},{6,7},{7,4},{8,9},{9,10},{10,1... | collective-permute-start | bytes 786440 | tf_op jit(solution)/shard_map/ppermute | solution.py:537
  66.5 16.5 %copy-start.16 = (s32[10]{0:T(128)S(1)}, s32[10]{0:T(128)}, u32[]{:S(2)}) copy-start(s32[10]{0:T(128)} %constant.11.clone.qi_ref) | copy-start | bytes 124
  66.6 16.5 %copy-start.17 = (s32[10]{0:T(128)S(1)}, s32[10]{0:T(128)}, u32[]{:S(2)}) copy-start(s32[10]{0:T(128)} %constant.12.clone.ci_ref) | copy-start | bytes 124
  66.6 6.3 %collective-permute-start.3 = (f32[136,256]{1,0:T(8,128)S(1)}, f32[136,256]{1,0:T(8,128)S(1)}, u32[]{:S(2)}, u32[]{:S(2)}) collective-permute-start(f32[136,256]{1,0:T(8,128)S(1)} %get-tuple-element.33), channel_id=1, source_target_pairs={{0,4},{4,8},{8,12},{12,0},{1,5},{5,9},{9,13},{13,1},{2,6},{6,10},{... | collective-permute-start | bytes 417800 | tf_op jit(solution)/shard_map/ppermute | solution.py:537
  68.1 7.2 %collective-permute-start.4 = (f32[136,256]{1,0:T(8,128)S(1)}, f32[136,256]{1,0:T(8,128)S(1)}, u32[]{:S(2)}, u32[]{:S(2)}) collective-permute-start(f32[136,256]{1,0:T(8,128)S(1)} %get-tuple-element.34), channel_id=1, source_target_pairs={{0,8},{4,12},{8,0},{12,4},{1,9},{5,13},{9,1},{13,5},{2,10},{6,14},... | collective-permute-start | bytes 417800 | tf_op jit(solution)/shard_map/ppermute | solution.py:537
  70.8 6.7 %collective-permute-start.5 = (f32[136,256]{1,0:T(8,128)S(1)}, f32[136,256]{1,0:T(8,128)S(1)}, u32[]{:S(2)}, u32[]{:S(2)}) collective-permute-start(f32[136,256]{1,0:T(8,128)S(1)} %get-tuple-element.35), channel_id=1, source_target_pairs={{0,12},{4,0},{8,4},{12,8},{1,13},{5,1},{9,5},{13,9},{2,14},{6,2},{... | collective-permute-start | bytes 417800 | tf_op jit(solution)/shard_map/ppermute | solution.py:537
  78.2 28.9 %collective-permute-start.6 = (f32[128,256]{1,0:T(8,128)S(1)}, f32[128,256]{1,0:T(8,128)S(1)}, u32[]{:S(2)}, u32[]{:S(2)}) collective-permute-start(f32[128,256]{1,0:T(8,128)S(1)} %get-tuple-element.37), channel_id=1, source_target_pairs={{0,12},{4,0},{8,4},{12,8},{1,13},{5,1},{9,5},{13,9},{2,14},{6,2},{... | collective-permute-start | bytes 393224 | tf_op jit(solution)/shard_map/ppermute | solution.py:537
  81.9 25.2 %collective-permute-start.7 = (f32[128,256]{1,0:T(8,128)S(1)}, f32[128,256]{1,0:T(8,128)S(1)}, u32[]{:S(2)}, u32[]{:S(2)}) collective-permute-start(f32[128,256]{1,0:T(8,128)S(1)} %get-tuple-element.38), channel_id=1, source_target_pairs={{0,8},{4,12},{8,0},{12,4},{1,9},{5,13},{9,1},{13,5},{2,10},{6,14},... | collective-permute-start | bytes 393224 | tf_op jit(solution)/shard_map/ppermute | solution.py:537
  81.9 25.2 %collective-permute-start.8 = (f32[128,256]{1,0:T(8,128)S(1)}, f32[128,256]{1,0:T(8,128)S(1)}, u32[]{:S(2)}, u32[]{:S(2)}) collective-permute-start(f32[128,256]{1,0:T(8,128)S(1)} %get-tuple-element.39), channel_id=1, source_target_pairs={{0,4},{4,8},{8,12},{12,0},{1,5},{5,9},{9,13},{13,1},{2,6},{6,10},{... | collective-permute-start | bytes 393224 | tf_op jit(solution)/shard_map/ppermute | solution.py:537
  104.1 3.0 %copy-start.2 = (f32[136,1024]{1,0:T(8,128)S(1)}, f32[136,1024]{1,0:T(8,128)}, u32[]{:S(2)}) copy-start(f32[136,1024]{1,0:T(8,128)} %copy-done.1) | copy-start | bytes 1671172
  104.1 3.0 %copy-start.4 = (f32[136,1024]{1,0:T(8,128)S(1)}, f32[136,1024]{1,0:T(8,128)}, u32[]{:S(2)}) copy-start(f32[136,1024]{1,0:T(8,128)} %copy-done.3) | copy-start | bytes 1671172
  104.1 13.8 %copy-start.22 = (bf16[4096]{0:T(1024)(128)(2,1)S(1)}, bf16[4096]{0:T(1024)(128)(2,1)}, u32[]{:S(2)}) copy-start(bf16[4096]{0:T(1024)(128)(2,1)} %param.20) | copy-start | bytes 24580
  104.9 12.3 %collective-permute-start.22 = (bf16[256,512]{1,0:T(8,128)(2,1)S(1)}, bf16[256,512]{1,0:T(8,128)(2,1)S(1)}, u32[]{:S(2)}, u32[]{:S(2)}) collective-permute-start(bf16[256,512]{1,0:T(8,128)(2,1)S(1)} %get-tuple-element.54), channel_id=1, source_target_pairs={{0,12},{4,0},{8,4},{12,8},{1,13},{5,1},{9,5},{13,9},{2,14},{6,2},{... | collective-permute-start | bytes 786440 | tf_op jit(solution)/shard_map/ppermute | solution.py:537
  107.1 22.3 %copy-start = (bf16[256,4096]{1,0:T(8,128)(2,1)S(1)}, bf16[256,4096]{1,0:T(8,128)(2,1)}, u32[]{:S(2)}) copy-start(bf16[256,4096]{1,0:T(8,128)(2,1)} %x_ref.3) | copy-start | bytes 6291460
  107.1 22.3 %copy-start.13 = (s32[2]{0:T(128)S(1)}, s32[2]{0:T(128)}, u32[]{:S(2)}) copy-start(s32[2]{0:T(128)} %pad_add_fusion.at_ref) | copy-start | bytes 28
  107.1 22.3 %copy-start.15 = (f32[32]{0:T(128)S(1)}, f32[32]{0:T(128)}, u32[]{:S(2)}) copy-start(f32[32]{0:T(128)} %param.19) | copy-start | bytes 388
  109.6 0.8 copy-start.8
  110.4 19.1 %copy-start.7 = (bf16[256,512]{1,0:T(8,128)(2,1)S(1)}, bf16[256,512]{1,0:T(8,128)(2,1)}, u32[]{:S(2)}) copy-start(bf16[256,512]{1,0:T(8,128)(2,1)} %w_ref.3) | copy-start | bytes 786436
  110.4 19.1 %copy-start.10 = (bf16[256,512]{1,0:T(8,128)(2,1)S(1)}, bf16[256,512]{1,0:T(8,128)(2,1)}, u32[]{:S(2)}) copy-start(bf16[256,512]{1,0:T(8,128)(2,1)} %r_ref.1) | copy-start | bytes 786436
  110.4 19.1 %copy-start.9 = (f32[128,1024]{1,0:T(8,128)S(1)}, f32[128,1024]{1,0:T(8,128)}, u32[]{:S(2)}) copy-start(f32[128,1024]{1,0:T(8,128)} %copy-done.8) | copy-start | bytes 1572868
  110.4 19.0 %collective-permute-start.9 = (f32[128,1024]{1,0:T(8,128)}, f32[128,1024]{1,0:T(8,128)}, u32[]{:S(2)}, u32[]{:S(2)}) collective-permute-start(f32[128,1024]{1,0:T(8,128)} %get-tuple-element.41), channel_id=1, source_target_pairs={{0,3},{1,0},{2,1},{3,2},{4,7},{5,4},{6,5},{7,6},{8,11},{9,8},{10,9... | collective-permute-start | bytes 1572872 | tf_op jit(solution)/shard_map/ppermute | solution.py:537
  112.3 17.2 %collective-permute-start.10 = (f32[128,1024]{1,0:T(8,128)}, f32[128,1024]{1,0:T(8,128)}, u32[]{:S(2)}, u32[]{:S(2)}) collective-permute-start(f32[128,1024]{1,0:T(8,128)} %get-tuple-element.42), channel_id=1, source_target_pairs={{0,2},{1,3},{2,0},{3,1},{4,6},{5,7},{6,4},{7,5},{8,10},{9,11},{10,... | collective-permute-start | bytes 1572872 | tf_op jit(solution)/shard_map/ppermute | solution.py:537
  113.9 15.6 %collective-permute-start.11 = (f32[128,1024]{1,0:T(8,128)}, f32[128,1024]{1,0:T(8,128)}, u32[]{:S(2)}, u32[]{:S(2)}) collective-permute-start(f32[128,1024]{1,0:T(8,128)} %get-tuple-element.43), channel_id=1, source_target_pairs={{0,1},{1,2},{2,3},{3,0},{4,5},{5,6},{6,7},{7,4},{8,9},{9,10},{10,1... | collective-permute-start | bytes 1572872 | tf_op jit(solution)/shard_map/ppermute | solution.py:537
  115.2 8.0 %collective-permute-start.23 = (bf16[256,512]{1,0:T(8,128)(2,1)S(1)}, bf16[256,512]{1,0:T(8,128)(2,1)}, u32[]{:S(2)}, u32[]{:S(2)}) collective-permute-start(bf16[256,512]{1,0:T(8,128)(2,1)S(1)} %get-tuple-element.53), channel_id=1, source_target_pairs={{0,8},{4,12},{8,0},{12,4},{1,9},{5,13},{9,1},{13,5},{2,10},{6,14},... | collective-permute-start | bytes 786440 | tf_op jit(solution)/shard_map/ppermute | solution.py:537
  117.2 0.7 copy-start.18
  117.9 8.1 %collective-permute-start.24 = (bf16[256,512]{1,0:T(8,128)(2,1)S(1)}, bf16[256,512]{1,0:T(8,128)(2,1)}, u32[]{:S(2)}, u32[]{:S(2)}) collective-permute-start(bf16[256,512]{1,0:T(8,128)(2,1)S(1)} %get-tuple-element.52), channel_id=1, source_target_pairs={{0,4},{4,8},{8,12},{12,0},{1,5},{5,9},{9,13},{13,1},{2,6},{6,10},{... | collective-permute-start | bytes 786440 | tf_op jit(solution)/shard_map/ppermute | solution.py:537

commit v2 on v1

v2 whole, which is shorter than its diff:
```python
import math

import jax
import jax.numpy as jnp
from jax import lax
from jax.experimental import pallas as pl
from jax.experimental.pallas import tpu as pltpu
from jax.sharding import Mesh, PartitionSpec as P

SSD_HEADS = 32
GROUPS = 4
PER = SSD_HEADS // GROUPS
D = 128
NQ = 4
KV_HEADS = 4
SIDE = 4
SCALE = (D**-0.5) * math.log2(math.e)
LOG2E = math.log2(math.e)
BF = jnp.bfloat16
F32 = jnp.float32
NEG = -1e30
EXTRA = 8


def params(mib=48):
    return pltpu.CompilerParams(vmem_limit_bytes=mib << 20)


def about(us):
    return pl.CostEstimate(
        flops=int(us * 1.0e9), bytes_accessed=int(us * 3.0e6), transcendentals=0
    )


def columns(begin, width):
    return pl.ds(pl.multiple_of(begin * width, D), width)


def pack_body(at_ref, *refs):
    outs = refs[3 * SIDE :]
    for s in range(SIDE):
        outs[s][:, :D] = refs[3 * s][...]
        outs[s][:, D : 2 * D] = refs[3 * s + 1][...]
        outs[s][:, 2 * D :] = refs[3 * s + 2][...]


def pack(at, k, v, q):
    rows, cols = q.shape
    width = cols // SIDE

    def spec(s, width):
        return pl.BlockSpec((rows, width), lambda g, at: (0, lax.rem(at[0] + s, SIDE)))

    return pl.pallas_call(
        pack_body,
        grid_spec=pltpu.PrefetchScalarGridSpec(
            num_scalar_prefetch=1,
            grid=(1,),
            in_specs=[spec(s, w) for s in range(SIDE) for w in (D, D, width)],
            out_specs=[pl.BlockSpec((rows, 2 * D + width), lambda g, at: (0, 0))] * SIDE,
        ),
        out_shape=[jax.ShapeDtypeStruct((rows, 2 * D + width), BF)] * SIDE,
        compiler_params=params(),
        cost_estimate=about(3),
        name="pack",
    )(at, *([k, v, q] * SIDE))


def stack_body(*refs):
    ins, out = refs[:SIDE], refs[SIDE]
    rows = ins[0].shape[0]
    for s in range(SIDE):
        out[s * rows : (s + 1) * rows, :] = ins[s][...]


def stack(pieces):
    rows = pieces[0].shape[0]
    return pl.pallas_call(
        stack_body,
        grid=(1,),
        in_specs=[pl.BlockSpec((rows, 2 * D), lambda g: (0, 0))] * SIDE,
        out_specs=pl.BlockSpec((SIDE * rows, 2 * D), lambda g: (0, 0)),
        out_shape=jax.ShapeDtypeStruct((SIDE * rows, 2 * D), BF),
        compiler_params=params(),
        cost_estimate=about(2),
        name="stack",
    )(*pieces)


def span_sums(log_decay, span):
    row = lax.rem(lax.broadcasted_iota(jnp.int32, log_decay.shape, 0), span)
    step = 1
    while step < span:
        moved = pltpu.roll(log_decay, step, 0)
        log_decay = log_decay + jnp.where(row >= step, moved, 0.0)
        step *= 2
    return log_decay


def state_body(at_ref, x_ref, w_ref, dt_ref, rate_ref, *rest):
    outs, first_ref, (to_end, total) = rest[:SIDE], rest[SIDE], rest[SIDE + 1 :]
    s = pl.program_id(0)
    rows = dt_ref.shape[0]
    half = rows // 2
    group = lax.rem(at_ref[1] + s, SIDE)

    @pl.when(s == 0)
    def _():
        dt = dt_ref[...]
        sums = span_sums(dt * (-jnp.exp(rate_ref[...])), half)
        ends = jnp.concatenate(
            [jnp.broadcast_to(sums[half * c + half - 1 : half * c + half], (half, SSD_HEADS)) for c in range(2)],
            axis=0,
        )
        to_end[...] = jnp.exp(ends - sums) * dt
        total[0:8, :] = ends[half : half + 8]
        total[8:16, :] = ends[:8] + ends[half : half + 8]

    for g in range(GROUPS):

        @pl.when(group == g)
        def _():
            scaled, last, decays = [], [], []
            for j in range(PER):
                h = g * PER + j
                scaled.append(
                    (to_end[:, h : h + 1] * x_ref[:, j * D : (j + 1) * D].astype(F32)).astype(BF)
                )
                last.append(jnp.broadcast_to(total[0:1, h : h + 1], (1, D)))
                decays.append(jnp.broadcast_to(total[8:16, h : h + 1], (8, D)))
            scaled = jnp.concatenate(scaled, axis=1)
            first, second = [
                lax.dot_general(
                    w_ref[c * half : (c + 1) * half, :],
                    scaled[c * half : (c + 1) * half],
                    (((0,), (0,)), ((), ())),
                    preferred_element_type=F32,
                )
                for c in range(2)
            ]
            first_ref[0] = first
            state = jnp.exp(jnp.concatenate(last, axis=1)) * first + second
            decay = jnp.concatenate(decays, axis=1)
            for t in range(SIDE):

                @pl.when(s == t)
                def _():
                    outs[t][:D, :] = state
                    outs[t][D:, :] = decay


def local_states(at, x, w, dt, rate):
    rows = x.shape[0]
    width = PER * D
    return pl.pallas_call(
        state_body,
        grid_spec=pltpu.PrefetchScalarGridSpec(
            num_scalar_prefetch=1,
            grid=(SIDE,),
            in_specs=[
                pl.BlockSpec((rows, width), lambda s, at: (0, lax.rem(at[1] + s, SIDE))),
                pl.BlockSpec((rows, D), lambda s, at: (0, lax.rem(at[1] + s, SIDE))),
                pl.BlockSpec((rows, SSD_HEADS), lambda s, at: (0, 0)),
                pl.BlockSpec((1, SSD_HEADS), lambda s, at: (0, 0)),
            ],
            out_specs=[pl.BlockSpec((D + EXTRA, width), lambda s, at: (0, 0))] * SIDE
            + [pl.BlockSpec((1, D, width), lambda s, at: (s, 0, 0))],
            scratch_shapes=[pltpu.VMEM((rows, SSD_HEADS), F32), pltpu.VMEM((16, SSD_HEADS), F32)],
        ),
        out_shape=[jax.ShapeDtypeStruct((D + EXTRA, width), F32)] * SIDE
        + [jax.ShapeDtypeStruct((SIDE, D, width), F32)],
        compiler_params=params(),
        cost_estimate=about(6),
        name="local_states",
    )(at, x, w, dt, rate)


def flag(condition):
    return jnp.where(condition, 1.0, 0.0).astype(F32)


def row_total_body(at_ref, *refs):
    ins, outs, total = refs[:SIDE], refs[SIDE : 2 * SIDE], refs[2 * SIDE]
    x, y = at_ref[0], at_ref[1]
    place = [lax.rem(y - s + SIDE, SIDE) for s in range(SIDE)]
    logs = [ref[D : D + 1, :] for ref in ins]
    value = None
    for s in range(SIDE):
        later = sum(flag(place[u] > place[s]) * logs[u] for u in range(SIDE) if u != s)
        term = ins[s][:D, :] * jnp.exp(later)
        value = term if value is None else value + term
    total[:D, :] = value
    total[D:, :] = jnp.broadcast_to(logs[0] + logs[1] + logs[2] + logs[3], (EXTRA, value.shape[1]))
    width = value.shape[1] // SIDE
    for s in range(SIDE):
        begin = pl.multiple_of(lax.rem(x + s, SIDE) * width, width)
        outs[s][...] = total[:, pl.ds(begin, width)]


def row_total(at, states):
    rows, width = states[0].shape
    return pl.pallas_call(
        row_total_body,
        in_specs=[pl.BlockSpec(memory_space=pltpu.SMEM)] + [pl.BlockSpec(memory_space=pltpu.VMEM)] * SIDE,
        out_specs=[pl.BlockSpec(memory_space=pltpu.VMEM)] * SIDE,
        out_shape=[jax.ShapeDtypeStruct((rows, width // SIDE), F32)] * SIDE,
        scratch_shapes=[pltpu.VMEM((rows, width), F32)],
        compiler_params=params(),
        cost_estimate=about(2),
        name="row_total",
    )(at, *states)


def entering_body(at_ref, *refs):
    ins, outs = refs[:SIDE], refs[SIDE:]
    prefixes(at_ref[0], ins, outs, None)


def prefixes(mine, ins, outs, entering):
    place = [lax.rem(mine - s + SIDE, SIDE) for s in range(SIDE)]
    logs = [ref[D : D + 1, :] for ref in ins]
    for t in range(SIDE):
        if entering is None:
            state = jnp.zeros((D, ins[0].shape[1]), F32)
        else:
            before = sum(flag(place[u] < place[t]) * logs[u] for u in range(SIDE) if u != t)
            state = jnp.exp(before) * entering
        for s in range(SIDE):
            if s == t:
                continue
            gap = sum(
                flag((place[u] > place[s]) & (place[u] < place[t])) * logs[u]
                for u in range(SIDE)
                if u != t and u != s
            )
            state = state + (flag(place[s] < place[t]) * jnp.exp(gap)) * ins[s][:D, :]
        outs[t][...] = state


def entering_rows(at, totals):
    width = totals[0].shape[1]
    return pl.pallas_call(
        entering_body,
        in_specs=[pl.BlockSpec(memory_space=pltpu.SMEM)] + [pl.BlockSpec(memory_space=pltpu.VMEM)] * SIDE,
        out_specs=[pl.BlockSpec(memory_space=pltpu.VMEM)] * SIDE,
        out_shape=[jax.ShapeDtypeStruct((D, width), F32)] * SIDE,
        compiler_params=params(),
        cost_estimate=about(1),
        name="entering_rows",
    )(at, *totals)


def starts_body(at_ref, *refs):
    ins, pieces = refs[:SIDE], refs[SIDE : 2 * SIDE]
    outs, whole = refs[2 * SIDE : 3 * SIDE], refs[3 * SIDE]
    width = pieces[0].shape[1]
    for s in range(SIDE):
        begin = pl.multiple_of(lax.rem(at_ref[0] + s, SIDE) * width, width)
        whole[:, pl.ds(begin, width)] = pieces[s][...]
    prefixes(at_ref[1], ins, outs, whole[...])


def start_states(at, states, entering):
    width = states[0].shape[1]
    return pl.pallas_call(
        starts_body,
        in_specs=[pl.BlockSpec(memory_space=pltpu.SMEM)]
        + [pl.BlockSpec(memory_space=pltpu.VMEM)] * (2 * SIDE),
        out_specs=[pl.BlockSpec(memory_space=pltpu.VMEM)] * SIDE,
        out_shape=[jax.ShapeDtypeStruct((D, width), F32)] * SIDE,
        scratch_shapes=[pltpu.VMEM((D, width), F32)],
        compiler_params=params(),
        cost_estimate=about(2),
        name="start_states",
    )(at, *states, *entering)


def inside_body(at_ref, x_ref, w_ref, r_ref, dt_ref, rate_ref, skip_ref, out_ref, cum, cum_t):
    s = pl.program_id(0)
    rows = dt_ref.shape[0]
    half = rows // 2
    group = lax.rem(at_ref[1] + s, SIDE)

    @pl.when(s == 0)
    def _():
        dt = dt_ref[...]
        sums = span_sums(dt * (-jnp.exp(rate_ref[...])), half)
        cum[...] = sums * LOG2E
        cum_t[...] = jnp.transpose((sums - jnp.log(dt)) * LOG2E)

    row = lax.broadcasted_iota(jnp.int32, (half, half), 0)
    col = lax.broadcasted_iota(jnp.int32, (half, half), 1)
    causal = col <= row
    spans = [slice(c * half, (c + 1) * half) for c in range(2)]
    pairs = [row_dot(r_ref[span, :], w_ref[span, :]) for span in spans]

    for g in range(GROUPS):

        @pl.when(group == g)
        def _():
            for j in range(PER):
                h = g * PER + j
                lanes = slice(j * D, (j + 1) * D)
                for c, span in enumerate(spans):
                    x = x_ref[span, lanes]
                    down = jnp.broadcast_to(cum[span, h : h + 1], (half, half))
                    weights = pairs[c] * jnp.exp2(down - cum_t[h : h + 1, span])
                    weights = jnp.where(causal, weights, 0.0).astype(BF)
                    out_ref[span, lanes] = jnp.dot(
                        weights, x, preferred_element_type=F32
                    ) + skip_ref[0, h] * x.astype(F32)


def inside_spans(at, x, w, r, dt, rate, skip):
    rows = x.shape[0]
    width = PER * D

    def turned(s, at):
        return (0, lax.rem(at[1] + s, SIDE))

    def fixed(s, at):
        return (0, 0)

    return pl.pallas_call(
        inside_body,
        grid_spec=pltpu.PrefetchScalarGridSpec(
            num_scalar_prefetch=1,
            grid=(SIDE,),
            in_specs=[
                pl.BlockSpec((rows, width), turned),
                pl.BlockSpec((rows, D), turned),
                pl.BlockSpec((rows, D), turned),
                pl.BlockSpec((rows, SSD_HEADS), fixed),
                pl.BlockSpec((1, SSD_HEADS), fixed),
                pl.BlockSpec(memory_space=pltpu.SMEM),
            ],
            out_specs=pl.BlockSpec((rows, width), turned),
            scratch_shapes=[
                pltpu.VMEM((rows, SSD_HEADS), F32),
                pltpu.VMEM((SSD_HEADS, rows), F32),
            ],
        ),
        out_shape=jax.ShapeDtypeStruct(x.shape, F32),
        compiler_params=params(),
        cost_estimate=about(6),
        name="inside_spans",
    )(at, x, w, r, dt, rate, skip)


def ssd_body(
    at_ref, inside_ref, gate_ref, r_ref, dt_ref, rate_ref, gain_ref, first_ref, *rest
):
    starts, out_ref, (grown, ends, gated) = rest[:SIDE], rest[SIDE], rest[SIDE + 1 :]
    s = pl.program_id(0)
    rows = dt_ref.shape[0]
    half = rows // 2
    group = lax.rem(at_ref[1] + s, SIDE)
    spans = [slice(c * half, (c + 1) * half) for c in range(2)]

    @pl.when(s == 0)
    def _():
        sums = span_sums(dt_ref[...] * (-jnp.exp(rate_ref[...])), half)
        grown[...] = jnp.exp(sums)
        ends[...] = jnp.broadcast_to(jnp.exp(sums[half - 1 : half]), ends.shape)

    for g in range(GROUPS):

        @pl.when(group == g)
        def _():
            decay = jnp.concatenate(
                [
                    jnp.broadcast_to(ends[0:1, g * PER + j : g * PER + j + 1], (1, D))
                    for j in range(PER)
                ],
                axis=1,
            )
            for t in range(SIDE):

                @pl.when(s == t)
                def _():
                    start = starts[t][...]
                    gated[spans[0], :] = jnp.dot(
                        r_ref[spans[0], :], start.astype(BF), preferred_element_type=F32
                    )
                    gated[spans[1], :] = jnp.dot(
                        r_ref[spans[1], :],
                        (decay * start + first_ref[0]).astype(BF),
                        preferred_element_type=F32,
                    )

            square = jnp.zeros((rows, D), F32)
            for j in range(PER):
                h = g * PER + j
                lanes = slice(j * D, (j + 1) * D)
                mixed = inside_ref[:, lanes] + grown[:, h : h + 1] * gated[:, lanes]
                gate = gate_ref[:, lanes].astype(F32)
                value = mixed * (gate * (0.5 + 0.5 * jnp.tanh(0.5 * gate)))
                gated[:, lanes] = value
                square = square + value * value
            mean = jnp.sum(square, axis=1, keepdims=True) * (1.0 / (PER * D))
            inverse = lax.rsqrt(mean + 1e-05)
            for j in range(PER):
                lanes = slice(j * D, (j + 1) * D)
                out_ref[:, lanes] = (
                    gated[:, lanes] * inverse * gain_ref[:, lanes].astype(F32)
                ).astype(BF)


def ssd_out_of(at, inside, gate, r, dt, rate, gain, first, starts):
    rows = inside.shape[0]
    width = PER * D

    def turned(s, at):
        return (0, lax.rem(at[1] + s, SIDE))

    def fixed(s, at):
        return (0, 0)

    return pl.pallas_call(
        ssd_body,
        grid_spec=pltpu.PrefetchScalarGridSpec(
            num_scalar_prefetch=1,
            grid=(SIDE,),
            in_specs=[
                pl.BlockSpec((rows, width), turned),
                pl.BlockSpec((rows, width), turned),
                pl.BlockSpec((rows, D), turned),
                pl.BlockSpec((rows, SSD_HEADS), fixed),
                pl.BlockSpec((1, SSD_HEADS), fixed),
                pl.BlockSpec((1, width), turned),
                pl.BlockSpec((1, D, width), lambda s, at: (s, 0, 0)),
            ]
            + [pl.BlockSpec((D, width), fixed)] * SIDE,
            out_specs=pl.BlockSpec((rows, width), turned),
            scratch_shapes=[
                pltpu.VMEM((rows, SSD_HEADS), F32),
                pltpu.VMEM((8, SSD_HEADS), F32),
                pltpu.VMEM((rows, width), F32),
            ],
        ),
        out_shape=jax.ShapeDtypeStruct(gate.shape, BF),
        compiler_params=params(),
        cost_estimate=about(8),
        name="ssd_out",
    )(at, inside, gate, r, dt, rate, gain, first, *starts)


def load_queries(q_ref, qs):
    rows = q_ref.shape[0]
    for h in range(NQ):
        q = q_ref[:, (2 + h) * D : (3 + h) * D].astype(F32) * SCALE
        hi = q.astype(BF)
        qs[h * rows : (h + 1) * rows, :D] = hi
        qs[h * rows : (h + 1) * rows, D:] = (q - hi.astype(F32)).astype(BF)


def row_dot(a, b):
    return lax.dot_general(a, b, (((1,), (1,)), ((), ())), preferred_element_type=F32)


def lane_max(scores):
    return jnp.maximum(scores[:, :D], scores[:, D:])


def spread_max(parts):
    most = parts[0]
    for part in parts[1:]:
        most = jnp.maximum(most, part)
    return jnp.broadcast_to(jnp.max(most, axis=1, keepdims=True), most.shape)


def attention_body(at_ref, *rest):
    pieces, parts, outs = rest[:SIDE], rest[SIDE : 2 * SIDE - 1], rest[2 * SIDE - 1 : 3 * SIDE - 1]
    qs, kk, va, acc, top = rest[3 * SIDE - 1 :]
    place = pl.program_id(0)
    x, y = at_ref[0], at_ref[1]
    rows = pieces[0].shape[0]
    keys = SIDE * rows

    @pl.when(place == 0)
    def _():
        for c in range(SIDE):
            for u in range(SIDE):
                if u == 0:
                    source = pieces[c]
                else:
                    source = parts[u - 1].at[c * rows : (c + 1) * rows, :]
                to = slice(c * keys + u * rows, c * keys + (u + 1) * rows)
                kk[to, :D] = source[:, :D]
                kk[to, D:] = source[:, :D]
                va[to, :D] = source[:, D : 2 * D]
        va[:, D:] = jnp.ones((SIDE * keys, D), BF)

    for s in range(SIDE):

        @pl.when(lax.rem(x - place + SIDE, SIDE) == s)
        def _():
            load_queries(pieces[s], qs)

    acc[...] = jnp.zeros_like(acc)
    top[...] = jnp.full_like(top, NEG)

    def chunk(c, newest):
        where = pl.ds(pl.multiple_of(lax.rem(x - c + SIDE, SIDE) * keys, keys), keys)
        kc, vc = kk.at[where, :], va.at[where, :]
        if newest:
            causal = lax.broadcasted_iota(jnp.int32, (rows, rows), 1) <= lax.broadcasted_iota(
                jnp.int32, (rows, rows), 0
            )
            shown = [0.0] + [
                jnp.where(lax.rem(y - u + SIDE, SIDE) > y, NEG, 0.0).astype(F32)
                for u in range(1, SIDE)
            ]

        def scores(h):
            mine = qs[h * rows : (h + 1) * rows, :]
            found = [row_dot(mine, kc[u * rows : (u + 1) * rows, :]) for u in range(SIDE)]
            if newest:
                found[0] = jnp.where(causal, found[0], NEG)
            return found

        now = scores(0)
        for h in range(NQ):
            following = scores(h + 1) if h + 1 < NQ else None
            mine = slice(h * rows, (h + 1) * rows)
            old = top[mine, :]
            most = [lane_max(part) for part in now]
            if newest:
                most = [part + shift for part, shift in zip(most, shown)]
            new = jnp.maximum(old, spread_max(most))
            wide = jnp.concatenate([new] * (rows // D), axis=1)
            factor = jnp.exp2(old - new)
            top[mine, :] = new
            out = acc[mine, :] * jnp.concatenate([factor, factor], axis=1)
            for u in range(SIDE):
                base = wide - shown[u] if newest and u else wide
                weights = jnp.exp2(now[u] - base).astype(BF)
                out = out + jnp.dot(
                    weights, vc[u * rows : (u + 1) * rows, :], preferred_element_type=F32
                )
            acc[mine, :] = out
            now = following

    def older(c, carry):
        chunk(c, False)
        return carry

    lax.fori_loop(0, place, older, 0)
    chunk(place, True)
    for s in range(SIDE):

        @pl.when(lax.rem(x - place + SIDE, SIDE) == s)
        def _():
            for h in range(NQ):
                mine = slice(h * rows, (h + 1) * rows)
                outs[s][:, h * D : (h + 1) * D] = (acc[mine, :D] / acc[mine, D:]).astype(BF)


def attention(at, pieces, parts):
    rows, width = pieces[0].shape
    given = width - 2 * D
    keys = parts[0].shape[0]

    def fixed(place, at):
        return (0, 0)

    return pl.pallas_call(
        attention_body,
        grid_spec=pltpu.PrefetchScalarGridSpec(
            num_scalar_prefetch=1,
            grid=(SIDE,),
            in_specs=[pl.BlockSpec((rows, width), fixed)] * SIDE
            + [pl.BlockSpec((keys, 2 * D), fixed)] * (SIDE - 1),
            out_specs=[pl.BlockSpec((rows, given), fixed)] * SIDE,
            scratch_shapes=[
                pltpu.VMEM((NQ * rows, 2 * D), BF),
                pltpu.VMEM((SIDE * keys, 2 * D), BF),
                pltpu.VMEM((SIDE * keys, 2 * D), BF),
                pltpu.VMEM((NQ * rows, 2 * D), F32),
                pltpu.VMEM((NQ * rows, D), F32),
            ],
        ),
        out_shape=[jax.ShapeDtypeStruct((rows, given), BF)] * SIDE,
        compiler_params=params(),
        cost_estimate=about(18),
        name="attention",
    )(at, *pieces, *parts)


def unpack_body(at_ref, *refs):
    ins, out = refs[:SIDE], refs[SIDE]
    width = ins[0].shape[1]
    for s in range(SIDE):
        out[:, columns(lax.rem(at_ref[0] + s, SIDE), width)] = ins[s][...]


def unpack(at, pieces):
    rows, width = pieces[0].shape
    return pl.pallas_call(
        unpack_body,
        in_specs=[pl.BlockSpec(memory_space=pltpu.SMEM)]
        + [pl.BlockSpec(memory_space=pltpu.VMEM)] * SIDE,
        out_specs=pl.BlockSpec(memory_space=pltpu.VMEM),
        out_shape=jax.ShapeDtypeStruct((rows, SIDE * width), BF),
        compiler_params=params(),
        cost_estimate=about(2),
        name="unpack",
    )(at, *pieces)


def shifted(value, axis, by):
    return lax.ppermute(value, axis, [(i, (i + by) % SIDE) for i in range(SIDE)])


def exchange(pieces, axis, sign):
    return [pieces[0]] + [shifted(pieces[s], axis, sign * s) for s in range(1, SIDE)]


def local(
    ssd_input, gate_input, write_map, read_map, step_size, decay_log, skip_gain, norm_gain,
    query_rows, key_rows, value_rows,
):
    at = jnp.stack([lax.axis_index("x"), lax.axis_index("y")]).astype(jnp.int32)
    rate = decay_log.reshape(1, -1)
    skip = skip_gain.reshape(1, -1)
    gain = norm_gain.reshape(1, -1)
    tie = lax.optimization_barrier
    *states, first = local_states(at, ssd_input, write_map, step_size, rate)
    states = exchange(states, "y", 1)
    pieces = exchange(pack(at, key_rows, value_rows, query_rows), "x", 1)
    inside = inside_spans(at, ssd_input, write_map, read_map, step_size, rate, skip)
    own = stack(pieces)
    middle = own.shape[0] // 2
    before = shifted(own, "y", 1)
    after = shifted(own, "y", -1)
    states, inside = tie((states, inside))
    totals = exchange(row_total(at, states), "x", 1)
    entering = entering_rows(at, totals)
    entering, before, after = tie((entering, before, after))
    far = [shifted(before[:middle], "y", 1), shifted(after[middle:], "y", -1)]
    entering = exchange(entering, "x", -1)
    starts = start_states(at, states, entering)
    starts, pieces = tie((starts, pieces))
    starts = exchange(starts, "y", -1)
    parts = [before, jnp.concatenate(far, axis=0), after]
    back = exchange(attention(at, pieces, parts), "x", -1)
    ssd = ssd_out_of(at, inside, gate_input, read_map, step_size, rate, gain, first, starts)
    ssd, back = tie((ssd, back))
    return (ssd, unpack(at, back))


def solution(mesh):
    grid = Mesh(mesh.devices.reshape(-1, SIDE, SIDE), ("dp", "x", "y"))
    split = P(("dp", "x", "y"), None)
    in_specs = (split,) * 5 + (P(), P(), P()) + (split,) * 3
    return jax.shard_map(
        local, mesh=grid, in_specs=in_specs, out_specs=(split, split), check_vma=False
    )
```

time: 140 us -> 108 us (0.77)
  starting transfers between devices: 45 us -> 30.3 us
  Pallas kernels: 50.2 us -> 41.3 us
  waiting for transfers between devices: 35 us -> 30 us
  local copies, waits for them, and re-layouts: 7.45 us -> 4.68 us
    ppermute x25 -> x22, starting transfers between devices: 45 us -> 30.3 us  [shifted(): lax.ppermute(value, axis, [(i, (i + by) % SIDE) for i in range(SIDE)])]
    ppermute x25 -> x22, waiting for transfers between devices: 35 us -> 30 us  [shifted(): lax.ppermute(value, axis, [(i, (i + by) % SIDE) for i in range(SIDE)])]
    pallas_call x4 -> x5, Pallas kernels: 30.1 us -> 25.3 us  [the longest x1 17.5 us: attention(): pl.pallas_call(attention_body, grid_spec=pltpu.PrefetchScalarGridSpec(num...]
    pallas_call x1, Pallas kernels: 9.94 us -> 7.78 us  [ssd_out_of(): pl.pallas_call(ssd_body, grid_spec=pltpu.PrefetchScalarGridSpec(num_scala...]
    slice x3 -> x2, local copies, waits for them, and re-layouts: 1.75 us -> 0.04 us  [local(): far = [shifted(before[:middle], 'y', 1), shifted(after[middle:], 'y', -1)]]
    unnamed x54 -> x25, local copies, waits for them, and re-layouts: 5.02 us -> 4.63 us
  transfers between devices with their start and end apart: 25 -> 22, of which waited for: 10 -> 10; matrix products, arithmetic and copies ran while one was open for 3% -> 0% of each run, Pallas kernels for 27% -> 36%
where the time goes in v2:
time: 108 us; the launch traced here: 107 us
  Pallas kernels  41.3 us (38%)
  starting transfers between devices  30.3 us (28%)
  waiting for transfers between devices  30 us (28%)
  local copies, waits for them, and re-layouts  4.68 us (4%)
    ppermute x22, starting transfers between devices, shifted(): lax.ppermute(value, axis, [(i, (i + by) % SIDE) for i in range(SIDE)])  30.3 us
    ppermute x22, waiting for transfers between devices, shifted(): lax.ppermute(value, axis, [(i, (i + by) % SIDE) for i in range(SIDE)])  30 us
    pallas_call x1, Pallas kernels, attention(): pl.pallas_call(attention_body, grid_spec=pltpu.PrefetchScalarGridSpec(num...  17.5 us
    pallas_call x1, Pallas kernels, ssd_out_of(): pl.pallas_call(ssd_body, grid_spec=pltpu.PrefetchScalarGridSpec(num_scala...  7.78 us
    pallas_call x1, Pallas kernels, inside_spans(): pl.pallas_call(inside_body, grid_spec=pltpu.PrefetchScalarGridSpec(num_sc...  5.44 us
    pallas_call x1, Pallas kernels, local_states(): pl.pallas_call(state_body, grid_spec=pltpu.PrefetchScalarGridSpec(num_sca...  4.94 us
    unnamed x25, local copies, waits for them, and re-layouts  4.63 us
  transfers between devices with their start and end apart: 22, of which 10 were waited for; matrix products, arithmetic and copies ran while one was open for 0% of the time, Pallas kernels for 36%

profile of v2, /device:TPU:64, one launch (start us, length us, event | category | flops | bytes accessed | tf_op | source)
XLA Modules:
  0.0 107.2 jit_solution(14837434086543522544)
XLA Ops:
  0.6 0.1 pad_add_fusion.at_ref
  0.7 1.2 %copy-done.2 = bf16[256,2048]{1,0:T(8,128)(2,1)S(1)} copy-done((bf16[256,2048]{1,0:T(8,128)(2,1)S(1)}, bf16[256,2048]{1,0:T(8,128)(2,1)}, u32[]{:S(2)}) %copy-start.2) | copy-done | bytes 1048600
  1.9 0.9 copy-done.3
  2.9 0.9 copy-done.4
  3.8 0.8 pack.1
  4.6 1.6 %collective-permute-start.6 = (bf16[256,768]{1,0:T(8,128)(2,1)S(1)}, bf16[256,768]{1,0:T(8,128)(2,1)S(1)}, u32[]{:S(2)}, u32[]{:S(2)}) collective-permute-start(bf16[256,768]{1,0:T(8,128)(2,1)S(1)} %get-tuple-element.70), channel_id=1, source_target_pairs={{0,4},{4,8},{8,12},{12,0},{1,5},{5,9},{9,13},{13,1},{2,6},{6,10},{... | collective-permute-start | bytes 1179656 | tf_op jit(solution)/shard_map/ppermute | solution.py:612
  6.2 2.7 %collective-permute-start.7 = (bf16[256,768]{1,0:T(8,128)(2,1)S(1)}, bf16[256,768]{1,0:T(8,128)(2,1)S(1)}, u32[]{:S(2)}, u32[]{:S(2)}) collective-permute-start(bf16[256,768]{1,0:T(8,128)(2,1)S(1)} %get-tuple-element.71), channel_id=1, source_target_pairs={{0,8},{4,12},{8,0},{12,4},{1,9},{5,13},{9,1},{13,5},{2,10},{6,14},... | collective-permute-start | bytes 1179656 | tf_op jit(solution)/shard_map/ppermute | solution.py:612
  8.9 1.4 %collective-permute-start.8 = (bf16[256,768]{1,0:T(8,128)(2,1)S(1)}, bf16[256,768]{1,0:T(8,128)(2,1)S(1)}, u32[]{:S(2)}, u32[]{:S(2)}) collective-permute-start(bf16[256,768]{1,0:T(8,128)(2,1)S(1)} %get-tuple-element.72), channel_id=1, source_target_pairs={{0,12},{4,0},{8,4},{12,8},{1,13},{5,1},{9,5},{13,9},{2,14},{6,2},{... | collective-permute-start | bytes 1179656 | tf_op jit(solution)/shard_map/ppermute | solution.py:612
  10.4 0.0 copy-done.10
  10.4 0.1 copy.13.dt_ref
  10.5 0.0 copy-done.5
  10.5 0.0 copy-done.8
  10.5 4.9 %local_states.1 = (f32[136,1024]{1,0:T(8,128)S(1)}, f32[136,1024]{1,0:T(8,128)S(1)}, f32[136,1024]{1,0:T(8,128)S(1)}, f32[136,1024]{1,0:T(8,128)S(1)}, f32[4,128,1024]{2,1,0:T(8,128)S(1)}) custom-call(s32[2]{0:T(128)S(1)} %pad_add_fusion.at_ref, bf16[256,4096]{1,0:T(8,128)(2,1)} %x_ref.3, bf16[256,512]{1,0:T(8,128)(2,1)S(1)} %copy-done.5, ...), custom_call_target="tpu_custom_call" | custom-call | flops 6000000000 | bytes 18000000 | tf_op jit(solution)/shard_map/local_states/pallas_call | solution.py:155
  15.5 1.4 %copy-done.9 = f32[4,128,1024]{2,1,0:T(8,128)} copy-done((f32[4,128,1024]{2,1,0:T(8,128)}, f32[4,128,1024]{2,1,0:T(8,128)S(1)}, u32[]{:S(2)}) %copy-start.9) | copy-done | bytes 2097176
  16.8 1.6 %collective-permute-start = (f32[136,1024]{1,0:T(8,128)S(1)}, f32[136,1024]{1,0:T(8,128)S(1)}, u32[]{:S(2)}, u32[]{:S(2)}) collective-permute-start(f32[136,1024]{1,0:T(8,128)S(1)} %get-tuple-element.52), channel_id=1, source_target_pairs={{0,1},{1,2},{2,3},{3,0},{4,5},{5,6},{6,7},{7,4},{8,9},{9,10},{10,1... | collective-permute-start | bytes 1671176 | tf_op jit(solution)/shard_map/ppermute | solution.py:612
  18.4 2.9 %collective-permute-start.1 = (f32[136,1024]{1,0:T(8,128)S(1)}, f32[136,1024]{1,0:T(8,128)S(1)}, u32[]{:S(2)}, u32[]{:S(2)}) collective-permute-start(f32[136,1024]{1,0:T(8,128)S(1)} %get-tuple-element.53), channel_id=1, source_target_pairs={{0,2},{1,3},{2,0},{3,1},{4,6},{5,7},{6,4},{7,5},{8,10},{9,11},{10,... | collective-permute-start | bytes 1671176 | tf_op jit(solution)/shard_map/ppermute | solution.py:612
  21.3 0.0 collective-permute-done.6.refs_1_.rest_1_
  21.3 1.4 %collective-permute-start.2 = (f32[136,1024]{1,0:T(8,128)S(1)}, f32[136,1024]{1,0:T(8,128)S(1)}, u32[]{:S(2)}, u32[]{:S(2)}) collective-permute-start(f32[136,1024]{1,0:T(8,128)S(1)} %get-tuple-element.54), channel_id=1, source_target_pairs={{0,3},{1,0},{2,1},{3,2},{4,7},{5,4},{6,5},{7,6},{8,11},{9,8},{10,9... | collective-permute-start | bytes 1671176 | tf_op jit(solution)/shard_map/ppermute | solution.py:612
  22.7 3.5 %collective-permute-done.7.refs_2_.rest_2_ = bf16[256,768]{1,0:T(8,128)(2,1)S(1)} collective-permute-done((bf16[256,768]{1,0:T(8,128)(2,1)S(1)}, bf16[256,768]{1,0:T(8,128)(2,1)S(1)}, u32[]{:S(2)}, u32[]{:S(2)}) %collective-permute-start.7) | collective-permute-done | bytes 393248 | tf_op jit(solution)/shard_map/ppermute | solution.py:612
  26.2 0.0 collective-permute-done.8.refs_3_.rest_3_
  26.3 3.1 %collective-permute-start.10 = (bf16[1024,256]{1,0:T(8,128)(2,1)S(1)}, bf16[1024,256]{1,0:T(8,128)(2,1)S(1)}, u32[]{:S(2)}, u32[]{:S(2)}) collective-permute-start(bf16[1024,256]{1,0:T(8,128)(2,1)S(1)} %stack.13), channel_id=1, source_target_pairs={{0,3},{1,0},{2,1},{3,2},{4,7},{5,4},{6,5},{7,6},{8,11},{9,8},{10,9... | collective-permute-start | bytes 1572872 | tf_op jit(solution)/shard_map/ppermute | solution.py:612
  29.4 0.0 collective-permute-start.9
  29.4 5.4 %inside_spans.1.inside_ref = f32[256,4096]{1,0:T(8,128)} custom-call(s32[2]{0:T(128)S(1)} %pad_add_fusion.at_ref, bf16[256,4096]{1,0:T(8,128)(2,1)S(1)} %copy-done, bf16[256,512]{1,0:T(8,128)(2,1)S(1)} %copy-done.5, bf16[256,512]{1,0:T(8,128)(2,1)S(1)} %copy-done.6, f32[256,32]{1,0:T(8,128)S(1)} %copy.13.dt_ref, f32[1,32]{1,0:T(1,128)S(1)} %bitcast.6, ...), custom_call_target="tpu_custom_call" | custom-call | flops 6000000000 | bytes 18000000 | tf_op jit(solution)/shard_map/inside_spans/pallas_call | solution.py:324
  34.8 0.0 collective-permute-done.refs_1_
  34.8 12.0 %collective-permute-done.1.refs_2_ = f32[136,1024]{1,0:T(8,128)S(1)} collective-permute-done((f32[136,1024]{1,0:T(8,128)S(1)}, f32[136,1024]{1,0:T(8,128)S(1)}, u32[]{:S(2)}, u32[]{:S(2)}) %collective-permute-start.1) | collective-permute-done | bytes 557088 | tf_op jit(solution)/shard_map/ppermute | solution.py:612
  46.8 0.0 collective-permute-done.2.refs_3_
  46.8 0.9 row_total.1
  47.7 0.8 collective-permute-start.3
  48.6 0.9 collective-permute-start.4
  49.5 1.9 %collective-permute-start.5 = (f32[136,256]{1,0:T(8,128)S(1)}, f32[136,256]{1,0:T(8,128)S(1)}, u32[]{:S(2)}, u32[]{:S(2)}) collective-permute-start(f32[136,256]{1,0:T(8,128)S(1)} %get-tuple-element.64), channel_id=1, source_target_pairs={{0,12},{4,0},{8,4},{12,8},{1,13},{5,1},{9,5},{13,9},{2,14},{6,2},{... | collective-permute-start | bytes 417800 | tf_op jit(solution)/shard_map/ppermute | solution.py:612
  51.4 4.4 %collective-permute-done.3.refs_1_ = f32[136,256]{1,0:T(8,128)S(1)} collective-permute-done((f32[136,256]{1,0:T(8,128)S(1)}, f32[136,256]{1,0:T(8,128)S(1)}, u32[]{:S(2)}, u32[]{:S(2)}) %collective-permute-start.3) | collective-permute-done | bytes 139296 | tf_op jit(solution)/shard_map/ppermute | solution.py:612
  55.7 0.0 collective-permute-done.4.refs_2_
  55.7 0.9 collective-permute-done.5.refs_3_
  56.7 0.7 entering_rows.1
  57.3 0.0 collective-permute-done.10.rest_6_
  57.4 0.0 collective-permute-done.9.rest_4_
  57.4 2.5 %collective-permute-start.11 = (f32[128,256]{1,0:T(8,128)S(1)}, f32[128,256]{1,0:T(8,128)S(1)}, u32[]{:S(2)}, u32[]{:S(2)}) collective-permute-start(f32[128,256]{1,0:T(8,128)S(1)} %get-tuple-element.74), channel_id=1, source_target_pairs={{0,12},{4,0},{8,4},{12,8},{1,13},{5,1},{9,5},{13,9},{2,14},{6,2},{... | collective-permute-start | bytes 393224 | tf_op jit(solution)/shard_map/ppermute | solution.py:612
  59.9 0.1 collective-permute-start.12
  60.0 0.9 collective-permute-start.13
  60.9 1.8 %collective-permute-start.18 = (bf16[512,256]{1,0:T(8,128)(2,1)S(1)}, bf16[512,256]{1,0:T(8,128)(2,1)S(1)}, u32[]{:S(2)}, u32[]{:S(2)}) collective-permute-start(bf16[512,256]{1,0:T(8,128)(2,1)S(1)} %slice.7), channel_id=1, source_target_pairs={{0,3},{1,0},{2,1},{3,2},{4,7},{5,4},{6,5},{7,6},{8,11},{9,8},{10,9... | collective-permute-start | bytes 786440 | tf_op jit(solution)/shard_map/ppermute | solution.py:612
  62.7 0.3 collective-permute-start.17
  63.0 0.0 copy-done.11
  63.0 0.8 collective-permute-done.11.refs_5_
  63.8 2.7 %collective-permute-done.12.refs_6_ = f32[128,256]{1,0:T(8,128)S(1)} collective-permute-done((f32[128,256]{1,0:T(8,128)S(1)}, f32[128,256]{1,0:T(8,128)S(1)}, u32[]{:S(2)}, u32[]{:S(2)}) %collective-permute-start.12) | collective-permute-done | bytes 131104 | tf_op jit(solution)/shard_map/ppermute | solution.py:612
  66.5 1.1 %collective-permute-done.13.refs_7_ = f32[128,256]{1,0:T(8,128)S(1)} collective-permute-done((f32[128,256]{1,0:T(8,128)S(1)}, f32[128,256]{1,0:T(8,128)S(1)}, u32[]{:S(2)}, u32[]{:S(2)}) %collective-permute-start.13) | collective-permute-done | bytes 131104 | tf_op jit(solution)/shard_map/ppermute | solution.py:612
  67.6 1.7 %start_states.1 = (f32[128,1024]{1,0:T(8,128)S(1)}, f32[128,1024]{1,0:T(8,128)S(1)}, f32[128,1024]{1,0:T(8,128)S(1)}, f32[128,1024]{1,0:T(8,128)S(1)}) custom-call(s32[2]{0:T(128)S(1)} %pad_add_fusion.at_ref, f32[136,1024]{1,0:T(8,128)S(1)} %get-tuple-element.57.refs_0_, f32[136,1024]{1,0:T(8,128)S(1)} %collective-permute-done.refs_1_, ...), custom_call_target="tpu_custom_call" | custom-call | flops 2000000000 | bytes 6000000 | tf_op jit(solution)/shard_map/start_states/pallas_call | solution.py:265
  69.3 2.7 %collective-permute-start.14 = (f32[128,1024]{1,0:T(8,128)S(1)}, f32[128,1024]{1,0:T(8,128)S(1)}, u32[]{:S(2)}, u32[]{:S(2)}) collective-permute-start(f32[128,1024]{1,0:T(8,128)S(1)} %get-tuple-element.82), channel_id=1, source_target_pairs={{0,3},{1,0},{2,1},{3,2},{4,7},{5,4},{6,5},{7,6},{8,11},{9,8},{10,9... | collective-permute-start | bytes 1572872 | tf_op jit(solution)/shard_map/ppermute | solution.py:612
  72.0 1.2 %collective-permute-start.15 = (f32[128,1024]{1,0:T(8,128)S(1)}, f32[128,1024]{1,0:T(8,128)S(1)}, u32[]{:S(2)}, u32[]{:S(2)}) collective-permute-start(f32[128,1024]{1,0:T(8,128)S(1)} %get-tuple-element.83), channel_id=1, source_target_pairs={{0,2},{1,3},{2,0},{3,1},{4,6},{5,7},{6,4},{7,5},{8,10},{9,11},{10,... | collective-permute-start | bytes 1572872 | tf_op jit(solution)/shard_map/ppermute | solution.py:612
  73.1 1.3 %collective-permute-start.16 = (f32[128,1024]{1,0:T(8,128)S(1)}, f32[128,1024]{1,0:T(8,128)S(1)}, u32[]{:S(2)}, u32[]{:S(2)}) collective-permute-start(f32[128,1024]{1,0:T(8,128)S(1)} %get-tuple-element.84), channel_id=1, source_target_pairs={{0,1},{1,2},{2,3},{3,0},{4,5},{5,6},{6,7},{7,4},{8,9},{9,10},{10,1... | collective-permute-start | bytes 1572872 | tf_op jit(solution)/shard_map/ppermute | solution.py:612
  74.5 0.0 collective-permute-done.18
  74.5 0.0 collective-permute-done.17
  74.5 0.0 copy-start.1
  74.5 17.5 %attention.1 = (bf16[256,512]{1,0:T(8,128)(2,1)S(1)}, bf16[256,512]{1,0:T(8,128)(2,1)S(1)}, bf16[256,512]{1,0:T(8,128)(2,1)S(1)}, bf16[256,512]{1,0:T(8,128)(2,1)S(1)}) custom-call(s32[2]{0:T(128)S(1)} %pad_add_fusion.at_ref, bf16[256,768]{1,0:T(8,128)(2,1)S(1)} %get-tuple-element.85.refs_0_.rest_0_, ...), custom_call_target="tpu_custom_call" | custom-call | flops 17999998976 | bytes 54000000 | tf_op jit(solution)/shard_map/attention/pallas_call | solution.py:567
  92.0 1.0 collective-permute-start.19
  93.0 0.1 collective-permute-start.20
  93.1 1.1 %collective-permute-done.14.rest_1_ = f32[128,1024]{1,0:T(8,128)S(1)} collective-permute-done((f32[128,1024]{1,0:T(8,128)S(1)}, f32[128,1024]{1,0:T(8,128)S(1)}, u32[]{:S(2)}, u32[]{:S(2)}) %collective-permute-start.14) | collective-permute-done | bytes 524320 | tf_op jit(solution)/shard_map/ppermute | solution.py:612
  94.2 0.2 collective-permute-start.21
  94.4 0.0 collective-permute-done.15.rest_2_
  94.4 3.2 %collective-permute-done.16.rest_3_ = f32[128,1024]{1,0:T(8,128)S(1)} collective-permute-done((f32[128,1024]{1,0:T(8,128)S(1)}, f32[128,1024]{1,0:T(8,128)S(1)}, u32[]{:S(2)}, u32[]{:S(2)}) %collective-permute-start.16) | collective-permute-done | bytes 524320 | tf_op jit(solution)/shard_map/ppermute | solution.py:612
  97.6 7.8 %ssd_out.1 = bf16[256,4096]{1,0:T(8,128)(2,1)} custom-call(s32[2]{0:T(128)S(1)} %pad_add_fusion.at_ref, f32[256,4096]{1,0:T(8,128)} %inside_spans.1.inside_ref, bf16[256,4096]{1,0:T(8,128)(2,1)S(1)} %copy-done.1, bf16[256,512]{1,0:T(8,128)(2,1)S(1)} %copy-done.6, f32[256,32]{1,0:T(8,128)S(1)} %copy.13.dt_ref, f32[1,32]{1,0:T(1,128)S(1)} %bitcast.7, ...), custom_call_target="tpu_custom_call" | custom-call | flops 8000000000 | bytes 24000000 | tf_op jit(solution)/shard_map/ssd_out/pallas_call | solution.py:419
  105.4 0.0 collective-permute-done.19.refs_1_
  105.4 0.0 collective-permute-done.20.refs_2_
  105.4 0.2 collective-permute-done.21.refs_3_
  105.7 1.6 %unpack.1 = bf16[256,2048]{1,0:T(8,128)(2,1)} custom-call(s32[2]{0:T(128)S(1)} %pad_add_fusion.at_ref, bf16[256,512]{1,0:T(8,128)(2,1)S(1)} %get-tuple-element.96.refs_0_, bf16[256,512]{1,0:T(8,128)(2,1)S(1)} %collective-permute-done.19.refs_1_, bf16[256,512]{1,0:T(8,128)(2,1)S(1)} %collective-permute-done.20.refs_2_, ...), custom_call_target="tpu_custom_call" | custom-call | flops 2000000000 | bytes 6000000 | tf_op jit(solution)/shard_map/unpack/pallas_call | solution.py:599
  (20 shorter events, 0.1 us)
Async XLA Ops:
  0.7 1.2 %copy-start.2 = (bf16[256,2048]{1,0:T(8,128)(2,1)S(1)}, bf16[256,2048]{1,0:T(8,128)(2,1)}, u32[]{:S(2)}) copy-start(bf16[256,2048]{1,0:T(8,128)(2,1)} %refs_11_.1) | copy-start | bytes 3145732
  1.9 0.9 copy-start.3
  2.9 0.9 copy-start.4
  3.8 6.5 %copy-start.10 = (f32[256,32]{0,1:T(8,128)S(1)}, f32[256,32]{0,1:T(8,128)}, u32[]{:S(2)}) copy-start(f32[256,32]{0,1:T(8,128)} %param.15) | copy-start | bytes 98308
  3.8 6.6 %copy-start.5 = (bf16[256,512]{1,0:T(8,128)(2,1)S(1)}, bf16[256,512]{1,0:T(8,128)(2,1)}, u32[]{:S(2)}) copy-start(bf16[256,512]{1,0:T(8,128)(2,1)} %w_ref.3) | copy-start | bytes 786436
  3.8 6.7 %copy-start.8 = (f32[32]{0:T(128)S(1)}, f32[32]{0:T(128)}, u32[]{:S(2)}) copy-start(f32[32]{0:T(128)} %param.16) | copy-start | bytes 388
  4.6 16.7 %collective-permute-start.6 = (bf16[256,768]{1,0:T(8,128)(2,1)S(1)}, bf16[256,768]{1,0:T(8,128)(2,1)S(1)}, u32[]{:S(2)}, u32[]{:S(2)}) collective-permute-start(bf16[256,768]{1,0:T(8,128)(2,1)S(1)} %get-tuple-element.70), channel_id=1, source_target_pairs={{0,4},{4,8},{8,12},{12,0},{1,5},{5,9},{9,13},{13,1},{2,6},{6,10},{... | collective-permute-start | bytes 1179656 | tf_op jit(solution)/shard_map/ppermute | solution.py:612
  6.2 20.0 %collective-permute-start.7 = (bf16[256,768]{1,0:T(8,128)(2,1)S(1)}, bf16[256,768]{1,0:T(8,128)(2,1)S(1)}, u32[]{:S(2)}, u32[]{:S(2)}) collective-permute-start(bf16[256,768]{1,0:T(8,128)(2,1)S(1)} %get-tuple-element.71), channel_id=1, source_target_pairs={{0,8},{4,12},{8,0},{12,4},{1,9},{5,13},{9,1},{13,5},{2,10},{6,14},... | collective-permute-start | bytes 1179656 | tf_op jit(solution)/shard_map/ppermute | solution.py:612
  8.9 17.3 %collective-permute-start.8 = (bf16[256,768]{1,0:T(8,128)(2,1)S(1)}, bf16[256,768]{1,0:T(8,128)(2,1)S(1)}, u32[]{:S(2)}, u32[]{:S(2)}) collective-permute-start(bf16[256,768]{1,0:T(8,128)(2,1)S(1)} %get-tuple-element.72), channel_id=1, source_target_pairs={{0,12},{4,0},{8,4},{12,8},{1,13},{5,1},{9,5},{13,9},{2,14},{6,2},{... | collective-permute-start | bytes 1179656 | tf_op jit(solution)/shard_map/ppermute | solution.py:612
  15.4 1.4 %copy-start.9 = (f32[4,128,1024]{2,1,0:T(8,128)}, f32[4,128,1024]{2,1,0:T(8,128)S(1)}, u32[]{:S(2)}) copy-start(f32[4,128,1024]{2,1,0:T(8,128)S(1)} %get-tuple-element.56.first_ref) | copy-start | bytes 6291460
  16.8 18.0 %collective-permute-start = (f32[136,1024]{1,0:T(8,128)S(1)}, f32[136,1024]{1,0:T(8,128)S(1)}, u32[]{:S(2)}, u32[]{:S(2)}) collective-permute-start(f32[136,1024]{1,0:T(8,128)S(1)} %get-tuple-element.52), channel_id=1, source_target_pairs={{0,1},{1,2},{2,3},{3,0},{4,5},{5,6},{6,7},{7,4},{8,9},{9,10},{10,1... | collective-permute-start | bytes 1671176 | tf_op jit(solution)/shard_map/ppermute | solution.py:612
  18.4 28.4 %collective-permute-start.1 = (f32[136,1024]{1,0:T(8,128)S(1)}, f32[136,1024]{1,0:T(8,128)S(1)}, u32[]{:S(2)}, u32[]{:S(2)}) collective-permute-start(f32[136,1024]{1,0:T(8,128)S(1)} %get-tuple-element.53), channel_id=1, source_target_pairs={{0,2},{1,3},{2,0},{3,1},{4,6},{5,7},{6,4},{7,5},{8,10},{9,11},{10,... | collective-permute-start | bytes 1671176 | tf_op jit(solution)/shard_map/ppermute | solution.py:612
  21.3 25.5 %collective-permute-start.2 = (f32[136,1024]{1,0:T(8,128)S(1)}, f32[136,1024]{1,0:T(8,128)S(1)}, u32[]{:S(2)}, u32[]{:S(2)}) collective-permute-start(f32[136,1024]{1,0:T(8,128)S(1)} %get-tuple-element.54), channel_id=1, source_target_pairs={{0,3},{1,0},{2,1},{3,2},{4,7},{5,4},{6,5},{7,6},{8,11},{9,8},{10,9... | collective-permute-start | bytes 1671176 | tf_op jit(solution)/shard_map/ppermute | solution.py:612
  26.2 3.2 %copy-start = (bf16[256,4096]{1,0:T(8,128)(2,1)S(1)}, bf16[256,4096]{1,0:T(8,128)(2,1)}, u32[]{:S(2)}) copy-start(bf16[256,4096]{1,0:T(8,128)(2,1)} %x_ref.3) | copy-start | bytes 6291460
  26.2 3.2 %copy-start.6 = (bf16[256,512]{1,0:T(8,128)(2,1)S(1)}, bf16[256,512]{1,0:T(8,128)(2,1)}, u32[]{:S(2)}) copy-start(bf16[256,512]{1,0:T(8,128)(2,1)} %r_ref.3) | copy-start | bytes 786436
  26.2 3.2 %copy-start.7 = (f32[32]{0:T(128)S(1)}, f32[32]{0:T(128)}, u32[]{:S(2)}) copy-start(f32[32]{0:T(128)} %param.17) | copy-start | bytes 388
  26.3 31.1 %collective-permute-start.10 = (bf16[1024,256]{1,0:T(8,128)(2,1)S(1)}, bf16[1024,256]{1,0:T(8,128)(2,1)S(1)}, u32[]{:S(2)}, u32[]{:S(2)}) collective-permute-start(bf16[1024,256]{1,0:T(8,128)(2,1)S(1)} %stack.13), channel_id=1, source_target_pairs={{0,3},{1,0},{2,1},{3,2},{4,7},{5,4},{6,5},{7,6},{8,11},{9,8},{10,9... | collective-permute-start | bytes 1572872 | tf_op jit(solution)/shard_map/ppermute | solution.py:612
  29.4 28.0 %collective-permute-start.9 = (bf16[1024,256]{1,0:T(8,128)(2,1)S(1)}, bf16[1024,256]{1,0:T(8,128)(2,1)S(1)}, u32[]{:S(2)}, u32[]{:S(2)}) collective-permute-start(bf16[1024,256]{1,0:T(8,128)(2,1)S(1)} %stack.13), channel_id=1, source_target_pairs={{0,1},{1,2},{2,3},{3,0},{4,5},{5,6},{6,7},{7,4},{8,9},{9,10},{10,1... | collective-permute-start | bytes 1572872 | tf_op jit(solution)/shard_map/ppermute | solution.py:612
  47.7 8.0 %collective-permute-start.3 = (f32[136,256]{1,0:T(8,128)S(1)}, f32[136,256]{1,0:T(8,128)S(1)}, u32[]{:S(2)}, u32[]{:S(2)}) collective-permute-start(f32[136,256]{1,0:T(8,128)S(1)} %get-tuple-element.62), channel_id=1, source_target_pairs={{0,4},{4,8},{8,12},{12,0},{1,5},{5,9},{9,13},{13,1},{2,6},{6,10},{... | collective-permute-start | bytes 417800 | tf_op jit(solution)/shard_map/ppermute | solution.py:612
  48.6 7.2 %collective-permute-start.4 = (f32[136,256]{1,0:T(8,128)S(1)}, f32[136,256]{1,0:T(8,128)S(1)}, u32[]{:S(2)}, u32[]{:S(2)}) collective-permute-start(f32[136,256]{1,0:T(8,128)S(1)} %get-tuple-element.63), channel_id=1, source_target_pairs={{0,8},{4,12},{8,0},{12,4},{1,9},{5,13},{9,1},{13,5},{2,10},{6,14},... | collective-permute-start | bytes 417800 | tf_op jit(solution)/shard_map/ppermute | solution.py:612
  49.5 7.2 %collective-permute-start.5 = (f32[136,256]{1,0:T(8,128)S(1)}, f32[136,256]{1,0:T(8,128)S(1)}, u32[]{:S(2)}, u32[]{:S(2)}) collective-permute-start(f32[136,256]{1,0:T(8,128)S(1)} %get-tuple-element.64), channel_id=1, source_target_pairs={{0,12},{4,0},{8,4},{12,8},{1,13},{5,1},{9,5},{13,9},{2,14},{6,2},{... | collective-permute-start | bytes 417800 | tf_op jit(solution)/shard_map/ppermute | solution.py:612
  56.6 6.4 %copy-start.11 = (bf16[4096]{0:T(1024)(128)(2,1)S(1)}, bf16[4096]{0:T(1024)(128)(2,1)}, u32[]{:S(2)}) copy-start(bf16[4096]{0:T(1024)(128)(2,1)} %param.18) | copy-start | bytes 24580
  57.4 6.5 %collective-permute-start.11 = (f32[128,256]{1,0:T(8,128)S(1)}, f32[128,256]{1,0:T(8,128)S(1)}, u32[]{:S(2)}, u32[]{:S(2)}) collective-permute-start(f32[128,256]{1,0:T(8,128)S(1)} %get-tuple-element.74), channel_id=1, source_target_pairs={{0,12},{4,0},{8,4},{12,8},{1,13},{5,1},{9,5},{13,9},{2,14},{6,2},{... | collective-permute-start | bytes 393224 | tf_op jit(solution)/shard_map/ppermute | solution.py:612
  59.9 6.6 %collective-permute-start.12 = (f32[128,256]{1,0:T(8,128)S(1)}, f32[128,256]{1,0:T(8,128)S(1)}, u32[]{:S(2)}, u32[]{:S(2)}) collective-permute-start(f32[128,256]{1,0:T(8,128)S(1)} %get-tuple-element.75), channel_id=1, source_target_pairs={{0,8},{4,12},{8,0},{12,4},{1,9},{5,13},{9,1},{13,5},{2,10},{6,14},... | collective-permute-start | bytes 393224 | tf_op jit(solution)/shard_map/ppermute | solution.py:612
  60.0 7.6 %collective-permute-start.13 = (f32[128,256]{1,0:T(8,128)S(1)}, f32[128,256]{1,0:T(8,128)S(1)}, u32[]{:S(2)}, u32[]{:S(2)}) collective-permute-start(f32[128,256]{1,0:T(8,128)S(1)} %get-tuple-element.76), channel_id=1, source_target_pairs={{0,4},{4,8},{8,12},{12,0},{1,5},{5,9},{9,13},{13,1},{2,6},{6,10},{... | collective-permute-start | bytes 393224 | tf_op jit(solution)/shard_map/ppermute | solution.py:612
  60.9 13.6 %collective-permute-start.18 = (bf16[512,256]{1,0:T(8,128)(2,1)S(1)}, bf16[512,256]{1,0:T(8,128)(2,1)S(1)}, u32[]{:S(2)}, u32[]{:S(2)}) collective-permute-start(bf16[512,256]{1,0:T(8,128)(2,1)S(1)} %slice.7), channel_id=1, source_target_pairs={{0,3},{1,0},{2,1},{3,2},{4,7},{5,4},{6,5},{7,6},{8,11},{9,8},{10,9... | collective-permute-start | bytes 786440 | tf_op jit(solution)/shard_map/ppermute | solution.py:612
  62.7 11.7 %collective-permute-start.17 = (bf16[512,256]{1,0:T(8,128)(2,1)S(1)}, bf16[512,256]{1,0:T(8,128)(2,1)S(1)}, u32[]{:S(2)}, u32[]{:S(2)}) collective-permute-start(bf16[512,256]{1,0:T(8,128)(2,1)S(1)} %slice.6), channel_id=1, source_target_pairs={{0,1},{1,2},{2,3},{3,0},{4,5},{5,6},{6,7},{7,4},{8,9},{9,10},{10,1... | collective-permute-start | bytes 786440 | tf_op jit(solution)/shard_map/ppermute | solution.py:612
  69.3 24.9 %collective-permute-start.14 = (f32[128,1024]{1,0:T(8,128)S(1)}, f32[128,1024]{1,0:T(8,128)S(1)}, u32[]{:S(2)}, u32[]{:S(2)}) collective-permute-start(f32[128,1024]{1,0:T(8,128)S(1)} %get-tuple-element.82), channel_id=1, source_target_pairs={{0,3},{1,0},{2,1},{3,2},{4,7},{5,4},{6,5},{7,6},{8,11},{9,8},{10,9... | collective-permute-start | bytes 1572872 | tf_op jit(solution)/shard_map/ppermute | solution.py:612
  72.0 22.4 %collective-permute-start.15 = (f32[128,1024]{1,0:T(8,128)S(1)}, f32[128,1024]{1,0:T(8,128)S(1)}, u32[]{:S(2)}, u32[]{:S(2)}) collective-permute-start(f32[128,1024]{1,0:T(8,128)S(1)} %get-tuple-element.83), channel_id=1, source_target_pairs={{0,2},{1,3},{2,0},{3,1},{4,6},{5,7},{6,4},{7,5},{8,10},{9,11},{10,... | collective-permute-start | bytes 1572872 | tf_op jit(solution)/shard_map/ppermute | solution.py:612
  73.1 24.5 %collective-permute-start.16 = (f32[128,1024]{1,0:T(8,128)S(1)}, f32[128,1024]{1,0:T(8,128)S(1)}, u32[]{:S(2)}, u32[]{:S(2)}) collective-permute-start(f32[128,1024]{1,0:T(8,128)S(1)} %get-tuple-element.84), channel_id=1, source_target_pairs={{0,1},{1,2},{2,3},{3,0},{4,5},{5,6},{6,7},{7,4},{8,9},{9,10},{10,1... | collective-permute-start | bytes 1572872 | tf_op jit(solution)/shard_map/ppermute | solution.py:612
  74.5 23.1 %copy-start.1 = (bf16[256,4096]{1,0:T(8,128)(2,1)S(1)}, bf16[256,4096]{1,0:T(8,128)(2,1)}, u32[]{:S(2)}) copy-start(bf16[256,4096]{1,0:T(8,128)(2,1)} %gate_ref.1) | copy-start | bytes 6291460
  92.0 13.4 %collective-permute-start.19 = (bf16[256,512]{1,0:T(8,128)(2,1)S(1)}, bf16[256,512]{1,0:T(8,128)(2,1)S(1)}, u32[]{:S(2)}, u32[]{:S(2)}) collective-permute-start(bf16[256,512]{1,0:T(8,128)(2,1)S(1)} %get-tuple-element.92), channel_id=1, source_target_pairs={{0,12},{4,0},{8,4},{12,8},{1,13},{5,1},{9,5},{13,9},{2,14},{6,2},{... | collective-permute-start | bytes 786440 | tf_op jit(solution)/shard_map/ppermute | solution.py:612
  93.0 12.4 %collective-permute-start.20 = (bf16[256,512]{1,0:T(8,128)(2,1)S(1)}, bf16[256,512]{1,0:T(8,128)(2,1)S(1)}, u32[]{:S(2)}, u32[]{:S(2)}) collective-permute-start(bf16[256,512]{1,0:T(8,128)(2,1)S(1)} %get-tuple-element.93), channel_id=1, source_target_pairs={{0,8},{4,12},{8,0},{12,4},{1,9},{5,13},{9,1},{13,5},{2,10},{6,14},... | collective-permute-start | bytes 786440 | tf_op jit(solution)/shard_map/ppermute | solution.py:612
  94.2 11.4 %collective-permute-start.21 = (bf16[256,512]{1,0:T(8,128)(2,1)S(1)}, bf16[256,512]{1,0:T(8,128)(2,1)S(1)}, u32[]{:S(2)}, u32[]{:S(2)}) collective-permute-start(bf16[256,512]{1,0:T(8,128)(2,1)S(1)} %get-tuple-element.94), channel_id=1, source_target_pairs={{0,4},{4,8},{8,12},{12,0},{1,5},{5,9},{9,13},{13,1},{2,6},{6,10},{... | collective-permute-start | bytes 786440 | tf_op jit(solution)/shard_map/ppermute | solution.py:612

commit v3 on v2

--- a/solution.py
+++ b/solution.py
@@ -22,7 +22,7 @@
 EXTRA = 8
 
 
-def params(mib=48):
+def params(mib=16):
     return pltpu.CompilerParams(vmem_limit_bytes=mib << 20)
 
 
@@ -61,7 +61,6 @@
         ),
         out_shape=[jax.ShapeDtypeStruct((rows, 2 * D + width), BF)] * SIDE,
         compiler_params=params(),
-        cost_estimate=about(3),
         name="pack",
     )(at, *([k, v, q] * SIDE))
 
@@ -82,7 +81,6 @@
         out_specs=pl.BlockSpec((SIDE * rows, 2 * D), lambda g: (0, 0)),
         out_shape=jax.ShapeDtypeStruct((SIDE * rows, 2 * D), BF),
         compiler_params=params(),
-        cost_estimate=about(2),
         name="stack",
     )(*pieces)
 
@@ -100,13 +98,13 @@
 def state_body(at_ref, x_ref, w_ref, dt_ref, rate_ref, *rest):
     outs, first_ref, (to_end, total) = rest[:SIDE], rest[SIDE], rest[SIDE + 1 :]
     s = pl.program_id(0)
-    rows = dt_ref.shape[0]
+    rows = dt_ref.shape[1]
     half = rows // 2
     group = lax.rem(at_ref[1] + s, SIDE)
 
     @pl.when(s == 0)
     def _():
-        dt = dt_ref[...]
+        dt = jnp.transpose(dt_ref[...])
         sums = span_sums(dt * (-jnp.exp(rate_ref[...])), half)
         ends = jnp.concatenate(
             [jnp.broadcast_to(sums[half * c + half - 1 : half * c + half], (half, SSD_HEADS)) for c in range(2)],
@@ -160,7 +158,7 @@
             in_specs=[
                 pl.BlockSpec((rows, width), lambda s, at: (0, lax.rem(at[1] + s, SIDE))),
                 pl.BlockSpec((rows, D), lambda s, at: (0, lax.rem(at[1] + s, SIDE))),
-                pl.BlockSpec((rows, SSD_HEADS), lambda s, at: (0, 0)),
+                pl.BlockSpec((SSD_HEADS, rows), lambda s, at: (0, 0)),
                 pl.BlockSpec((1, SSD_HEADS), lambda s, at: (0, 0)),
             ],
             out_specs=[pl.BlockSpec((D + EXTRA, width), lambda s, at: (0, 0))] * SIDE
@@ -170,7 +168,6 @@
         out_shape=[jax.ShapeDtypeStruct((D + EXTRA, width), F32)] * SIDE
         + [jax.ShapeDtypeStruct((SIDE, D, width), F32)],
         compiler_params=params(),
-        cost_estimate=about(6),
         name="local_states",
     )(at, x, w, dt, rate)
 
@@ -277,13 +274,13 @@
 
 def inside_body(at_ref, x_ref, w_ref, r_ref, dt_ref, rate_ref, skip_ref, out_ref, cum, cum_t):
     s = pl.program_id(0)
-    rows = dt_ref.shape[0]
+    rows = dt_ref.shape[1]
     half = rows // 2
     group = lax.rem(at_ref[1] + s, SIDE)
 
     @pl.when(s == 0)
     def _():
-        dt = dt_ref[...]
+        dt = jnp.transpose(dt_ref[...])
         sums = span_sums(dt * (-jnp.exp(rate_ref[...])), half)
         cum[...] = sums * LOG2E
         cum_t[...] = jnp.transpose((sums - jnp.log(dt)) * LOG2E)
@@ -330,7 +327,7 @@
                 pl.BlockSpec((rows, width), turned),
                 pl.BlockSpec((rows, D), turned),
                 pl.BlockSpec((rows, D), turned),
-                pl.BlockSpec((rows, SSD_HEADS), fixed),
+                pl.BlockSpec((SSD_HEADS, rows), fixed),
                 pl.BlockSpec((1, SSD_HEADS), fixed),
                 pl.BlockSpec(memory_space=pltpu.SMEM),
             ],
@@ -342,7 +339,6 @@
         ),
         out_shape=jax.ShapeDtypeStruct(x.shape, F32),
         compiler_params=params(),
-        cost_estimate=about(6),
         name="inside_spans",
     )(at, x, w, r, dt, rate, skip)
 
@@ -352,14 +348,14 @@
 ):
     starts, out_ref, (grown, ends, gated) = rest[:SIDE], rest[SIDE], rest[SIDE + 1 :]
     s = pl.program_id(0)
-    rows = dt_ref.shape[0]
+    rows = dt_ref.shape[1]
     half = rows // 2
     group = lax.rem(at_ref[1] + s, SIDE)
     spans = [slice(c * half, (c + 1) * half) for c in range(2)]
 
     @pl.when(s == 0)
     def _():
-        sums = span_sums(dt_ref[...] * (-jnp.exp(rate_ref[...])), half)
+        sums = span_sums(jnp.transpose(dt_ref[...]) * (-jnp.exp(rate_ref[...])), half)
         grown[...] = jnp.exp(sums)
         ends[...] = jnp.broadcast_to(jnp.exp(sums[half - 1 : half]), ends.shape)
 
@@ -425,7 +421,7 @@
                 pl.BlockSpec((rows, width), turned),
                 pl.BlockSpec((rows, width), turned),
                 pl.BlockSpec((rows, D), turned),
-                pl.BlockSpec((rows, SSD_HEADS), fixed),
+                pl.BlockSpec((SSD_HEADS, rows), fixed),
                 pl.BlockSpec((1, SSD_HEADS), fixed),
                 pl.BlockSpec((1, width), turned),
                 pl.BlockSpec((1, D, width), lambda s, at: (s, 0, 0)),
@@ -448,10 +444,7 @@
 def load_queries(q_ref, qs):
     rows = q_ref.shape[0]
     for h in range(NQ):
-        q = q_ref[:, (2 + h) * D : (3 + h) * D].astype(F32) * SCALE
-        hi = q.astype(BF)
-        qs[h * rows : (h + 1) * rows, :D] = hi
-        qs[h * rows : (h + 1) * rows, D:] = (q - hi.astype(F32)).astype(BF)
+        qs[h * rows : (h + 1) * rows, :] = q_ref[:, (2 + h) * D : (3 + h) * D]
 
 
 def row_dot(a, b):
@@ -486,8 +479,7 @@
                 else:
                     source = parts[u - 1].at[c * rows : (c + 1) * rows, :]
                 to = slice(c * keys + u * rows, c * keys + (u + 1) * rows)
-                kk[to, :D] = source[:, :D]
-                kk[to, D:] = source[:, :D]
+                kk[to, :] = source[:, :D]
                 va[to, :D] = source[:, D : 2 * D]
         va[:, D:] = jnp.ones((SIDE * keys, D), BF)
 
@@ -513,28 +505,28 @@
             ]
 
         def scores(h):
-            mine = qs[h * rows : (h + 1) * rows, :]
+            mine = qs[h * 2 * rows : (h + 1) * 2 * rows, :]
             found = [row_dot(mine, kc[u * rows : (u + 1) * rows, :]) for u in range(SIDE)]
             if newest:
-                found[0] = jnp.where(causal, found[0], NEG)
+                found[0] = jnp.where(jnp.concatenate([causal, causal], axis=0), found[0], NEG)
             return found
 
         now = scores(0)
-        for h in range(NQ):
-            following = scores(h + 1) if h + 1 < NQ else None
-            mine = slice(h * rows, (h + 1) * rows)
+        for h in range(NQ // 2):
+            following = scores(h + 1) if h + 1 < NQ // 2 else None
+            mine = slice(h * 2 * rows, (h + 1) * 2 * rows)
             old = top[mine, :]
             most = [lane_max(part) for part in now]
             if newest:
                 most = [part + shift for part, shift in zip(most, shown)]
             new = jnp.maximum(old, spread_max(most))
             wide = jnp.concatenate([new] * (rows // D), axis=1)
-            factor = jnp.exp2(old - new)
+            factor = jnp.exp2((old - new) * SCALE)
             top[mine, :] = new
             out = acc[mine, :] * jnp.concatenate([factor, factor], axis=1)
             for u in range(SIDE):
                 base = wide - shown[u] if newest and u else wide
-                weights = jnp.exp2(now[u] - base).astype(BF)
+                weights = jnp.exp2((now[u] - base) * SCALE).astype(BF)
                 out = out + jnp.dot(
                     weights, vc[u * rows : (u + 1) * rows, :], preferred_element_type=F32
                 )
@@ -573,15 +565,15 @@
             + [pl.BlockSpec((keys, 2 * D), fixed)] * (SIDE - 1),
             out_specs=[pl.BlockSpec((rows, given), fixed)] * SIDE,
             scratch_shapes=[
-                pltpu.VMEM((NQ * rows, 2 * D), BF),
-                pltpu.VMEM((SIDE * keys, 2 * D), BF),
+                pltpu.VMEM((NQ * rows, D), BF),
+                pltpu.VMEM((SIDE * keys, D), BF),
                 pltpu.VMEM((SIDE * keys, 2 * D), BF),
                 pltpu.VMEM((NQ * rows, 2 * D), F32),
                 pltpu.VMEM((NQ * rows, D), F32),
             ],
         ),
         out_shape=[jax.ShapeDtypeStruct((rows, given), BF)] * SIDE,
-        compiler_params=params(),
+        compiler_params=params(28),
         cost_estimate=about(18),
         name="attention",
     )(at, *pieces, *parts)
@@ -620,15 +612,18 @@
     ssd_input, gate_input, write_map, read_map, step_size, decay_log, skip_gain, norm_gain,
     query_rows, key_rows, value_rows,
 ):
+    step_size = step_size.T
     at = jnp.stack([lax.axis_index("x"), lax.axis_index("y")]).astype(jnp.int32)
     rate = decay_log.reshape(1, -1)
     skip = skip_gain.reshape(1, -1)
     gain = norm_gain.reshape(1, -1)
     tie = lax.optimization_barrier
     *states, first = local_states(at, ssd_input, write_map, step_size, rate)
+    states, packed = tie((states, (key_rows, value_rows, query_rows)))
     states = exchange(states, "y", 1)
-    pieces = exchange(pack(at, key_rows, value_rows, query_rows), "x", 1)
+    pieces = exchange(pack(at, *packed), "x", 1)
     inside = inside_spans(at, ssd_input, write_map, read_map, step_size, rate, skip)
+    pieces, inside = tie((pieces, inside))
     own = stack(pieces)
     middle = own.shape[0] // 2
     before = shifted(own, "y", 1)

time: 108 us -> 101 us (0.935)
  waiting for transfers between devices: 30 us -> 25.3 us
  Pallas kernels: 41.3 us -> 36.6 us
  starting transfers between devices: 30.3 us -> 33.1 us
    ppermute x22, waiting for transfers between devices: 30 us -> 25.3 us  [shifted(): lax.ppermute(value, axis, [(i, (i + by) % SIDE) for i in range(SIDE)])]
    ppermute x22, starting transfers between devices: 30.3 us -> 33.1 us  [shifted(): lax.ppermute(value, axis, [(i, (i + by) % SIDE) for i in range(SIDE)])]
    pallas_call x1, Pallas kernels: 17.5 us -> 15.9 us  [attention(): pl.pallas_call(attention_body, grid_spec=pltpu.PrefetchScalarGridSpec(num...]
    pallas_call x1, Pallas kernels: 7.78 us -> 6.55 us  [ssd_out_of(): pl.pallas_call(ssd_body, grid_spec=pltpu.PrefetchScalarGridSpec(num_scala...]
    pallas_call x1, Pallas kernels: 4.94 us -> 3.86 us  [local_states(): pl.pallas_call(state_body, grid_spec=pltpu.PrefetchScalarGridSpec(num_sca...]
    unnamed x25 -> x30, local copies, waits for them, and re-layouts: 4.63 us -> 4.08 us
  transfers between devices with their start and end apart: 22 -> 22, of which waited for: 10 -> 12; matrix products, arithmetic and copies ran while one was open for 0% -> 0% of each run, Pallas kernels for 36% -> 30%
where the time goes in v3:
time: 101 us; the launch traced here: 100 us
  Pallas kernels  36.6 us (36%)
  starting transfers between devices  33.1 us (33%)
  waiting for transfers between devices  25.3 us (25%)
  local copies, waits for them, and re-layouts  4.13 us (4%)
    ppermute x22, starting transfers between devices, shifted(): lax.ppermute(value, axis, [(i, (i + by) % SIDE) for i in range(SIDE)])  33.1 us
    ppermute x22, waiting for transfers between devices, shifted(): lax.ppermute(value, axis, [(i, (i + by) % SIDE) for i in range(SIDE)])  25.3 us
    pallas_call x1, Pallas kernels, attention(): pl.pallas_call(attention_body, grid_spec=pltpu.PrefetchScalarGridSpec(num...  15.9 us
    pallas_call x1, Pallas kernels, ssd_out_of(): pl.pallas_call(ssd_body, grid_spec=pltpu.PrefetchScalarGridSpec(num_scala...  6.55 us
    pallas_call x1, Pallas kernels, inside_spans(): pl.pallas_call(inside_body, grid_spec=pltpu.PrefetchScalarGridSpec(num_sc...  4.65 us
    unnamed x30, local copies, waits for them, and re-layouts  4.08 us
    pallas_call x1, Pallas kernels, local_states(): pl.pallas_call(state_body, grid_spec=pltpu.PrefetchScalarGridSpec(num_sca...  3.86 us
  transfers between devices with their start and end apart: 22, of which 12 were waited for; matrix products, arithmetic and copies ran while one was open for 0% of the time, Pallas kernels for 30%

profile of v3, /device:TPU:64, one launch (start us, length us, event | category | flops | bytes accessed | tf_op | source)
XLA Modules:
  0.0 100.2 jit_solution(9841702489633593603)
XLA Ops:
  0.6 0.1 pad_add_fusion.at_ref
  0.7 1.7 %copy-done.1 = bf16[256,4096]{1,0:T(8,128)(2,1)S(1)} copy-done((bf16[256,4096]{1,0:T(8,128)(2,1)S(1)}, bf16[256,4096]{1,0:T(8,128)(2,1)}, u32[]{:S(2)}) %copy-start.1) | copy-done | bytes 2097176
  2.4 0.9 copy-done.5
  3.3 0.8 copy-done.8
  4.1 0.7 copy-done.10
  4.8 3.9 %local_states.1 = (f32[136,1024]{1,0:T(8,128)S(1)}, f32[136,1024]{1,0:T(8,128)S(1)}, f32[136,1024]{1,0:T(8,128)S(1)}, f32[136,1024]{1,0:T(8,128)S(1)}, f32[4,128,1024]{2,1,0:T(8,128)S(1)}) custom-call(s32[2]{0:T(128)S(1)} %pad_add_fusion.at_ref, bf16[256,4096]{1,0:T(8,128)(2,1)S(1)} %copy-done.1, bf16[256,512]{1,0:T(8,128)(2,1)S(1)} %copy-done.5, ...), custom_call_target="tpu_custom_call" | custom-call | tf_op jit(solution)/shard_map/local_states/pallas_call | solution.py:153
  8.6 0.0 copy-start.2
  8.7 0.0 copy-start.6
  8.7 0.0 copy-start.7
  8.7 0.0 copy-start.9
  8.7 0.0 copy-start.12
  8.7 0.8 pack.1
  9.5 1.6 %collective-permute-start.3 = (bf16[256,768]{1,0:T(8,128)(2,1)S(1)}, bf16[256,768]{1,0:T(8,128)(2,1)S(1)}, u32[]{:S(2)}, u32[]{:S(2)}) collective-permute-start(bf16[256,768]{1,0:T(8,128)(2,1)S(1)} %get-tuple-element.75), channel_id=1, source_target_pairs={{0,4},{4,8},{8,12},{12,0},{1,5},{5,9},{9,13},{13,1},{2,6},{6,10},{... | collective-permute-start | bytes 1179656 | tf_op jit(solution)/shard_map/ppermute | solution.py:604
  11.1 1.6 %collective-permute-start = (f32[136,1024]{1,0:T(8,128)S(1)}, f32[136,1024]{1,0:T(8,128)S(1)}, u32[]{:S(2)}, u32[]{:S(2)}) collective-permute-start(f32[136,1024]{1,0:T(8,128)S(1)} %get-tuple-element.68), channel_id=1, source_target_pairs={{0,1},{1,2},{2,3},{3,0},{4,5},{5,6},{6,7},{7,4},{8,9},{9,10},{10,1... | collective-permute-start | bytes 1671176 | tf_op jit(solution)/shard_map/ppermute | solution.py:604
  12.7 2.9 %collective-permute-start.1 = (f32[136,1024]{1,0:T(8,128)S(1)}, f32[136,1024]{1,0:T(8,128)S(1)}, u32[]{:S(2)}, u32[]{:S(2)}) collective-permute-start(f32[136,1024]{1,0:T(8,128)S(1)} %get-tuple-element.69), channel_id=1, source_target_pairs={{0,2},{1,3},{2,0},{3,1},{4,6},{5,7},{6,4},{7,5},{8,10},{9,11},{10,... | collective-permute-start | bytes 1671176 | tf_op jit(solution)/shard_map/ppermute | solution.py:604
  15.6 1.3 %collective-permute-start.2 = (f32[136,1024]{1,0:T(8,128)S(1)}, f32[136,1024]{1,0:T(8,128)S(1)}, u32[]{:S(2)}, u32[]{:S(2)}) collective-permute-start(f32[136,1024]{1,0:T(8,128)S(1)} %get-tuple-element.70), channel_id=1, source_target_pairs={{0,3},{1,0},{2,1},{3,2},{4,7},{5,4},{6,5},{7,6},{8,11},{9,8},{10,9... | collective-permute-start | bytes 1671176 | tf_op jit(solution)/shard_map/ppermute | solution.py:604
  16.9 2.7 %collective-permute-start.4 = (bf16[256,768]{1,0:T(8,128)(2,1)S(1)}, bf16[256,768]{1,0:T(8,128)(2,1)S(1)}, u32[]{:S(2)}, u32[]{:S(2)}) collective-permute-start(bf16[256,768]{1,0:T(8,128)(2,1)S(1)} %get-tuple-element.76), channel_id=1, source_target_pairs={{0,8},{4,12},{8,0},{12,4},{1,9},{5,13},{9,1},{13,5},{2,10},{6,14},... | collective-permute-start | bytes 1179656 | tf_op jit(solution)/shard_map/ppermute | solution.py:604
  19.6 2.2 %collective-permute-done.3.refs_1_.rest_1_ = bf16[256,768]{1,0:T(8,128)(2,1)S(1)} collective-permute-done((bf16[256,768]{1,0:T(8,128)(2,1)S(1)}, bf16[256,768]{1,0:T(8,128)(2,1)S(1)}, u32[]{:S(2)}, u32[]{:S(2)}) %collective-permute-start.3) | collective-permute-done | bytes 393248 | tf_op jit(solution)/shard_map/ppermute | solution.py:604
  21.8 2.5 %collective-permute-start.5 = (bf16[256,768]{1,0:T(8,128)(2,1)S(1)}, bf16[256,768]{1,0:T(8,128)(2,1)S(1)}, u32[]{:S(2)}, u32[]{:S(2)}) collective-permute-start(bf16[256,768]{1,0:T(8,128)(2,1)S(1)} %get-tuple-element.77), channel_id=1, source_target_pairs={{0,12},{4,0},{8,4},{12,8},{1,13},{5,1},{9,5},{13,9},{2,14},{6,2},{... | collective-permute-start | bytes 1179656 | tf_op jit(solution)/shard_map/ppermute | solution.py:604
  24.4 4.6 %inside_spans.1.inside_ref = f32[256,4096]{1,0:T(8,128)S(1)} custom-call(s32[2]{0:T(128)S(1)} %pad_add_fusion.at_ref, bf16[256,4096]{1,0:T(8,128)(2,1)S(1)} %copy-done.2, bf16[256,512]{1,0:T(8,128)(2,1)S(1)} %copy-done.6, bf16[256,512]{1,0:T(8,128)(2,1)S(1)} %copy-done.7, f32[32,256]{1,0:T(8,128)S(1)} %bitcast.6, f32[1,32]{1,0:T(1,128)S(1)} %bitcast.9, ...), custom_call_target="tpu_custom_call" | custom-call | tf_op jit(solution)/shard_map/inside_spans/pallas_call | solution.py:321
  29.0 2.0 %collective-permute-done.4.refs_2_.rest_2_ = bf16[256,768]{1,0:T(8,128)(2,1)S(1)} collective-permute-done((bf16[256,768]{1,0:T(8,128)(2,1)S(1)}, bf16[256,768]{1,0:T(8,128)(2,1)S(1)}, u32[]{:S(2)}, u32[]{:S(2)}) %collective-permute-start.4) | collective-permute-done | bytes 393248 | tf_op jit(solution)/shard_map/ppermute | solution.py:604
  31.1 4.6 %collective-permute-done.5.refs_3_.rest_3_ = bf16[256,768]{1,0:T(8,128)(2,1)S(1)} collective-permute-done((bf16[256,768]{1,0:T(8,128)(2,1)S(1)}, bf16[256,768]{1,0:T(8,128)(2,1)S(1)}, u32[]{:S(2)}, u32[]{:S(2)}) %collective-permute-start.5) | collective-permute-done | bytes 393248 | tf_op jit(solution)/shard_map/ppermute | solution.py:604
  35.7 0.3 collective-permute-start.10
  36.1 1.8 %collective-permute-start.9 = (bf16[1024,256]{1,0:T(8,128)(2,1)S(1)}, bf16[1024,256]{1,0:T(8,128)(2,1)S(1)}, u32[]{:S(2)}, u32[]{:S(2)}) collective-permute-start(bf16[1024,256]{1,0:T(8,128)(2,1)S(1)} %stack.13), channel_id=1, source_target_pairs={{0,1},{1,2},{2,3},{3,0},{4,5},{5,6},{6,7},{7,4},{8,9},{9,10},{10,1... | collective-permute-start | bytes 1572872 | tf_op jit(solution)/shard_map/ppermute | solution.py:604
  37.8 0.0 collective-permute-done.refs_1_
  37.8 3.2 %collective-permute-done.1.refs_2_ = f32[136,1024]{1,0:T(8,128)S(1)} collective-permute-done((f32[136,1024]{1,0:T(8,128)S(1)}, f32[136,1024]{1,0:T(8,128)S(1)}, u32[]{:S(2)}, u32[]{:S(2)}) %collective-permute-start.1) | collective-permute-done | bytes 557088 | tf_op jit(solution)/shard_map/ppermute | solution.py:604
  41.0 0.0 collective-permute-done.2.refs_3_
  41.0 0.9 row_total.1
  41.9 0.3 collective-permute-start.6
  42.2 2.5 %collective-permute-start.7 = (f32[136,256]{1,0:T(8,128)S(1)}, f32[136,256]{1,0:T(8,128)S(1)}, u32[]{:S(2)}, u32[]{:S(2)}) collective-permute-start(f32[136,256]{1,0:T(8,128)S(1)} %get-tuple-element.87), channel_id=1, source_target_pairs={{0,8},{4,12},{8,0},{12,4},{1,9},{5,13},{9,1},{13,5},{2,10},{6,14},... | collective-permute-start | bytes 417800 | tf_op jit(solution)/shard_map/ppermute | solution.py:604
  44.7 2.5 %collective-permute-start.8 = (f32[136,256]{1,0:T(8,128)S(1)}, f32[136,256]{1,0:T(8,128)S(1)}, u32[]{:S(2)}, u32[]{:S(2)}) collective-permute-start(f32[136,256]{1,0:T(8,128)S(1)} %get-tuple-element.88), channel_id=1, source_target_pairs={{0,12},{4,0},{8,4},{12,8},{1,13},{5,1},{9,5},{13,9},{2,14},{6,2},{... | collective-permute-start | bytes 417800 | tf_op jit(solution)/shard_map/ppermute | solution.py:604
  47.2 2.7 %collective-permute-done.6.refs_1_ = f32[136,256]{1,0:T(8,128)S(1)} collective-permute-done((f32[136,256]{1,0:T(8,128)S(1)}, f32[136,256]{1,0:T(8,128)S(1)}, u32[]{:S(2)}, u32[]{:S(2)}) %collective-permute-start.6) | collective-permute-done | bytes 139296 | tf_op jit(solution)/shard_map/ppermute | solution.py:604
  49.9 0.0 collective-permute-done.7.refs_2_
  49.9 0.9 collective-permute-done.8.refs_3_
  50.8 0.7 entering_rows.1
  51.5 0.0 collective-permute-done.10.rest_6_
  51.5 0.0 collective-permute-done.9.rest_4_
  51.5 2.8 %collective-permute-start.11 = (f32[128,256]{1,0:T(8,128)S(1)}, f32[128,256]{1,0:T(8,128)S(1)}, u32[]{:S(2)}, u32[]{:S(2)}) collective-permute-start(f32[128,256]{1,0:T(8,128)S(1)} %get-tuple-element.98), channel_id=1, source_target_pairs={{0,12},{4,0},{8,4},{12,8},{1,13},{5,1},{9,5},{13,9},{2,14},{6,2},{... | collective-permute-start | bytes 393224 | tf_op jit(solution)/shard_map/ppermute | solution.py:604
  54.3 1.2 %collective-permute-start.12 = (f32[128,256]{1,0:T(8,128)S(1)}, f32[128,256]{1,0:T(8,128)S(1)}, u32[]{:S(2)}, u32[]{:S(2)}) collective-permute-start(f32[128,256]{1,0:T(8,128)S(1)} %get-tuple-element.99), channel_id=1, source_target_pairs={{0,8},{4,12},{8,0},{12,4},{1,9},{5,13},{9,1},{13,5},{2,10},{6,14},... | collective-permute-start | bytes 393224 | tf_op jit(solution)/shard_map/ppermute | solution.py:604
  55.5 0.0 collective-permute-start.13
  55.5 2.7 %collective-permute-start.18 = (bf16[512,256]{1,0:T(8,128)(2,1)S(1)}, bf16[512,256]{1,0:T(8,128)(2,1)S(1)}, u32[]{:S(2)}, u32[]{:S(2)}) collective-permute-start(bf16[512,256]{1,0:T(8,128)(2,1)S(1)} %slice.7), channel_id=1, source_target_pairs={{0,3},{1,0},{2,1},{3,2},{4,7},{5,4},{6,5},{7,6},{8,11},{9,8},{10,9... | collective-permute-start | bytes 786440 | tf_op jit(solution)/shard_map/ppermute | solution.py:604
  58.3 0.0 collective-permute-start.17
  58.3 0.1 collective-permute-done.11.refs_5_
  58.4 2.5 %collective-permute-done.12.refs_6_ = f32[128,256]{1,0:T(8,128)S(1)} collective-permute-done((f32[128,256]{1,0:T(8,128)S(1)}, f32[128,256]{1,0:T(8,128)S(1)}, u32[]{:S(2)}, u32[]{:S(2)}) %collective-permute-start.12) | collective-permute-done | bytes 131104 | tf_op jit(solution)/shard_map/ppermute | solution.py:604
  60.8 1.3 %collective-permute-done.13.refs_7_ = f32[128,256]{1,0:T(8,128)S(1)} collective-permute-done((f32[128,256]{1,0:T(8,128)S(1)}, f32[128,256]{1,0:T(8,128)S(1)}, u32[]{:S(2)}, u32[]{:S(2)}) %collective-permute-start.13) | collective-permute-done | bytes 131104 | tf_op jit(solution)/shard_map/ppermute | solution.py:604
  62.2 1.7 %start_states.1 = (f32[128,1024]{1,0:T(8,128)S(1)}, f32[128,1024]{1,0:T(8,128)S(1)}, f32[128,1024]{1,0:T(8,128)S(1)}, f32[128,1024]{1,0:T(8,128)S(1)}) custom-call(s32[2]{0:T(128)S(1)} %pad_add_fusion.at_ref, f32[136,1024]{1,0:T(8,128)S(1)} %get-tuple-element.81.refs_0_, f32[136,1024]{1,0:T(8,128)S(1)} %collective-permute-done.refs_1_, ...), custom_call_target="tpu_custom_call" | custom-call | flops 2000000000 | bytes 6000000 | tf_op jit(solution)/shard_map/start_states/pallas_call | solution.py:262
  63.9 3.1 %collective-permute-start.14 = (f32[128,1024]{1,0:T(8,128)S(1)}, f32[128,1024]{1,0:T(8,128)S(1)}, u32[]{:S(2)}, u32[]{:S(2)}) collective-permute-start(f32[128,1024]{1,0:T(8,128)S(1)} %get-tuple-element.106), channel_id=1, source_target_pairs={{0,3},{1,0},{2,1},{3,2},{4,7},{5,4},{6,5},{7,6},{8,11},{9,8},{10,9... | collective-permute-start | bytes 1572872 | tf_op jit(solution)/shard_map/ppermute | solution.py:604
  67.0 0.2 collective-permute-start.15
  67.2 1.3 %collective-permute-start.16 = (f32[128,1024]{1,0:T(8,128)S(1)}, f32[128,1024]{1,0:T(8,128)S(1)}, u32[]{:S(2)}, u32[]{:S(2)}) collective-permute-start(f32[128,1024]{1,0:T(8,128)S(1)} %get-tuple-element.108), channel_id=1, source_target_pairs={{0,1},{1,2},{2,3},{3,0},{4,5},{5,6},{6,7},{7,4},{8,9},{9,10},{10,1... | collective-permute-start | bytes 1572872 | tf_op jit(solution)/shard_map/ppermute | solution.py:604
  68.5 0.0 collective-permute-done.18
  68.5 0.0 collective-permute-done.17
  68.5 0.0 copy-start.11
  68.5 0.0 copy-start.13
  68.6 15.9 %attention.1 = (bf16[256,512]{1,0:T(8,128)(2,1)S(1)}, bf16[256,512]{1,0:T(8,128)(2,1)S(1)}, bf16[256,512]{1,0:T(8,128)(2,1)S(1)}, bf16[256,512]{1,0:T(8,128)(2,1)S(1)}) custom-call(s32[2]{0:T(128)S(1)} %pad_add_fusion.at_ref, bf16[256,768]{1,0:T(8,128)(2,1)S(1)} %get-tuple-element.109.refs_0_.rest_0_, ...), custom_call_target="tpu_custom_call" | custom-call | flops 17999998976 | bytes 54000000 | tf_op jit(solution)/shard_map/attention/pallas_call | solution.py:559
  84.4 0.6 collective-permute-start.19
  85.1 1.1 %collective-permute-start.20 = (bf16[256,512]{1,0:T(8,128)(2,1)S(1)}, bf16[256,512]{1,0:T(8,128)(2,1)S(1)}, u32[]{:S(2)}, u32[]{:S(2)}) collective-permute-start(bf16[256,512]{1,0:T(8,128)(2,1)S(1)} %get-tuple-element.117), channel_id=1, source_target_pairs={{0,8},{4,12},{8,0},{12,4},{1,9},{5,13},{9,1},{13,5},{2,10},{6,14},... | collective-permute-start | bytes 786440 | tf_op jit(solution)/shard_map/ppermute | solution.py:604
  86.2 2.3 %collective-permute-done.14.rest_1_ = f32[128,1024]{1,0:T(8,128)S(1)} collective-permute-done((f32[128,1024]{1,0:T(8,128)S(1)}, f32[128,1024]{1,0:T(8,128)S(1)}, u32[]{:S(2)}, u32[]{:S(2)}) %collective-permute-start.14) | collective-permute-done | bytes 524320 | tf_op jit(solution)/shard_map/ppermute | solution.py:604
  88.5 0.0 collective-permute-start.21
  88.5 3.4 %collective-permute-done.16.rest_3_ = f32[128,1024]{1,0:T(8,128)S(1)} collective-permute-done((f32[128,1024]{1,0:T(8,128)S(1)}, f32[128,1024]{1,0:T(8,128)S(1)}, u32[]{:S(2)}, u32[]{:S(2)}) %collective-permute-start.16) | collective-permute-done | bytes 524320 | tf_op jit(solution)/shard_map/ppermute | solution.py:604
  91.9 6.6 %ssd_out.1 = bf16[256,4096]{1,0:T(8,128)(2,1)} custom-call(s32[2]{0:T(128)S(1)} %pad_add_fusion.at_ref, f32[256,4096]{1,0:T(8,128)S(1)} %inside_spans.1.inside_ref, bf16[256,4096]{1,0:T(8,128)(2,1)S(1)} %copy-done.13, bf16[256,512]{1,0:T(8,128)(2,1)S(1)} %copy-done.7, f32[32,256]{1,0:T(8,128)S(1)} %bitcast.7, f32[1,32]{1,0:T(1,128)S(1)} %bitcast.10, ...), custom_call_target="tpu_custom_call" | custom-call | flops 8000000000 | bytes 24000000 | tf_op jit(solution)/shard_map/ssd_out/pallas_call | solution.py:415
  98.4 0.0 collective-permute-done.19.refs_1_
  98.4 0.0 collective-permute-done.20.refs_2_
  98.4 0.1 collective-permute-done.21.refs_3_
  98.6 1.6 %unpack.1 = bf16[256,2048]{1,0:T(8,128)(2,1)} custom-call(s32[2]{0:T(128)S(1)} %pad_add_fusion.at_ref, bf16[256,512]{1,0:T(8,128)(2,1)S(1)} %get-tuple-element.120.refs_0_, bf16[256,512]{1,0:T(8,128)(2,1)S(1)} %collective-permute-done.19.refs_1_, bf16[256,512]{1,0:T(8,128)(2,1)S(1)} %collective-permute-done.20.refs_2_, ...), custom_call_target="tpu_custom_call" | custom-call | flops 2000000000 | bytes 6000000 | tf_op jit(solution)/shard_map/unpack/pallas_call | solution.py:591
  (25 shorter events, 0.2 us)
Async XLA Ops:
  0.6 8.0 %copy-start = (bf16[256,2048]{1,0:T(8,128)(2,1)S(1)}, bf16[256,2048]{1,0:T(8,128)(2,1)}, u32[]{:S(2)}) copy-start(bf16[256,2048]{1,0:T(8,128)(2,1)} %refs_11_) | copy-start | bytes 3145732
  0.7 1.7 %copy-start.1 = (bf16[256,4096]{1,0:T(8,128)(2,1)S(1)}, bf16[256,4096]{1,0:T(8,128)(2,1)}, u32[]{:S(2)}) copy-start(bf16[256,4096]{1,0:T(8,128)(2,1)} %x_ref.3) | copy-start | bytes 6291460
  2.4 0.9 copy-start.5
  3.3 0.8 copy-start.8
  4.1 0.7 copy-start.10
  4.7 3.9 %copy-start.3 = (bf16[256,512]{1,0:T(8,128)(2,1)S(1)}, bf16[256,512]{1,0:T(8,128)(2,1)}, u32[]{:S(2)}) copy-start(bf16[256,512]{1,0:T(8,128)(2,1)} %refs_9_) | copy-start | bytes 786436
  4.8 3.9 %copy-start.4 = (bf16[256,512]{1,0:T(8,128)(2,1)S(1)}, bf16[256,512]{1,0:T(8,128)(2,1)}, u32[]{:S(2)}) copy-start(bf16[256,512]{1,0:T(8,128)(2,1)} %refs_10_) | copy-start | bytes 786436
  8.6 15.7 %copy-start.2 = (bf16[256,4096]{1,0:T(8,128)(2,1)S(1)}, bf16[256,4096]{1,0:T(8,128)(2,1)}, u32[]{:S(2)}) copy-start(bf16[256,4096]{1,0:T(8,128)(2,1)} %x_ref.3) | copy-start | bytes 6291460
  8.7 15.7 %copy-start.6 = (bf16[256,512]{1,0:T(8,128)(2,1)S(1)}, bf16[256,512]{1,0:T(8,128)(2,1)}, u32[]{:S(2)}) copy-start(bf16[256,512]{1,0:T(8,128)(2,1)} %w_ref.3) | copy-start | bytes 786436
  8.7 15.7 %copy-start.7 = (bf16[256,512]{1,0:T(8,128)(2,1)S(1)}, bf16[256,512]{1,0:T(8,128)(2,1)}, u32[]{:S(2)}) copy-start(bf16[256,512]{1,0:T(8,128)(2,1)} %r_ref.3) | copy-start | bytes 786436
  8.7 15.7 %copy-start.9 = (f32[256,32]{0,1:T(8,128)S(1)}, f32[256,32]{0,1:T(8,128)}, u32[]{:S(2)}) copy-start(f32[256,32]{0,1:T(8,128)} %param.15) | copy-start | bytes 98308
  8.7 15.7 %copy-start.12 = (f32[32]{0:T(128)S(1)}, f32[32]{0:T(128)}, u32[]{:S(2)}) copy-start(f32[32]{0:T(128)} %param.17) | copy-start | bytes 388
  9.5 12.3 %collective-permute-start.3 = (bf16[256,768]{1,0:T(8,128)(2,1)S(1)}, bf16[256,768]{1,0:T(8,128)(2,1)S(1)}, u32[]{:S(2)}, u32[]{:S(2)}) collective-permute-start(bf16[256,768]{1,0:T(8,128)(2,1)S(1)} %get-tuple-element.75), channel_id=1, source_target_pairs={{0,4},{4,8},{8,12},{12,0},{1,5},{5,9},{9,13},{13,1},{2,6},{6,10},{... | collective-permute-start | bytes 1179656 | tf_op jit(solution)/shard_map/ppermute | solution.py:604
  11.1 26.7 %collective-permute-start = (f32[136,1024]{1,0:T(8,128)S(1)}, f32[136,1024]{1,0:T(8,128)S(1)}, u32[]{:S(2)}, u32[]{:S(2)}) collective-permute-start(f32[136,1024]{1,0:T(8,128)S(1)} %get-tuple-element.68), channel_id=1, source_target_pairs={{0,1},{1,2},{2,3},{3,0},{4,5},{5,6},{6,7},{7,4},{8,9},{9,10},{10,1... | collective-permute-start | bytes 1671176 | tf_op jit(solution)/shard_map/ppermute | solution.py:604
  12.7 28.4 %collective-permute-start.1 = (f32[136,1024]{1,0:T(8,128)S(1)}, f32[136,1024]{1,0:T(8,128)S(1)}, u32[]{:S(2)}, u32[]{:S(2)}) collective-permute-start(f32[136,1024]{1,0:T(8,128)S(1)} %get-tuple-element.69), channel_id=1, source_target_pairs={{0,2},{1,3},{2,0},{3,1},{4,6},{5,7},{6,4},{7,5},{8,10},{9,11},{10,... | collective-permute-start | bytes 1671176 | tf_op jit(solution)/shard_map/ppermute | solution.py:604
  15.6 25.5 %collective-permute-start.2 = (f32[136,1024]{1,0:T(8,128)S(1)}, f32[136,1024]{1,0:T(8,128)S(1)}, u32[]{:S(2)}, u32[]{:S(2)}) collective-permute-start(f32[136,1024]{1,0:T(8,128)S(1)} %get-tuple-element.70), channel_id=1, source_target_pairs={{0,3},{1,0},{2,1},{3,2},{4,7},{5,4},{6,5},{7,6},{8,11},{9,8},{10,9... | collective-permute-start | bytes 1671176 | tf_op jit(solution)/shard_map/ppermute | solution.py:604
  16.9 14.2 %collective-permute-start.4 = (bf16[256,768]{1,0:T(8,128)(2,1)S(1)}, bf16[256,768]{1,0:T(8,128)(2,1)S(1)}, u32[]{:S(2)}, u32[]{:S(2)}) collective-permute-start(bf16[256,768]{1,0:T(8,128)(2,1)S(1)} %get-tuple-element.76), channel_id=1, source_target_pairs={{0,8},{4,12},{8,0},{12,4},{1,9},{5,13},{9,1},{13,5},{2,10},{6,14},... | collective-permute-start | bytes 1179656 | tf_op jit(solution)/shard_map/ppermute | solution.py:604
  21.8 13.8 %collective-permute-start.5 = (bf16[256,768]{1,0:T(8,128)(2,1)S(1)}, bf16[256,768]{1,0:T(8,128)(2,1)S(1)}, u32[]{:S(2)}, u32[]{:S(2)}) collective-permute-start(bf16[256,768]{1,0:T(8,128)(2,1)S(1)} %get-tuple-element.77), channel_id=1, source_target_pairs={{0,12},{4,0},{8,4},{12,8},{1,13},{5,1},{9,5},{13,9},{2,14},{6,2},{... | collective-permute-start | bytes 1179656 | tf_op jit(solution)/shard_map/ppermute | solution.py:604
  35.7 15.8 %collective-permute-start.10 = (bf16[1024,256]{1,0:T(8,128)(2,1)S(1)}, bf16[1024,256]{1,0:T(8,128)(2,1)S(1)}, u32[]{:S(2)}, u32[]{:S(2)}) collective-permute-start(bf16[1024,256]{1,0:T(8,128)(2,1)S(1)} %stack.13), channel_id=1, source_target_pairs={{0,3},{1,0},{2,1},{3,2},{4,7},{5,4},{6,5},{7,6},{8,11},{9,8},{10,9... | collective-permute-start | bytes 1572872 | tf_op jit(solution)/shard_map/ppermute | solution.py:604
  36.1 15.5 %collective-permute-start.9 = (bf16[1024,256]{1,0:T(8,128)(2,1)S(1)}, bf16[1024,256]{1,0:T(8,128)(2,1)S(1)}, u32[]{:S(2)}, u32[]{:S(2)}) collective-permute-start(bf16[1024,256]{1,0:T(8,128)(2,1)S(1)} %stack.13), channel_id=1, source_target_pairs={{0,1},{1,2},{2,3},{3,0},{4,5},{5,6},{6,7},{7,4},{8,9},{9,10},{10,1... | collective-permute-start | bytes 1572872 | tf_op jit(solution)/shard_map/ppermute | solution.py:604
  41.9 8.0 %collective-permute-start.6 = (f32[136,256]{1,0:T(8,128)S(1)}, f32[136,256]{1,0:T(8,128)S(1)}, u32[]{:S(2)}, u32[]{:S(2)}) collective-permute-start(f32[136,256]{1,0:T(8,128)S(1)} %get-tuple-element.86), channel_id=1, source_target_pairs={{0,4},{4,8},{8,12},{12,0},{1,5},{5,9},{9,13},{13,1},{2,6},{6,10},{... | collective-permute-start | bytes 417800 | tf_op jit(solution)/shard_map/ppermute | solution.py:604
  42.2 7.7 %collective-permute-start.7 = (f32[136,256]{1,0:T(8,128)S(1)}, f32[136,256]{1,0:T(8,128)S(1)}, u32[]{:S(2)}, u32[]{:S(2)}) collective-permute-start(f32[136,256]{1,0:T(8,128)S(1)} %get-tuple-element.87), channel_id=1, source_target_pairs={{0,8},{4,12},{8,0},{12,4},{1,9},{5,13},{9,1},{13,5},{2,10},{6,14},... | collective-permute-start | bytes 417800 | tf_op jit(solution)/shard_map/ppermute | solution.py:604
  44.7 6.1 %collective-permute-start.8 = (f32[136,256]{1,0:T(8,128)S(1)}, f32[136,256]{1,0:T(8,128)S(1)}, u32[]{:S(2)}, u32[]{:S(2)}) collective-permute-start(f32[136,256]{1,0:T(8,128)S(1)} %get-tuple-element.88), channel_id=1, source_target_pairs={{0,12},{4,0},{8,4},{12,8},{1,13},{5,1},{9,5},{13,9},{2,14},{6,2},{... | collective-permute-start | bytes 417800 | tf_op jit(solution)/shard_map/ppermute | solution.py:604
  50.8 7.5 %copy-start.14 = (bf16[4096]{0:T(1024)(128)(2,1)S(1)}, bf16[4096]{0:T(1024)(128)(2,1)}, u32[]{:S(2)}) copy-start(bf16[4096]{0:T(1024)(128)(2,1)} %param.18) | copy-start | bytes 24580
  51.5 6.8 %collective-permute-start.11 = (f32[128,256]{1,0:T(8,128)S(1)}, f32[128,256]{1,0:T(8,128)S(1)}, u32[]{:S(2)}, u32[]{:S(2)}) collective-permute-start(f32[128,256]{1,0:T(8,128)S(1)} %get-tuple-element.98), channel_id=1, source_target_pairs={{0,12},{4,0},{8,4},{12,8},{1,13},{5,1},{9,5},{13,9},{2,14},{6,2},{... | collective-permute-start | bytes 393224 | tf_op jit(solution)/shard_map/ppermute | solution.py:604
  54.3 6.5 %collective-permute-start.12 = (f32[128,256]{1,0:T(8,128)S(1)}, f32[128,256]{1,0:T(8,128)S(1)}, u32[]{:S(2)}, u32[]{:S(2)}) collective-permute-start(f32[128,256]{1,0:T(8,128)S(1)} %get-tuple-element.99), channel_id=1, source_target_pairs={{0,8},{4,12},{8,0},{12,4},{1,9},{5,13},{9,1},{13,5},{2,10},{6,14},... | collective-permute-start | bytes 393224 | tf_op jit(solution)/shard_map/ppermute | solution.py:604
  55.5 6.7 %collective-permute-start.13 = (f32[128,256]{1,0:T(8,128)S(1)}, f32[128,256]{1,0:T(8,128)S(1)}, u32[]{:S(2)}, u32[]{:S(2)}) collective-permute-start(f32[128,256]{1,0:T(8,128)S(1)} %get-tuple-element.100), channel_id=1, source_target_pairs={{0,4},{4,8},{8,12},{12,0},{1,5},{5,9},{9,13},{13,1},{2,6},{6,10},{... | collective-permute-start | bytes 393224 | tf_op jit(solution)/shard_map/ppermute | solution.py:604
  55.5 13.0 %collective-permute-start.18 = (bf16[512,256]{1,0:T(8,128)(2,1)S(1)}, bf16[512,256]{1,0:T(8,128)(2,1)S(1)}, u32[]{:S(2)}, u32[]{:S(2)}) collective-permute-start(bf16[512,256]{1,0:T(8,128)(2,1)S(1)} %slice.7), channel_id=1, source_target_pairs={{0,3},{1,0},{2,1},{3,2},{4,7},{5,4},{6,5},{7,6},{8,11},{9,8},{10,9... | collective-permute-start | bytes 786440 | tf_op jit(solution)/shard_map/ppermute | solution.py:604
  58.3 10.2 %collective-permute-start.17 = (bf16[512,256]{1,0:T(8,128)(2,1)S(1)}, bf16[512,256]{1,0:T(8,128)(2,1)S(1)}, u32[]{:S(2)}, u32[]{:S(2)}) collective-permute-start(bf16[512,256]{1,0:T(8,128)(2,1)S(1)} %slice.6), channel_id=1, source_target_pairs={{0,1},{1,2},{2,3},{3,0},{4,5},{5,6},{6,7},{7,4},{8,9},{9,10},{10,1... | collective-permute-start | bytes 786440 | tf_op jit(solution)/shard_map/ppermute | solution.py:604
  63.9 24.6 %collective-permute-start.14 = (f32[128,1024]{1,0:T(8,128)S(1)}, f32[128,1024]{1,0:T(8,128)S(1)}, u32[]{:S(2)}, u32[]{:S(2)}) collective-permute-start(f32[128,1024]{1,0:T(8,128)S(1)} %get-tuple-element.106), channel_id=1, source_target_pairs={{0,3},{1,0},{2,1},{3,2},{4,7},{5,4},{6,5},{7,6},{8,11},{9,8},{10,9... | collective-permute-start | bytes 1572872 | tf_op jit(solution)/shard_map/ppermute | solution.py:604
  67.0 21.5 %collective-permute-start.15 = (f32[128,1024]{1,0:T(8,128)S(1)}, f32[128,1024]{1,0:T(8,128)S(1)}, u32[]{:S(2)}, u32[]{:S(2)}) collective-permute-start(f32[128,1024]{1,0:T(8,128)S(1)} %get-tuple-element.107), channel_id=1, source_target_pairs={{0,2},{1,3},{2,0},{3,1},{4,6},{5,7},{6,4},{7,5},{8,10},{9,11},{10,... | collective-permute-start | bytes 1572872 | tf_op jit(solution)/shard_map/ppermute | solution.py:604
  67.2 24.7 %collective-permute-start.16 = (f32[128,1024]{1,0:T(8,128)S(1)}, f32[128,1024]{1,0:T(8,128)S(1)}, u32[]{:S(2)}, u32[]{:S(2)}) collective-permute-start(f32[128,1024]{1,0:T(8,128)S(1)} %get-tuple-element.108), channel_id=1, source_target_pairs={{0,1},{1,2},{2,3},{3,0},{4,5},{5,6},{6,7},{7,4},{8,9},{9,10},{10,1... | collective-permute-start | bytes 1572872 | tf_op jit(solution)/shard_map/ppermute | solution.py:604
  68.5 23.4 %copy-start.11 = (f32[32]{0:T(128)S(1)}, f32[32]{0:T(128)}, u32[]{:S(2)}) copy-start(f32[32]{0:T(128)} %param.16) | copy-start | bytes 388
  68.5 23.3 %copy-start.13 = (bf16[256,4096]{1,0:T(8,128)(2,1)S(1)}, bf16[256,4096]{1,0:T(8,128)(2,1)}, u32[]{:S(2)}) copy-start(bf16[256,4096]{1,0:T(8,128)(2,1)} %gate_ref.1) | copy-start | bytes 6291460
  84.4 14.0 %collective-permute-start.19 = (bf16[256,512]{1,0:T(8,128)(2,1)S(1)}, bf16[256,512]{1,0:T(8,128)(2,1)S(1)}, u32[]{:S(2)}, u32[]{:S(2)}) collective-permute-start(bf16[256,512]{1,0:T(8,128)(2,1)S(1)} %get-tuple-element.116), channel_id=1, source_target_pairs={{0,12},{4,0},{8,4},{12,8},{1,13},{5,1},{9,5},{13,9},{2,14},{6,2},{... | collective-permute-start | bytes 786440 | tf_op jit(solution)/shard_map/ppermute | solution.py:604
  85.1 13.4 %collective-permute-start.20 = (bf16[256,512]{1,0:T(8,128)(2,1)S(1)}, bf16[256,512]{1,0:T(8,128)(2,1)S(1)}, u32[]{:S(2)}, u32[]{:S(2)}) collective-permute-start(bf16[256,512]{1,0:T(8,128)(2,1)S(1)} %get-tuple-element.117), channel_id=1, source_target_pairs={{0,8},{4,12},{8,0},{12,4},{1,9},{5,13},{9,1},{13,5},{2,10},{6,14},... | collective-permute-start | bytes 786440 | tf_op jit(solution)/shard_map/ppermute | solution.py:604
  88.5 10.1 %collective-permute-start.21 = (bf16[256,512]{1,0:T(8,128)(2,1)S(1)}, bf16[256,512]{1,0:T(8,128)(2,1)S(1)}, u32[]{:S(2)}, u32[]{:S(2)}) collective-permute-start(bf16[256,512]{1,0:T(8,128)(2,1)S(1)} %get-tuple-element.118), channel_id=1, source_target_pairs={{0,4},{4,8},{8,12},{12,0},{1,5},{5,9},{9,13},{13,1},{2,6},{6,10},{... | collective-permute-start | bytes 786440 | tf_op jit(solution)/shard_map/ppermute | solution.py:604

commit v4 on v3

--- a/solution.py
+++ b/solution.py
@@ -95,81 +95,99 @@
     return log_decay
 
 
-def state_body(at_ref, x_ref, w_ref, dt_ref, rate_ref, *rest):
-    outs, first_ref, (to_end, total) = rest[:SIDE], rest[SIDE], rest[SIDE + 1 :]
-    s = pl.program_id(0)
+def state_body(at_ref, x_hbm, w_hbm, dt_hbm, rate_hbm, *rest):
+    outs, first_ref, (x_ref, w_ref, dt_ref, rate_ref, sems) = rest[:SIDE], rest[SIDE], rest[SIDE + 1 :]
     rows = dt_ref.shape[1]
     half = rows // 2
-    group = lax.rem(at_ref[1] + s, SIDE)
-
-    @pl.when(s == 0)
-    def _():
-        dt = jnp.transpose(dt_ref[...])
-        sums = span_sums(dt * (-jnp.exp(rate_ref[...])), half)
-        ends = jnp.concatenate(
-            [jnp.broadcast_to(sums[half * c + half - 1 : half * c + half], (half, SSD_HEADS)) for c in range(2)],
-            axis=0,
-        )
-        to_end[...] = jnp.exp(ends - sums) * dt
-        total[0:8, :] = ends[half : half + 8]
-        total[8:16, :] = ends[:8] + ends[half : half + 8]
-
-    for g in range(GROUPS):
-
-        @pl.when(group == g)
-        def _():
-            scaled, last, decays = [], [], []
-            for j in range(PER):
-                h = g * PER + j
-                scaled.append(
-                    (to_end[:, h : h + 1] * x_ref[:, j * D : (j + 1) * D].astype(F32)).astype(BF)
-                )
-                last.append(jnp.broadcast_to(total[0:1, h : h + 1], (1, D)))
-                decays.append(jnp.broadcast_to(total[8:16, h : h + 1], (8, D)))
-            scaled = jnp.concatenate(scaled, axis=1)
-            first, second = [
-                lax.dot_general(
-                    w_ref[c * half : (c + 1) * half, :],
-                    scaled[c * half : (c + 1) * half],
-                    (((0,), (0,)), ((), ())),
-                    preferred_element_type=F32,
-                )
-                for c in range(2)
-            ]
-            first_ref[0] = first
-            state = jnp.exp(jnp.concatenate(last, axis=1)) * first + second
-            decay = jnp.concatenate(decays, axis=1)
-            for t in range(SIDE):
-
-                @pl.when(s == t)
-                def _():
-                    outs[t][:D, :] = state
-                    outs[t][D:, :] = decay
+    width = PER * D
+    y = at_ref[1]
+    steps = pltpu.make_async_copy(dt_hbm, dt_ref, sems.at[2 * SIDE])
+    steps.start()
+    rates = pltpu.make_async_copy(rate_hbm, rate_ref, sems.at[2 * SIDE + 1])
+    rates.start()
+    arrivals = []
+    for s in (1, 3, 2, 0):
+        group = lax.rem(y + s, SIDE)
+        arrivals.append(
+            (
+                s,
+                pltpu.make_async_copy(
+                    w_hbm.at[:, columns(group, D)], w_ref.at[s], sems.at[SIDE + s]
+                ),
+                pltpu.make_async_copy(
+                    x_hbm.at[:, columns(group, width)], x_ref.at[s], sems.at[s]
+                ),
+            )
+        )
+    for _, w_copy, x_copy in arrivals:
+        w_copy.start()
+        x_copy.start()
+    steps.wait()
+    rates.wait()
+    dt = jnp.transpose(dt_ref[...])
+    sums = span_sums(dt * (-jnp.exp(rate_ref[...])), half)
+    ends = jnp.concatenate(
+        [jnp.broadcast_to(sums[half * c + half - 1 : half * c + half], (half, SSD_HEADS)) for c in range(2)],
+        axis=0,
+    )
+    to_end = jnp.exp(ends - sums) * dt
+    last = ends[half : half + 8]
+    total = ends[:8] + last
+    for s, w_copy, x_copy in arrivals:
+        turn = SSD_HEADS - PER * lax.rem(y + s, SIDE)
+        mine, last_mine, total_mine = [
+            pltpu.roll(jnp.concatenate([part] * (D // SSD_HEADS), axis=1), turn, 1)
+            for part in (to_end, last, total)
+        ]
+        w_copy.wait()
+        x_copy.wait()
+        scaled = jnp.concatenate(
+            [
+                (mine[:, j : j + 1] * x_ref[s, :, j * D : (j + 1) * D].astype(F32)).astype(BF)
+                for j in range(PER)
+            ],
+            axis=1,
+        )
+        first, second = [
+            lax.dot_general(
+                w_ref[s, c * half : (c + 1) * half, :],
+                scaled[c * half : (c + 1) * half],
+                (((0,), (0,)), ((), ())),
+                preferred_element_type=F32,
+            )
+            for c in range(2)
+        ]
+        first_ref[s] = first
+        decay = jnp.concatenate(
+            [jnp.broadcast_to(last_mine[0:1, j : j + 1], (1, D)) for j in range(PER)], axis=1
+        )
+        outs[s][:D, :] = jnp.exp(decay) * first + second
+        outs[s][D:, :] = jnp.concatenate(
+            [jnp.broadcast_to(total_mine[:, j : j + 1], (EXTRA, D)) for j in range(PER)], axis=1
+        )
 
 
 def local_states(at, x, w, dt, rate):
     rows = x.shape[0]
     width = PER * D
+    far = pl.BlockSpec(memory_space=pltpu.HBM)
+    near = pl.BlockSpec(memory_space=pltpu.VMEM)
     return pl.pallas_call(
         state_body,
-        grid_spec=pltpu.PrefetchScalarGridSpec(
-            num_scalar_prefetch=1,
-            grid=(SIDE,),
-            in_specs=[
-                pl.BlockSpec((rows, width), lambda s, at: (0, lax.rem(at[1] + s, SIDE))),
-                pl.BlockSpec((rows, D), lambda s, at: (0, lax.rem(at[1] + s, SIDE))),
-                pl.BlockSpec((SSD_HEADS, rows), lambda s, at: (0, 0)),
-                pl.BlockSpec((1, SSD_HEADS), lambda s, at: (0, 0)),
-            ],
-            out_specs=[pl.BlockSpec((D + EXTRA, width), lambda s, at: (0, 0))] * SIDE
-            + [pl.BlockSpec((1, D, width), lambda s, at: (s, 0, 0))],
-            scratch_shapes=[pltpu.VMEM((rows, SSD_HEADS), F32), pltpu.VMEM((16, SSD_HEADS), F32)],
-        ),
+        in_specs=[pl.BlockSpec(memory_space=pltpu.SMEM), far, far, far, far],
+        out_specs=[near] * (SIDE + 1),
+        scratch_shapes=[
+            pltpu.VMEM((SIDE, rows, width), BF),
+            pltpu.VMEM((SIDE, rows, D), BF),
+            pltpu.VMEM((SSD_HEADS, rows), F32),
+            pltpu.VMEM((1, SSD_HEADS), F32),
+            pltpu.SemaphoreType.DMA((2 * SIDE + 2,)),
+        ],
         out_shape=[jax.ShapeDtypeStruct((D + EXTRA, width), F32)] * SIDE
         + [jax.ShapeDtypeStruct((SIDE, D, width), F32)],
         compiler_params=params(),
         name="local_states",
-    )(at, x, w, dt, rate)
+    )(at, *[pltpu.with_memory_space_constraint(part, pltpu.HBM) for part in (x, w, dt, rate)])
 
 
 def flag(condition):
@@ -346,96 +364,71 @@
 def ssd_body(
     at_ref, inside_ref, gate_ref, r_ref, dt_ref, rate_ref, gain_ref, first_ref, *rest
 ):
-    starts, out_ref, (grown, ends, gated) = rest[:SIDE], rest[SIDE], rest[SIDE + 1 :]
-    s = pl.program_id(0)
+    starts, out_hbm, (gated, staged, sems) = rest[:SIDE], rest[SIDE], rest[SIDE + 1 :]
+    y = at_ref[1]
     rows = dt_ref.shape[1]
     half = rows // 2
-    group = lax.rem(at_ref[1] + s, SIDE)
-    spans = [slice(c * half, (c + 1) * half) for c in range(2)]
-
-    @pl.when(s == 0)
-    def _():
-        sums = span_sums(jnp.transpose(dt_ref[...]) * (-jnp.exp(rate_ref[...])), half)
-        grown[...] = jnp.exp(sums)
-        ends[...] = jnp.broadcast_to(jnp.exp(sums[half - 1 : half]), ends.shape)
-
-    for g in range(GROUPS):
-
-        @pl.when(group == g)
-        def _():
-            decay = jnp.concatenate(
-                [
-                    jnp.broadcast_to(ends[0:1, g * PER + j : g * PER + j + 1], (1, D))
-                    for j in range(PER)
-                ],
-                axis=1,
-            )
-            for t in range(SIDE):
-
-                @pl.when(s == t)
-                def _():
-                    start = starts[t][...]
-                    gated[spans[0], :] = jnp.dot(
-                        r_ref[spans[0], :], start.astype(BF), preferred_element_type=F32
-                    )
-                    gated[spans[1], :] = jnp.dot(
-                        r_ref[spans[1], :],
-                        (decay * start + first_ref[0]).astype(BF),
-                        preferred_element_type=F32,
-                    )
-
-            square = jnp.zeros((rows, D), F32)
-            for j in range(PER):
-                h = g * PER + j
-                lanes = slice(j * D, (j + 1) * D)
-                mixed = inside_ref[:, lanes] + grown[:, h : h + 1] * gated[:, lanes]
-                gate = gate_ref[:, lanes].astype(F32)
-                value = mixed * (gate * (0.5 + 0.5 * jnp.tanh(0.5 * gate)))
-                gated[:, lanes] = value
-                square = square + value * value
-            mean = jnp.sum(square, axis=1, keepdims=True) * (1.0 / (PER * D))
-            inverse = lax.rsqrt(mean + 1e-05)
-            for j in range(PER):
-                lanes = slice(j * D, (j + 1) * D)
-                out_ref[:, lanes] = (
-                    gated[:, lanes] * inverse * gain_ref[:, lanes].astype(F32)
-                ).astype(BF)
+    width = PER * D
+    sums = span_sums(jnp.transpose(dt_ref[...]) * (-jnp.exp(rate_ref[...])), half)
+    ends = jnp.broadcast_to(sums[half - 1 : half], (8, SSD_HEADS))
+    copies = []
+    for s in (0, 1, 3, 2):
+        group = lax.rem(y + s, SIDE)
+        turn = SSD_HEADS - PER * group
+        grown, decay = [
+            jnp.exp(pltpu.roll(jnp.concatenate([part] * (D // SSD_HEADS), axis=1), turn, 1))
+            for part in (sums, ends)
+        ]
+        decay = jnp.concatenate(
+            [jnp.broadcast_to(decay[0:1, j : j + 1], (1, D)) for j in range(PER)], axis=1
+        )
+        read = r_ref[:, columns(group, D)]
+        start = starts[s][...]
+        gated[:half, :] = jnp.dot(read[:half], start.astype(BF), preferred_element_type=F32)
+        gated[half:, :] = jnp.dot(
+            read[half:], (decay * start + first_ref[s]).astype(BF), preferred_element_type=F32
+        )
+        square = jnp.zeros((rows, D), F32)
+        for j in range(PER):
+            lanes = slice(j * D, (j + 1) * D)
+            there = columns(group * PER + j, D)
+            mixed = inside_ref[:, there] + grown[:, j : j + 1] * gated[:, lanes]
+            gate = gate_ref[:, there].astype(F32)
+            value = mixed * (gate * (0.5 + 0.5 * jnp.tanh(0.5 * gate)))
+            gated[:, lanes] = value
+            square = square + value * value
+        mean = jnp.sum(square, axis=1, keepdims=True) * (1.0 / width)
+        inverse = lax.rsqrt(mean + 1e-05)
+        for j in range(PER):
+            lanes = slice(j * D, (j + 1) * D)
+            there = columns(group * PER + j, D)
+            staged[s, :, lanes] = (
+                gated[:, lanes] * inverse * gain_ref[:, there].astype(F32)
+            ).astype(BF)
+        copy = pltpu.make_async_copy(
+            staged.at[s], out_hbm.at[:, columns(group, width)], sems.at[s]
+        )
+        copy.start()
+        copies.append(copy)
+    for copy in copies:
+        copy.wait()
 
 
 def ssd_out_of(at, inside, gate, r, dt, rate, gain, first, starts):
     rows = inside.shape[0]
     width = PER * D
-
-    def turned(s, at):
-        return (0, lax.rem(at[1] + s, SIDE))
-
-    def fixed(s, at):
-        return (0, 0)
-
+    near = pl.BlockSpec(memory_space=pltpu.VMEM)
     return pl.pallas_call(
         ssd_body,
-        grid_spec=pltpu.PrefetchScalarGridSpec(
-            num_scalar_prefetch=1,
-            grid=(SIDE,),
-            in_specs=[
-                pl.BlockSpec((rows, width), turned),
-                pl.BlockSpec((rows, width), turned),
-                pl.BlockSpec((rows, D), turned),
-                pl.BlockSpec((SSD_HEADS, rows), fixed),
-                pl.BlockSpec((1, SSD_HEADS), fixed),
-                pl.BlockSpec((1, width), turned),
-                pl.BlockSpec((1, D, width), lambda s, at: (s, 0, 0)),
-            ]
-            + [pl.BlockSpec((D, width), fixed)] * SIDE,
-            out_specs=pl.BlockSpec((rows, width), turned),
-            scratch_shapes=[
-                pltpu.VMEM((rows, SSD_HEADS), F32),
-                pltpu.VMEM((8, SSD_HEADS), F32),
-                pltpu.VMEM((rows, width), F32),
-            ],
-        ),
+        in_specs=[pl.BlockSpec(memory_space=pltpu.SMEM)] + [near] * (7 + SIDE),
+        out_specs=pl.BlockSpec(memory_space=pltpu.HBM),
+        scratch_shapes=[
+            pltpu.VMEM((rows, width), F32),
+            pltpu.VMEM((SIDE, rows, width), BF),
+            pltpu.SemaphoreType.DMA((SIDE,)),
+        ],
         out_shape=jax.ShapeDtypeStruct(gate.shape, BF),
-        compiler_params=params(),
+        compiler_params=params(24),
         cost_estimate=about(8),
         name="ssd_out",
     )(at, inside, gate, r, dt, rate, gain, first, *starts)
@@ -463,25 +456,12 @@
 
 
 def attention_body(at_ref, *rest):
-    pieces, parts, outs = rest[:SIDE], rest[SIDE : 2 * SIDE - 1], rest[2 * SIDE - 1 : 3 * SIDE - 1]
-    qs, kk, va, acc, top = rest[3 * SIDE - 1 :]
+    pieces, parts, outs = rest[:SIDE], rest[SIDE : 2 * SIDE], rest[2 * SIDE : 3 * SIDE]
+    qs, acc, top = rest[3 * SIDE :]
     place = pl.program_id(0)
     x, y = at_ref[0], at_ref[1]
     rows = pieces[0].shape[0]
-    keys = SIDE * rows
-
-    @pl.when(place == 0)
-    def _():
-        for c in range(SIDE):
-            for u in range(SIDE):
-                if u == 0:
-                    source = pieces[c]
-                else:
-                    source = parts[u - 1].at[c * rows : (c + 1) * rows, :]
-                to = slice(c * keys + u * rows, c * keys + (u + 1) * rows)
-                kk[to, :] = source[:, :D]
-                va[to, :D] = source[:, D : 2 * D]
-        va[:, D:] = jnp.ones((SIDE * keys, D), BF)
+    ones = jnp.ones((rows, D), BF)
 
     for s in range(SIDE):
 
@@ -493,8 +473,7 @@
     top[...] = jnp.full_like(top, NEG)
 
     def chunk(c, newest):
-        where = pl.ds(pl.multiple_of(lax.rem(x - c + SIDE, SIDE) * keys, keys), keys)
-        kc, vc = kk.at[where, :], va.at[where, :]
+        where = pl.ds(pl.multiple_of(lax.rem(x - c + SIDE, SIDE) * rows, rows), rows)
         if newest:
             causal = lax.broadcasted_iota(jnp.int32, (rows, rows), 1) <= lax.broadcasted_iota(
                 jnp.int32, (rows, rows), 0
@@ -506,7 +485,7 @@
 
         def scores(h):
             mine = qs[h * 2 * rows : (h + 1) * 2 * rows, :]
-            found = [row_dot(mine, kc[u * rows : (u + 1) * rows, :]) for u in range(SIDE)]
+            found = [row_dot(mine, part[where, :D]) for part in parts]
             if newest:
                 found[0] = jnp.where(jnp.concatenate([causal, causal], axis=0), found[0], NEG)
             return found
@@ -527,9 +506,8 @@
             for u in range(SIDE):
                 base = wide - shown[u] if newest and u else wide
                 weights = jnp.exp2((now[u] - base) * SCALE).astype(BF)
-                out = out + jnp.dot(
-                    weights, vc[u * rows : (u + 1) * rows, :], preferred_element_type=F32
-                )
+                values = jnp.concatenate([parts[u][where, D:], ones], axis=1)
+                out = out + jnp.dot(weights, values, preferred_element_type=F32)
             acc[mine, :] = out
             now = following
 
@@ -551,23 +529,18 @@
 def attention(at, pieces, parts):
     rows, width = pieces[0].shape
     given = width - 2 * D
-    keys = parts[0].shape[0]
-
-    def fixed(place, at):
-        return (0, 0)
+
+    near = pl.BlockSpec(memory_space=pltpu.VMEM)
 
     return pl.pallas_call(
         attention_body,
         grid_spec=pltpu.PrefetchScalarGridSpec(
             num_scalar_prefetch=1,
             grid=(SIDE,),
-            in_specs=[pl.BlockSpec((rows, width), fixed)] * SIDE
-            + [pl.BlockSpec((keys, 2 * D), fixed)] * (SIDE - 1),
-            out_specs=[pl.BlockSpec((rows, given), fixed)] * SIDE,
+            in_specs=[near] * (2 * SIDE),
+            out_specs=[near] * SIDE,
             scratch_shapes=[
                 pltpu.VMEM((NQ * rows, D), BF),
-                pltpu.VMEM((SIDE * keys, D), BF),
-                pltpu.VMEM((SIDE * keys, 2 * D), BF),
                 pltpu.VMEM((NQ * rows, 2 * D), F32),
                 pltpu.VMEM((NQ * rows, D), F32),
             ],
@@ -580,10 +553,18 @@
 
 
 def unpack_body(at_ref, *refs):
-    ins, out = refs[:SIDE], refs[SIDE]
+    ins, out, sems = refs[:SIDE], refs[SIDE], refs[SIDE + 1]
     width = ins[0].shape[1]
-    for s in range(SIDE):
-        out[:, columns(lax.rem(at_ref[0] + s, SIDE), width)] = ins[s][...]
+    copies = [
+        pltpu.make_async_copy(
+            ins[s], out.at[:, columns(lax.rem(at_ref[0] + s, SIDE), width)], sems.at[s]
+        )
+        for s in range(SIDE)
+    ]
+    for copy in copies:
+        copy.start()
+    for copy in copies:
+        copy.wait()
 
 
 def unpack(at, pieces):
@@ -592,8 +573,9 @@
         unpack_body,
         in_specs=[pl.BlockSpec(memory_space=pltpu.SMEM)]
         + [pl.BlockSpec(memory_space=pltpu.VMEM)] * SIDE,
-        out_specs=pl.BlockSpec(memory_space=pltpu.VMEM),
+        out_specs=pl.BlockSpec(memory_space=pltpu.HBM),
         out_shape=jax.ShapeDtypeStruct((rows, SIDE * width), BF),
+        scratch_shapes=[pltpu.SemaphoreType.DMA((SIDE,))],
         compiler_params=params(),
         cost_estimate=about(2),
         name="unpack",
@@ -637,7 +619,7 @@
     starts = start_states(at, states, entering)
     starts, pieces = tie((starts, pieces))
     starts = exchange(starts, "y", -1)
-    parts = [before, jnp.concatenate(far, axis=0), after]
+    parts = [own, before, jnp.concatenate(far, axis=0), after]
     back = exchange(attention(at, pieces, parts), "x", -1)
     ssd = ssd_out_of(at, inside, gate_input, read_map, step_size, rate, gain, first, starts)
     ssd, back = tie((ssd, back))

time: 101 us -> 96.4 us (0.954)
  local copies, waits for them, and re-layouts: 4.13 us -> 0.11 us
  waiting for transfers between devices: 25.3 us -> 27 us
  Pallas kernels: 36.6 us -> 35 us
    unnamed x30 -> x22, local copies, waits for them, and re-layouts: 4.08 us -> 0.06 us
    ppermute x22, waiting for transfers between devices: 25.3 us -> 27 us  [shifted(): lax.ppermute(value, axis, [(i, (i + by) % SIDE) for i in range(SIDE)])]
    pallas_call x2, Pallas kernels: 10.4 us -> 9.25 us  [the longest x1 5.04 us: ssd_out_of(): pl.pallas_call(ssd_body, in_specs=[pl.BlockSpec(memory_space=pltpu.SMEM)]...]
where the time goes in v4:
time: 96.4 us; the launch traced here: 96.2 us
  Pallas kernels  35 us (36%)
  starting transfers between devices  32.9 us (34%)
  waiting for transfers between devices  27 us (28%)
  between operations  1.07 us (1%)
    ppermute x22, starting transfers between devices, shifted(): lax.ppermute(value, axis, [(i, (i + by) % SIDE) for i in range(SIDE)])  32.9 us
    ppermute x22, waiting for transfers between devices, shifted(): lax.ppermute(value, axis, [(i, (i + by) % SIDE) for i in range(SIDE)])  27 us
    pallas_call x1, Pallas kernels, attention(): pl.pallas_call(attention_body, grid_spec=pltpu.PrefetchScalarGridSpec(num...  15.4 us
    pallas_call x1, Pallas kernels, ssd_out_of(): pl.pallas_call(ssd_body, in_specs=[pl.BlockSpec(memory_space=pltpu.SMEM)]...  5.04 us
    pallas_call x1, Pallas kernels, inside_spans(): pl.pallas_call(inside_body, grid_spec=pltpu.PrefetchScalarGridSpec(num_sc...  4.65 us
    pallas_call x1, Pallas kernels, local_states(): pl.pallas_call(state_body, in_specs=[pl.BlockSpec(memory_space=pltpu.SMEM...  4.21 us
  transfers between devices with their start and end apart: 22, of which 12 were waited for; matrix products, arithmetic and copies ran while one was open for 0% of the time, Pallas kernels for 30%

profile of v4, /device:TPU:64, one launch (start us, length us, event | category | flops | bytes accessed | tf_op | source)
XLA Modules:
  0.0 96.2 jit_solution(16930481509443699604)
XLA Ops:
  0.6 0.0 copy-start.3
  0.6 0.0 copy-start.2
  0.7 0.0 copy-start
  0.7 0.1 pad_add_fusion.at_ref
  0.7 4.2 %local_states.1 = (f32[136,1024]{1,0:T(8,128)S(1)}, f32[136,1024]{1,0:T(8,128)S(1)}, f32[136,1024]{1,0:T(8,128)S(1)}, f32[136,1024]{1,0:T(8,128)S(1)}, f32[4,128,1024]{2,1,0:T(8,128)S(1)}) custom-call(s32[2]{0:T(128)S(1)} %pad_add_fusion.at_ref, bf16[256,4096]{1,0:T(8,128)(2,1)} %x_ref.1, bf16[256,512]{1,0:T(8,128)(2,1)} %w_ref.1, f32[32,256]{1,0:T(8,128)} %bitcast.5, ...), custom_call_target="tpu_custom_call" | custom-call | tf_op jit(solution)/shard_map/local_states/pallas_call | solution.py:175
  5.0 0.0 copy-start.1
  5.0 0.0 copy-start.4
  5.0 0.0 copy-start.5
  5.0 0.0 copy-start.6
  5.0 0.0 copy-start.7
  5.1 0.0 copy-start.8
  5.1 0.8 pack.1
  5.9 1.6 %collective-permute-start.3 = (bf16[256,768]{1,0:T(8,128)(2,1)S(1)}, bf16[256,768]{1,0:T(8,128)(2,1)S(1)}, u32[]{:S(2)}, u32[]{:S(2)}) collective-permute-start(bf16[256,768]{1,0:T(8,128)(2,1)S(1)} %get-tuple-element.75), channel_id=1, source_target_pairs={{0,4},{4,8},{8,12},{12,0},{1,5},{5,9},{9,13},{13,1},{2,6},{6,10},{... | collective-permute-start | bytes 1179656 | tf_op jit(solution)/shard_map/ppermute | solution.py:586
  7.4 1.6 %collective-permute-start = (f32[136,1024]{1,0:T(8,128)S(1)}, f32[136,1024]{1,0:T(8,128)S(1)}, u32[]{:S(2)}, u32[]{:S(2)}) collective-permute-start(f32[136,1024]{1,0:T(8,128)S(1)} %get-tuple-element.68), channel_id=1, source_target_pairs={{0,1},{1,2},{2,3},{3,0},{4,5},{5,6},{6,7},{7,4},{8,9},{9,10},{10,1... | collective-permute-start | bytes 1671176 | tf_op jit(solution)/shard_map/ppermute | solution.py:586
  9.0 2.9 %collective-permute-start.1 = (f32[136,1024]{1,0:T(8,128)S(1)}, f32[136,1024]{1,0:T(8,128)S(1)}, u32[]{:S(2)}, u32[]{:S(2)}) collective-permute-start(f32[136,1024]{1,0:T(8,128)S(1)} %get-tuple-element.69), channel_id=1, source_target_pairs={{0,2},{1,3},{2,0},{3,1},{4,6},{5,7},{6,4},{7,5},{8,10},{9,11},{10,... | collective-permute-start | bytes 1671176 | tf_op jit(solution)/shard_map/ppermute | solution.py:586
  11.9 1.3 %collective-permute-start.2 = (f32[136,1024]{1,0:T(8,128)S(1)}, f32[136,1024]{1,0:T(8,128)S(1)}, u32[]{:S(2)}, u32[]{:S(2)}) collective-permute-start(f32[136,1024]{1,0:T(8,128)S(1)} %get-tuple-element.70), channel_id=1, source_target_pairs={{0,3},{1,0},{2,1},{3,2},{4,7},{5,4},{6,5},{7,6},{8,11},{9,8},{10,9... | collective-permute-start | bytes 1671176 | tf_op jit(solution)/shard_map/ppermute | solution.py:586
  13.3 2.7 %collective-permute-start.4 = (bf16[256,768]{1,0:T(8,128)(2,1)S(1)}, bf16[256,768]{1,0:T(8,128)(2,1)S(1)}, u32[]{:S(2)}, u32[]{:S(2)}) collective-permute-start(bf16[256,768]{1,0:T(8,128)(2,1)S(1)} %get-tuple-element.76), channel_id=1, source_target_pairs={{0,8},{4,12},{8,0},{12,4},{1,9},{5,13},{9,1},{13,5},{2,10},{6,14},... | collective-permute-start | bytes 1179656 | tf_op jit(solution)/shard_map/ppermute | solution.py:586
  16.0 2.2 %collective-permute-done.3.refs_1_.rest_1_ = bf16[256,768]{1,0:T(8,128)(2,1)S(1)} collective-permute-done((bf16[256,768]{1,0:T(8,128)(2,1)S(1)}, bf16[256,768]{1,0:T(8,128)(2,1)S(1)}, u32[]{:S(2)}, u32[]{:S(2)}) %collective-permute-start.3) | collective-permute-done | bytes 393248 | tf_op jit(solution)/shard_map/ppermute | solution.py:586
  18.2 2.5 %collective-permute-start.5 = (bf16[256,768]{1,0:T(8,128)(2,1)S(1)}, bf16[256,768]{1,0:T(8,128)(2,1)S(1)}, u32[]{:S(2)}, u32[]{:S(2)}) collective-permute-start(bf16[256,768]{1,0:T(8,128)(2,1)S(1)} %get-tuple-element.77), channel_id=1, source_target_pairs={{0,12},{4,0},{8,4},{12,8},{1,13},{5,1},{9,5},{13,9},{2,14},{6,2},{... | collective-permute-start | bytes 1179656 | tf_op jit(solution)/shard_map/ppermute | solution.py:586
  20.8 4.6 %inside_spans.1.inside_ref = f32[256,4096]{1,0:T(8,128)S(1)} custom-call(s32[2]{0:T(128)S(1)} %pad_add_fusion.at_ref, bf16[256,4096]{1,0:T(8,128)(2,1)S(1)} %copy-done.1, bf16[256,512]{1,0:T(8,128)(2,1)S(1)} %copy-done.4, bf16[256,512]{1,0:T(8,128)(2,1)S(1)} %copy-done.5, f32[32,256]{1,0:T(8,128)S(1)} %bitcast.6, f32[1,32]{1,0:T(1,128)S(1)} %bitcast.9, ...), custom_call_target="tpu_custom_call" | custom-call | tf_op jit(solution)/shard_map/inside_spans/pallas_call | solution.py:339
  25.4 2.0 %collective-permute-done.4.refs_2_.rest_2_ = bf16[256,768]{1,0:T(8,128)(2,1)S(1)} collective-permute-done((bf16[256,768]{1,0:T(8,128)(2,1)S(1)}, bf16[256,768]{1,0:T(8,128)(2,1)S(1)}, u32[]{:S(2)}, u32[]{:S(2)}) %collective-permute-start.4) | collective-permute-done | bytes 393248 | tf_op jit(solution)/shard_map/ppermute | solution.py:586
  27.4 4.6 %collective-permute-done.5.refs_3_.rest_3_ = bf16[256,768]{1,0:T(8,128)(2,1)S(1)} collective-permute-done((bf16[256,768]{1,0:T(8,128)(2,1)S(1)}, bf16[256,768]{1,0:T(8,128)(2,1)S(1)}, u32[]{:S(2)}, u32[]{:S(2)}) %collective-permute-start.5) | collective-permute-done | bytes 393248 | tf_op jit(solution)/shard_map/ppermute | solution.py:586
  32.1 0.3 collective-permute-start.10
  32.4 1.8 %collective-permute-start.9 = (bf16[1024,256]{1,0:T(8,128)(2,1)S(1)}, bf16[1024,256]{1,0:T(8,128)(2,1)S(1)}, u32[]{:S(2)}, u32[]{:S(2)}) collective-permute-start(bf16[1024,256]{1,0:T(8,128)(2,1)S(1)} %stack.13.rest_4_), channel_id=1, source_target_pairs={{0,1},{1,2},{2,3},{3,0},{4,5},{5,6},{6,7},{7,4},{8,9},{9,10},{10,1... | collective-permute-start | bytes 1572872 | tf_op jit(solution)/shard_map/ppermute | solution.py:586
  34.2 0.0 collective-permute-done.refs_1_
  34.2 3.2 %collective-permute-done.1.refs_2_ = f32[136,1024]{1,0:T(8,128)S(1)} collective-permute-done((f32[136,1024]{1,0:T(8,128)S(1)}, f32[136,1024]{1,0:T(8,128)S(1)}, u32[]{:S(2)}, u32[]{:S(2)}) %collective-permute-start.1) | collective-permute-done | bytes 557088 | tf_op jit(solution)/shard_map/ppermute | solution.py:586
  37.4 0.0 collective-permute-done.2.refs_3_
  37.4 0.9 row_total.1
  38.3 0.1 collective-permute-start.6
  38.4 2.7 %collective-permute-start.7 = (f32[136,256]{1,0:T(8,128)S(1)}, f32[136,256]{1,0:T(8,128)S(1)}, u32[]{:S(2)}, u32[]{:S(2)}) collective-permute-start(f32[136,256]{1,0:T(8,128)S(1)} %get-tuple-element.87), channel_id=1, source_target_pairs={{0,8},{4,12},{8,0},{12,4},{1,9},{5,13},{9,1},{13,5},{2,10},{6,14},... | collective-permute-start | bytes 417800 | tf_op jit(solution)/shard_map/ppermute | solution.py:586
  41.1 2.4 %collective-permute-start.8 = (f32[136,256]{1,0:T(8,128)S(1)}, f32[136,256]{1,0:T(8,128)S(1)}, u32[]{:S(2)}, u32[]{:S(2)}) collective-permute-start(f32[136,256]{1,0:T(8,128)S(1)} %get-tuple-element.88), channel_id=1, source_target_pairs={{0,12},{4,0},{8,4},{12,8},{1,13},{5,1},{9,5},{13,9},{2,14},{6,2},{... | collective-permute-start | bytes 417800 | tf_op jit(solution)/shard_map/ppermute | solution.py:586
  43.4 2.7 %collective-permute-done.6.refs_1_ = f32[136,256]{1,0:T(8,128)S(1)} collective-permute-done((f32[136,256]{1,0:T(8,128)S(1)}, f32[136,256]{1,0:T(8,128)S(1)}, u32[]{:S(2)}, u32[]{:S(2)}) %collective-permute-start.6) | collective-permute-done | bytes 139296 | tf_op jit(solution)/shard_map/ppermute | solution.py:586
  46.1 0.0 collective-permute-done.7.refs_2_
  46.1 0.9 collective-permute-done.8.refs_3_
  47.0 0.7 entering_rows.1
  47.7 0.0 collective-permute-done.10.rest_7_
  47.7 0.0 collective-permute-done.9.rest_5_
  47.7 2.8 %collective-permute-start.11 = (f32[128,256]{1,0:T(8,128)S(1)}, f32[128,256]{1,0:T(8,128)S(1)}, u32[]{:S(2)}, u32[]{:S(2)}) collective-permute-start(f32[128,256]{1,0:T(8,128)S(1)} %get-tuple-element.98), channel_id=1, source_target_pairs={{0,12},{4,0},{8,4},{12,8},{1,13},{5,1},{9,5},{13,9},{2,14},{6,2},{... | collective-permute-start | bytes 393224 | tf_op jit(solution)/shard_map/ppermute | solution.py:586
  50.5 1.3 %collective-permute-start.12 = (f32[128,256]{1,0:T(8,128)S(1)}, f32[128,256]{1,0:T(8,128)S(1)}, u32[]{:S(2)}, u32[]{:S(2)}) collective-permute-start(f32[128,256]{1,0:T(8,128)S(1)} %get-tuple-element.99), channel_id=1, source_target_pairs={{0,8},{4,12},{8,0},{12,4},{1,9},{5,13},{9,1},{13,5},{2,10},{6,14},... | collective-permute-start | bytes 393224 | tf_op jit(solution)/shard_map/ppermute | solution.py:586
  51.8 0.0 collective-permute-start.13
  51.8 2.6 %collective-permute-start.18 = (bf16[512,256]{1,0:T(8,128)(2,1)S(1)}, bf16[512,256]{1,0:T(8,128)(2,1)S(1)}, u32[]{:S(2)}, u32[]{:S(2)}) collective-permute-start(bf16[512,256]{1,0:T(8,128)(2,1)S(1)} %slice.7), channel_id=1, source_target_pairs={{0,3},{1,0},{2,1},{3,2},{4,7},{5,4},{6,5},{7,6},{8,11},{9,8},{10,9... | collective-permute-start | bytes 786440 | tf_op jit(solution)/shard_map/ppermute | solution.py:586
  54.4 0.0 collective-permute-start.17
  54.5 0.3 collective-permute-done.11.refs_5_
  54.7 2.3 %collective-permute-done.12.refs_6_ = f32[128,256]{1,0:T(8,128)S(1)} collective-permute-done((f32[128,256]{1,0:T(8,128)S(1)}, f32[128,256]{1,0:T(8,128)S(1)}, u32[]{:S(2)}, u32[]{:S(2)}) %collective-permute-start.12) | collective-permute-done | bytes 131104 | tf_op jit(solution)/shard_map/ppermute | solution.py:586
  57.0 1.4 %collective-permute-done.13.refs_7_ = f32[128,256]{1,0:T(8,128)S(1)} collective-permute-done((f32[128,256]{1,0:T(8,128)S(1)}, f32[128,256]{1,0:T(8,128)S(1)}, u32[]{:S(2)}, u32[]{:S(2)}) %collective-permute-start.13) | collective-permute-done | bytes 131104 | tf_op jit(solution)/shard_map/ppermute | solution.py:586
  58.4 1.7 %start_states.1 = (f32[128,1024]{1,0:T(8,128)S(1)}, f32[128,1024]{1,0:T(8,128)S(1)}, f32[128,1024]{1,0:T(8,128)S(1)}, f32[128,1024]{1,0:T(8,128)S(1)}) custom-call(s32[2]{0:T(128)S(1)} %pad_add_fusion.at_ref, f32[136,1024]{1,0:T(8,128)S(1)} %get-tuple-element.81.refs_0_, f32[136,1024]{1,0:T(8,128)S(1)} %collective-permute-done.refs_1_, ...), custom_call_target="tpu_custom_call" | custom-call | flops 2000000000 | bytes 6000000 | tf_op jit(solution)/shard_map/start_states/pallas_call | solution.py:280
  60.0 3.1 %collective-permute-start.14 = (f32[128,1024]{1,0:T(8,128)S(1)}, f32[128,1024]{1,0:T(8,128)S(1)}, u32[]{:S(2)}, u32[]{:S(2)}) collective-permute-start(f32[128,1024]{1,0:T(8,128)S(1)} %get-tuple-element.106), channel_id=1, source_target_pairs={{0,3},{1,0},{2,1},{3,2},{4,7},{5,4},{6,5},{7,6},{8,11},{9,8},{10,9... | collective-permute-start | bytes 1572872 | tf_op jit(solution)/shard_map/ppermute | solution.py:586
  63.2 0.2 collective-permute-start.15
  63.3 1.3 %collective-permute-start.16 = (f32[128,1024]{1,0:T(8,128)S(1)}, f32[128,1024]{1,0:T(8,128)S(1)}, u32[]{:S(2)}, u32[]{:S(2)}) collective-permute-start(f32[128,1024]{1,0:T(8,128)S(1)} %get-tuple-element.108), channel_id=1, source_target_pairs={{0,1},{1,2},{2,3},{3,0},{4,5},{5,6},{6,7},{7,4},{8,9},{9,10},{10,1... | collective-permute-start | bytes 1572872 | tf_op jit(solution)/shard_map/ppermute | solution.py:586
  64.7 0.0 collective-permute-done.18
  64.7 0.0 collective-permute-done.17
  64.7 0.0 copy-start.9
  64.7 15.4 %attention.1 = (bf16[256,512]{1,0:T(8,128)(2,1)S(1)}, bf16[256,512]{1,0:T(8,128)(2,1)S(1)}, bf16[256,512]{1,0:T(8,128)(2,1)S(1)}, bf16[256,512]{1,0:T(8,128)(2,1)S(1)}) custom-call(s32[2]{0:T(128)S(1)} %pad_add_fusion.at_ref, bf16[256,768]{1,0:T(8,128)(2,1)S(1)} %get-tuple-element.109.refs_0_.rest_0_, ...), custom_call_target="tpu_custom_call" | custom-call | flops 17999998976 | bytes 54000000 | tf_op jit(solution)/shard_map/attention/pallas_call | solution.py:535
  80.1 0.6 collective-permute-start.19
  80.8 1.1 %collective-permute-start.20 = (bf16[256,512]{1,0:T(8,128)(2,1)S(1)}, bf16[256,512]{1,0:T(8,128)(2,1)S(1)}, u32[]{:S(2)}, u32[]{:S(2)}) collective-permute-start(bf16[256,512]{1,0:T(8,128)(2,1)S(1)} %get-tuple-element.117), channel_id=1, source_target_pairs={{0,8},{4,12},{8,0},{12,4},{1,9},{5,13},{9,1},{13,5},{2,10},{6,14},... | collective-permute-start | bytes 786440 | tf_op jit(solution)/shard_map/ppermute | solution.py:586
  81.9 2.8 %collective-permute-done.14.rest_1_ = f32[128,1024]{1,0:T(8,128)S(1)} collective-permute-done((f32[128,1024]{1,0:T(8,128)S(1)}, f32[128,1024]{1,0:T(8,128)S(1)}, u32[]{:S(2)}, u32[]{:S(2)}) %collective-permute-start.14) | collective-permute-done | bytes 524320 | tf_op jit(solution)/shard_map/ppermute | solution.py:586
  84.6 0.0 collective-permute-start.21
  84.6 0.0 collective-permute-done.15.rest_2_
  84.6 3.4 %collective-permute-done.16.rest_3_ = f32[128,1024]{1,0:T(8,128)S(1)} collective-permute-done((f32[128,1024]{1,0:T(8,128)S(1)}, f32[128,1024]{1,0:T(8,128)S(1)}, u32[]{:S(2)}, u32[]{:S(2)}) %collective-permute-start.16) | collective-permute-done | bytes 524320 | tf_op jit(solution)/shard_map/ppermute | solution.py:586
  88.1 5.0 %ssd_out.1 = bf16[256,4096]{1,0:T(8,128)(2,1)} custom-call(s32[2]{0:T(128)S(1)} %pad_add_fusion.at_ref, f32[256,4096]{1,0:T(8,128)S(1)} %inside_spans.1.inside_ref, bf16[256,4096]{1,0:T(8,128)(2,1)S(1)} %copy-done.9, bf16[256,512]{1,0:T(8,128)(2,1)S(1)} %copy-done.5, f32[32,256]{1,0:T(8,128)S(1)} %bitcast.7, f32[1,32]{1,0:T(1,128)S(1)} %bitcast.10, ...), custom_call_target="tpu_custom_call" | custom-call | flops 8000000000 | bytes 24000000 | tf_op jit(solution)/shard_map/ssd_out/pallas_call | solution.py:421
  93.1 0.0 collective-permute-done.19.refs_1_
  93.1 0.0 collective-permute-done.20.refs_2_
  93.1 1.4 %collective-permute-done.21.refs_3_ = bf16[256,512]{1,0:T(8,128)(2,1)S(1)} collective-permute-done((bf16[256,512]{1,0:T(8,128)(2,1)S(1)}, bf16[256,512]{1,0:T(8,128)(2,1)S(1)}, u32[]{:S(2)}, u32[]{:S(2)}) %collective-permute-start.21) | collective-permute-done | bytes 262176 | tf_op jit(solution)/shard_map/ppermute | solution.py:586
  94.5 1.5 %unpack.1 = bf16[256,2048]{1,0:T(8,128)(2,1)} custom-call(s32[2]{0:T(128)S(1)} %pad_add_fusion.at_ref, bf16[256,512]{1,0:T(8,128)(2,1)S(1)} %get-tuple-element.120.refs_0_, bf16[256,512]{1,0:T(8,128)(2,1)S(1)} %collective-permute-done.19.refs_1_, bf16[256,512]{1,0:T(8,128)(2,1)S(1)} %collective-permute-done.20.refs_2_, ...), custom_call_target="tpu_custom_call" | custom-call | flops 2000000000 | bytes 6000000 | tf_op jit(solution)/shard_map/unpack/pallas_call | solution.py:572
  (17 shorter events, 0.1 us)
Async XLA Ops:
  0.6 4.3 %copy-start.3 = (bf16[256,512]{1,0:T(8,128)(2,1)S(1)}, bf16[256,512]{1,0:T(8,128)(2,1)}, u32[]{:S(2)}) copy-start(bf16[256,512]{1,0:T(8,128)(2,1)} %refs_10_) | copy-start | bytes 786436
  0.6 4.3 %copy-start.2 = (bf16[256,512]{1,0:T(8,128)(2,1)S(1)}, bf16[256,512]{1,0:T(8,128)(2,1)}, u32[]{:S(2)}) copy-start(bf16[256,512]{1,0:T(8,128)(2,1)} %refs_9_) | copy-start | bytes 786436
  0.7 4.3 %copy-start = (bf16[256,2048]{1,0:T(8,128)(2,1)S(1)}, bf16[256,2048]{1,0:T(8,128)(2,1)}, u32[]{:S(2)}) copy-start(bf16[256,2048]{1,0:T(8,128)(2,1)} %refs_11_) | copy-start | bytes 3145732
  5.0 15.7 %copy-start.1 = (bf16[256,4096]{1,0:T(8,128)(2,1)S(1)}, bf16[256,4096]{1,0:T(8,128)(2,1)}, u32[]{:S(2)}) copy-start(bf16[256,4096]{1,0:T(8,128)(2,1)} %x_ref.1) | copy-start | bytes 6291460
  5.0 15.7 %copy-start.4 = (bf16[256,512]{1,0:T(8,128)(2,1)S(1)}, bf16[256,512]{1,0:T(8,128)(2,1)}, u32[]{:S(2)}) copy-start(bf16[256,512]{1,0:T(8,128)(2,1)} %w_ref.1) | copy-start | bytes 786436
  5.0 15.7 %copy-start.5 = (bf16[256,512]{1,0:T(8,128)(2,1)S(1)}, bf16[256,512]{1,0:T(8,128)(2,1)}, u32[]{:S(2)}) copy-start(bf16[256,512]{1,0:T(8,128)(2,1)} %r_ref.3) | copy-start | bytes 786436
  5.0 15.7 %copy-start.6 = (f32[256,32]{0,1:T(8,128)S(1)}, f32[256,32]{0,1:T(8,128)}, u32[]{:S(2)}) copy-start(f32[256,32]{0,1:T(8,128)} %param.15) | copy-start | bytes 98308
  5.0 15.7 %copy-start.7 = (f32[32]{0:T(128)S(1)}, f32[32]{0:T(128)}, u32[]{:S(2)}) copy-start(f32[32]{0:T(128)} %param.16) | copy-start | bytes 388
  5.1 15.7 %copy-start.8 = (f32[32]{0:T(128)S(1)}, f32[32]{0:T(128)}, u32[]{:S(2)}) copy-start(f32[32]{0:T(128)} %param.17) | copy-start | bytes 388
  5.9 12.3 %collective-permute-start.3 = (bf16[256,768]{1,0:T(8,128)(2,1)S(1)}, bf16[256,768]{1,0:T(8,128)(2,1)S(1)}, u32[]{:S(2)}, u32[]{:S(2)}) collective-permute-start(bf16[256,768]{1,0:T(8,128)(2,1)S(1)} %get-tuple-element.75), channel_id=1, source_target_pairs={{0,4},{4,8},{8,12},{12,0},{1,5},{5,9},{9,13},{13,1},{2,6},{6,10},{... | collective-permute-start | bytes 1179656 | tf_op jit(solution)/shard_map/ppermute | solution.py:586
  7.4 26.7 %collective-permute-start = (f32[136,1024]{1,0:T(8,128)S(1)}, f32[136,1024]{1,0:T(8,128)S(1)}, u32[]{:S(2)}, u32[]{:S(2)}) collective-permute-start(f32[136,1024]{1,0:T(8,128)S(1)} %get-tuple-element.68), channel_id=1, source_target_pairs={{0,1},{1,2},{2,3},{3,0},{4,5},{5,6},{6,7},{7,4},{8,9},{9,10},{10,1... | collective-permute-start | bytes 1671176 | tf_op jit(solution)/shard_map/ppermute | solution.py:586
  9.0 28.4 %collective-permute-start.1 = (f32[136,1024]{1,0:T(8,128)S(1)}, f32[136,1024]{1,0:T(8,128)S(1)}, u32[]{:S(2)}, u32[]{:S(2)}) collective-permute-start(f32[136,1024]{1,0:T(8,128)S(1)} %get-tuple-element.69), channel_id=1, source_target_pairs={{0,2},{1,3},{2,0},{3,1},{4,6},{5,7},{6,4},{7,5},{8,10},{9,11},{10,... | collective-permute-start | bytes 1671176 | tf_op jit(solution)/shard_map/ppermute | solution.py:586
  11.9 25.5 %collective-permute-start.2 = (f32[136,1024]{1,0:T(8,128)S(1)}, f32[136,1024]{1,0:T(8,128)S(1)}, u32[]{:S(2)}, u32[]{:S(2)}) collective-permute-start(f32[136,1024]{1,0:T(8,128)S(1)} %get-tuple-element.70), channel_id=1, source_target_pairs={{0,3},{1,0},{2,1},{3,2},{4,7},{5,4},{6,5},{7,6},{8,11},{9,8},{10,9... | collective-permute-start | bytes 1671176 | tf_op jit(solution)/shard_map/ppermute | solution.py:586
  13.3 14.2 %collective-permute-start.4 = (bf16[256,768]{1,0:T(8,128)(2,1)S(1)}, bf16[256,768]{1,0:T(8,128)(2,1)S(1)}, u32[]{:S(2)}, u32[]{:S(2)}) collective-permute-start(bf16[256,768]{1,0:T(8,128)(2,1)S(1)} %get-tuple-element.76), channel_id=1, source_target_pairs={{0,8},{4,12},{8,0},{12,4},{1,9},{5,13},{9,1},{13,5},{2,10},{6,14},... | collective-permute-start | bytes 1179656 | tf_op jit(solution)/shard_map/ppermute | solution.py:586
  18.2 13.8 %collective-permute-start.5 = (bf16[256,768]{1,0:T(8,128)(2,1)S(1)}, bf16[256,768]{1,0:T(8,128)(2,1)S(1)}, u32[]{:S(2)}, u32[]{:S(2)}) collective-permute-start(bf16[256,768]{1,0:T(8,128)(2,1)S(1)} %get-tuple-element.77), channel_id=1, source_target_pairs={{0,12},{4,0},{8,4},{12,8},{1,13},{5,1},{9,5},{13,9},{2,14},{6,2},{... | collective-permute-start | bytes 1179656 | tf_op jit(solution)/shard_map/ppermute | solution.py:586
  32.1 15.6 %collective-permute-start.10 = (bf16[1024,256]{1,0:T(8,128)(2,1)S(1)}, bf16[1024,256]{1,0:T(8,128)(2,1)S(1)}, u32[]{:S(2)}, u32[]{:S(2)}) collective-permute-start(bf16[1024,256]{1,0:T(8,128)(2,1)S(1)} %stack.13.rest_4_), channel_id=1, source_target_pairs={{0,3},{1,0},{2,1},{3,2},{4,7},{5,4},{6,5},{7,6},{8,11},{9,8},{10,9... | collective-permute-start | bytes 1572872 | tf_op jit(solution)/shard_map/ppermute | solution.py:586
  32.4 15.3 %collective-permute-start.9 = (bf16[1024,256]{1,0:T(8,128)(2,1)S(1)}, bf16[1024,256]{1,0:T(8,128)(2,1)S(1)}, u32[]{:S(2)}, u32[]{:S(2)}) collective-permute-start(bf16[1024,256]{1,0:T(8,128)(2,1)S(1)} %stack.13.rest_4_), channel_id=1, source_target_pairs={{0,1},{1,2},{2,3},{3,0},{4,5},{5,6},{6,7},{7,4},{8,9},{9,10},{10,1... | collective-permute-start | bytes 1572872 | tf_op jit(solution)/shard_map/ppermute | solution.py:586
  38.3 7.8 %collective-permute-start.6 = (f32[136,256]{1,0:T(8,128)S(1)}, f32[136,256]{1,0:T(8,128)S(1)}, u32[]{:S(2)}, u32[]{:S(2)}) collective-permute-start(f32[136,256]{1,0:T(8,128)S(1)} %get-tuple-element.86), channel_id=1, source_target_pairs={{0,4},{4,8},{8,12},{12,0},{1,5},{5,9},{9,13},{13,1},{2,6},{6,10},{... | collective-permute-start | bytes 417800 | tf_op jit(solution)/shard_map/ppermute | solution.py:586
  38.4 7.7 %collective-permute-start.7 = (f32[136,256]{1,0:T(8,128)S(1)}, f32[136,256]{1,0:T(8,128)S(1)}, u32[]{:S(2)}, u32[]{:S(2)}) collective-permute-start(f32[136,256]{1,0:T(8,128)S(1)} %get-tuple-element.87), channel_id=1, source_target_pairs={{0,8},{4,12},{8,0},{12,4},{1,9},{5,13},{9,1},{13,5},{2,10},{6,14},... | collective-permute-start | bytes 417800 | tf_op jit(solution)/shard_map/ppermute | solution.py:586
  41.1 5.9 %collective-permute-start.8 = (f32[136,256]{1,0:T(8,128)S(1)}, f32[136,256]{1,0:T(8,128)S(1)}, u32[]{:S(2)}, u32[]{:S(2)}) collective-permute-start(f32[136,256]{1,0:T(8,128)S(1)} %get-tuple-element.88), channel_id=1, source_target_pairs={{0,12},{4,0},{8,4},{12,8},{1,13},{5,1},{9,5},{13,9},{2,14},{6,2},{... | collective-permute-start | bytes 417800 | tf_op jit(solution)/shard_map/ppermute | solution.py:586
  47.0 7.5 %copy-start.10 = (bf16[4096]{0:T(1024)(128)(2,1)S(1)}, bf16[4096]{0:T(1024)(128)(2,1)}, u32[]{:S(2)}) copy-start(bf16[4096]{0:T(1024)(128)(2,1)} %param.18) | copy-start | bytes 24580
  47.7 7.0 %collective-permute-start.11 = (f32[128,256]{1,0:T(8,128)S(1)}, f32[128,256]{1,0:T(8,128)S(1)}, u32[]{:S(2)}, u32[]{:S(2)}) collective-permute-start(f32[128,256]{1,0:T(8,128)S(1)} %get-tuple-element.98), channel_id=1, source_target_pairs={{0,12},{4,0},{8,4},{12,8},{1,13},{5,1},{9,5},{13,9},{2,14},{6,2},{... | collective-permute-start | bytes 393224 | tf_op jit(solution)/shard_map/ppermute | solution.py:586
  50.5 6.5 %collective-permute-start.12 = (f32[128,256]{1,0:T(8,128)S(1)}, f32[128,256]{1,0:T(8,128)S(1)}, u32[]{:S(2)}, u32[]{:S(2)}) collective-permute-start(f32[128,256]{1,0:T(8,128)S(1)} %get-tuple-element.99), channel_id=1, source_target_pairs={{0,8},{4,12},{8,0},{12,4},{1,9},{5,13},{9,1},{13,5},{2,10},{6,14},... | collective-permute-start | bytes 393224 | tf_op jit(solution)/shard_map/ppermute | solution.py:586
  51.8 6.6 %collective-permute-start.13 = (f32[128,256]{1,0:T(8,128)S(1)}, f32[128,256]{1,0:T(8,128)S(1)}, u32[]{:S(2)}, u32[]{:S(2)}) collective-permute-start(f32[128,256]{1,0:T(8,128)S(1)} %get-tuple-element.100), channel_id=1, source_target_pairs={{0,4},{4,8},{8,12},{12,0},{1,5},{5,9},{9,13},{13,1},{2,6},{6,10},{... | collective-permute-start | bytes 393224 | tf_op jit(solution)/shard_map/ppermute | solution.py:586
  51.8 12.8 %collective-permute-start.18 = (bf16[512,256]{1,0:T(8,128)(2,1)S(1)}, bf16[512,256]{1,0:T(8,128)(2,1)S(1)}, u32[]{:S(2)}, u32[]{:S(2)}) collective-permute-start(bf16[512,256]{1,0:T(8,128)(2,1)S(1)} %slice.7), channel_id=1, source_target_pairs={{0,3},{1,0},{2,1},{3,2},{4,7},{5,4},{6,5},{7,6},{8,11},{9,8},{10,9... | collective-permute-start | bytes 786440 | tf_op jit(solution)/shard_map/ppermute | solution.py:586
  54.4 10.2 %collective-permute-start.17 = (bf16[512,256]{1,0:T(8,128)(2,1)S(1)}, bf16[512,256]{1,0:T(8,128)(2,1)S(1)}, u32[]{:S(2)}, u32[]{:S(2)}) collective-permute-start(bf16[512,256]{1,0:T(8,128)(2,1)S(1)} %slice.6), channel_id=1, source_target_pairs={{0,1},{1,2},{2,3},{3,0},{4,5},{5,6},{6,7},{7,4},{8,9},{9,10},{10,1... | collective-permute-start | bytes 786440 | tf_op jit(solution)/shard_map/ppermute | solution.py:586
  60.0 24.6 %collective-permute-start.14 = (f32[128,1024]{1,0:T(8,128)S(1)}, f32[128,1024]{1,0:T(8,128)S(1)}, u32[]{:S(2)}, u32[]{:S(2)}) collective-permute-start(f32[128,1024]{1,0:T(8,128)S(1)} %get-tuple-element.106), channel_id=1, source_target_pairs={{0,3},{1,0},{2,1},{3,2},{4,7},{5,4},{6,5},{7,6},{8,11},{9,8},{10,9... | collective-permute-start | bytes 1572872 | tf_op jit(solution)/shard_map/ppermute | solution.py:586
  63.2 21.5 %collective-permute-start.15 = (f32[128,1024]{1,0:T(8,128)S(1)}, f32[128,1024]{1,0:T(8,128)S(1)}, u32[]{:S(2)}, u32[]{:S(2)}) collective-permute-start(f32[128,1024]{1,0:T(8,128)S(1)} %get-tuple-element.107), channel_id=1, source_target_pairs={{0,2},{1,3},{2,0},{3,1},{4,6},{5,7},{6,4},{7,5},{8,10},{9,11},{10,... | collective-permute-start | bytes 1572872 | tf_op jit(solution)/shard_map/ppermute | solution.py:586
  63.3 24.7 %collective-permute-start.16 = (f32[128,1024]{1,0:T(8,128)S(1)}, f32[128,1024]{1,0:T(8,128)S(1)}, u32[]{:S(2)}, u32[]{:S(2)}) collective-permute-start(f32[128,1024]{1,0:T(8,128)S(1)} %get-tuple-element.108), channel_id=1, source_target_pairs={{0,1},{1,2},{2,3},{3,0},{4,5},{5,6},{6,7},{7,4},{8,9},{9,10},{10,1... | collective-permute-start | bytes 1572872 | tf_op jit(solution)/shard_map/ppermute | solution.py:586
  64.7 23.4 %copy-start.9 = (bf16[256,4096]{1,0:T(8,128)(2,1)S(1)}, bf16[256,4096]{1,0:T(8,128)(2,1)}, u32[]{:S(2)}) copy-start(bf16[256,4096]{1,0:T(8,128)(2,1)} %gate_ref.1) | copy-start | bytes 6291460
  80.1 13.0 %collective-permute-start.19 = (bf16[256,512]{1,0:T(8,128)(2,1)S(1)}, bf16[256,512]{1,0:T(8,128)(2,1)S(1)}, u32[]{:S(2)}, u32[]{:S(2)}) collective-permute-start(bf16[256,512]{1,0:T(8,128)(2,1)S(1)} %get-tuple-element.116), channel_id=1, source_target_pairs={{0,12},{4,0},{8,4},{12,8},{1,13},{5,1},{9,5},{13,9},{2,14},{6,2},{... | collective-permute-start | bytes 786440 | tf_op jit(solution)/shard_map/ppermute | solution.py:586
  80.8 12.3 %collective-permute-start.20 = (bf16[256,512]{1,0:T(8,128)(2,1)S(1)}, bf16[256,512]{1,0:T(8,128)(2,1)S(1)}, u32[]{:S(2)}, u32[]{:S(2)}) collective-permute-start(bf16[256,512]{1,0:T(8,128)(2,1)S(1)} %get-tuple-element.117), channel_id=1, source_target_pairs={{0,8},{4,12},{8,0},{12,4},{1,9},{5,13},{9,1},{13,5},{2,10},{6,14},... | collective-permute-start | bytes 786440 | tf_op jit(solution)/shard_map/ppermute | solution.py:586
  84.6 9.9 %collective-permute-start.21 = (bf16[256,512]{1,0:T(8,128)(2,1)S(1)}, bf16[256,512]{1,0:T(8,128)(2,1)S(1)}, u32[]{:S(2)}, u32[]{:S(2)}) collective-permute-start(bf16[256,512]{1,0:T(8,128)(2,1)S(1)} %get-tuple-element.118), channel_id=1, source_target_pairs={{0,4},{4,8},{8,12},{12,0},{1,5},{5,9},{9,13},{13,1},{2,6},{6,10},{... | collective-permute-start | bytes 786440 | tf_op jit(solution)/shard_map/ppermute | solution.py:586

commit v5 on v4

--- a/solution.py
+++ b/solution.py
@@ -1,3 +1,4 @@
+import functools
 import math
 
 import jax
@@ -95,31 +96,33 @@
     return log_decay
 
 
-def state_body(at_ref, x_hbm, w_hbm, dt_hbm, rate_hbm, *rest):
-    outs, first_ref, (x_ref, w_ref, dt_ref, rate_ref, sems) = rest[:SIDE], rest[SIDE], rest[SIDE + 1 :]
+def state_body(slots, at_ref, x_hbm, w_hbm, dt_hbm, rate_hbm, *rest):
+    n = len(slots)
+    outs, first_ref, (x_ref, w_ref, dt_ref, rate_ref, sems) = rest[:n], rest[n], rest[n + 1 :]
     rows = dt_ref.shape[1]
     half = rows // 2
     width = PER * D
     y = at_ref[1]
-    steps = pltpu.make_async_copy(dt_hbm, dt_ref, sems.at[2 * SIDE])
+    steps = pltpu.make_async_copy(dt_hbm, dt_ref, sems.at[2 * n])
     steps.start()
-    rates = pltpu.make_async_copy(rate_hbm, rate_ref, sems.at[2 * SIDE + 1])
+    rates = pltpu.make_async_copy(rate_hbm, rate_ref, sems.at[2 * n + 1])
     rates.start()
     arrivals = []
-    for s in (1, 3, 2, 0):
+    for i, s in enumerate(slots):
         group = lax.rem(y + s, SIDE)
         arrivals.append(
             (
+                i,
                 s,
                 pltpu.make_async_copy(
-                    w_hbm.at[:, columns(group, D)], w_ref.at[s], sems.at[SIDE + s]
+                    w_hbm.at[:, columns(group, D)], w_ref.at[i], sems.at[n + i]
                 ),
                 pltpu.make_async_copy(
-                    x_hbm.at[:, columns(group, width)], x_ref.at[s], sems.at[s]
+                    x_hbm.at[:, columns(group, width)], x_ref.at[i], sems.at[i]
                 ),
             )
         )
-    for _, w_copy, x_copy in arrivals:
+    for _, _, w_copy, x_copy in arrivals:
         w_copy.start()
         x_copy.start()
     steps.wait()
@@ -133,7 +136,7 @@
     to_end = jnp.exp(ends - sums) * dt
     last = ends[half : half + 8]
     total = ends[:8] + last
-    for s, w_copy, x_copy in arrivals:
+    for i, s, w_copy, x_copy in arrivals:
         turn = SSD_HEADS - PER * lax.rem(y + s, SIDE)
         mine, last_mine, total_mine = [
             pltpu.roll(jnp.concatenate([part] * (D // SSD_HEADS), axis=1), turn, 1)
@@ -143,48 +146,49 @@
         x_copy.wait()
         scaled = jnp.concatenate(
             [
-                (mine[:, j : j + 1] * x_ref[s, :, j * D : (j + 1) * D].astype(F32)).astype(BF)
+                (mine[:, j : j + 1] * x_ref[i, :, j * D : (j + 1) * D].astype(F32)).astype(BF)
                 for j in range(PER)
             ],
             axis=1,
         )
         first, second = [
             lax.dot_general(
-                w_ref[s, c * half : (c + 1) * half, :],
+                w_ref[i, c * half : (c + 1) * half, :],
                 scaled[c * half : (c + 1) * half],
                 (((0,), (0,)), ((), ())),
                 preferred_element_type=F32,
             )
             for c in range(2)
         ]
-        first_ref[s] = first
+        first_ref[i] = first
         decay = jnp.concatenate(
             [jnp.broadcast_to(last_mine[0:1, j : j + 1], (1, D)) for j in range(PER)], axis=1
         )
-        outs[s][:D, :] = jnp.exp(decay) * first + second
-        outs[s][D:, :] = jnp.concatenate(
+        outs[i][:D, :] = jnp.exp(decay) * first + second
+        outs[i][D:, :] = jnp.concatenate(
             [jnp.broadcast_to(total_mine[:, j : j + 1], (EXTRA, D)) for j in range(PER)], axis=1
         )
 
 
-def local_states(at, x, w, dt, rate):
+def local_states(at, slots, x, w, dt, rate):
+    n = len(slots)
     rows = x.shape[0]
     width = PER * D
     far = pl.BlockSpec(memory_space=pltpu.HBM)
     near = pl.BlockSpec(memory_space=pltpu.VMEM)
     return pl.pallas_call(
-        state_body,
+        functools.partial(state_body, slots),
         in_specs=[pl.BlockSpec(memory_space=pltpu.SMEM), far, far, far, far],
-        out_specs=[near] * (SIDE + 1),
+        out_specs=[near] * (n + 1),
         scratch_shapes=[
-            pltpu.VMEM((SIDE, rows, width), BF),
-            pltpu.VMEM((SIDE, rows, D), BF),
+            pltpu.VMEM((n, rows, width), BF),
+            pltpu.VMEM((n, rows, D), BF),
             pltpu.VMEM((SSD_HEADS, rows), F32),
             pltpu.VMEM((1, SSD_HEADS), F32),
-            pltpu.SemaphoreType.DMA((2 * SIDE + 2,)),
+            pltpu.SemaphoreType.DMA((2 * n + 2,)),
         ],
-        out_shape=[jax.ShapeDtypeStruct((D + EXTRA, width), F32)] * SIDE
-        + [jax.ShapeDtypeStruct((SIDE, D, width), F32)],
+        out_shape=[jax.ShapeDtypeStruct((D + EXTRA, width), F32)] * n
+        + [jax.ShapeDtypeStruct((n, D, width), F32)],
         compiler_params=params(),
         name="local_states",
     )(at, *[pltpu.with_memory_space_constraint(part, pltpu.HBM) for part in (x, w, dt, rate)])
@@ -362,9 +366,10 @@
 
 
 def ssd_body(
-    at_ref, inside_ref, gate_ref, r_ref, dt_ref, rate_ref, gain_ref, first_ref, *rest
+    at_ref, inside_ref, gate_ref, r_ref, dt_ref, rate_ref, gain_ref, sides_ref, ends_ref, *rest
 ):
     starts, out_hbm, (gated, staged, sems) = rest[:SIDE], rest[SIDE], rest[SIDE + 1 :]
+    firsts = {1: sides_ref.at[0], 3: sides_ref.at[1], 2: ends_ref.at[0], 0: ends_ref.at[1]}
     y = at_ref[1]
     rows = dt_ref.shape[1]
     half = rows // 2
@@ -386,7 +391,7 @@
         start = starts[s][...]
         gated[:half, :] = jnp.dot(read[:half], start.astype(BF), preferred_element_type=F32)
         gated[half:, :] = jnp.dot(
-            read[half:], (decay * start + first_ref[s]).astype(BF), preferred_element_type=F32
+            read[half:], (decay * start + firsts[s][...]).astype(BF), preferred_element_type=F32
         )
         square = jnp.zeros((rows, D), F32)
         for j in range(PER):
@@ -420,7 +425,7 @@
     near = pl.BlockSpec(memory_space=pltpu.VMEM)
     return pl.pallas_call(
         ssd_body,
-        in_specs=[pl.BlockSpec(memory_space=pltpu.SMEM)] + [near] * (7 + SIDE),
+        in_specs=[pl.BlockSpec(memory_space=pltpu.SMEM)] + [near] * (8 + SIDE),
         out_specs=pl.BlockSpec(memory_space=pltpu.HBM),
         scratch_shapes=[
             pltpu.VMEM((rows, width), F32),
@@ -431,7 +436,7 @@
         compiler_params=params(24),
         cost_estimate=about(8),
         name="ssd_out",
-    )(at, inside, gate, r, dt, rate, gain, first, *starts)
+    )(at, inside, gate, r, dt, rate, gain, *first, *starts)
 
 
 def load_queries(q_ref, qs):
@@ -600,9 +605,12 @@
     skip = skip_gain.reshape(1, -1)
     gain = norm_gain.reshape(1, -1)
     tie = lax.optimization_barrier
-    *states, first = local_states(at, ssd_input, write_map, step_size, rate)
-    states, packed = tie((states, (key_rows, value_rows, query_rows)))
-    states = exchange(states, "y", 1)
+    given = (ssd_input, write_map, step_size, rate)
+    one, three, sides = local_states(at, (1, 3), *given)
+    one, three, given, packed = tie((one, three, given, (key_rows, value_rows, query_rows)))
+    two, mine, rest = local_states(at, (2, 0), *given)
+    first = [sides, rest]
+    states = exchange([mine, one, two, three], "y", 1)
     pieces = exchange(pack(at, *packed), "x", 1)
     inside = inside_spans(at, ssd_input, write_map, read_map, step_size, rate, skip)
     pieces, inside = tie((pieces, inside))

time: 96.4 us -> 95.7 us (level)
  waiting for transfers between devices: 27 us -> 24.2 us
  Pallas kernels: 35 us -> 36.6 us
    ppermute x22, waiting for transfers between devices: 27 us -> 24.2 us  [shifted(): lax.ppermute(value, axis, [(i, (i + by) % SIDE) for i in range(SIDE)])]
    pallas_call x1 -> x2, Pallas kernels: 4.21 us -> 5.9 us  [local_states(): pl.pallas_call(functools.partial(state_body, slots), in_specs=[pl.BlockSp...]
  transfers between devices with their start and end apart: 22 -> 22, of which waited for: 12 -> 9; matrix products, arithmetic and copies ran while one was open for 0% -> 0% of each run, Pallas kernels for 30% -> 33%
where the time goes in v5:
time: 95.7 us; the launch traced here: 94.9 us
  Pallas kernels  36.6 us (38%)
  starting transfers between devices  32.7 us (34%)
  waiting for transfers between devices  24.2 us (25%)
  between operations  1.08 us (1%)
    ppermute x22, starting transfers between devices, shifted(): lax.ppermute(value, axis, [(i, (i + by) % SIDE) for i in range(SIDE)])  32.7 us
    ppermute x22, waiting for transfers between devices, shifted(): lax.ppermute(value, axis, [(i, (i + by) % SIDE) for i in range(SIDE)])  24.2 us
    pallas_call x1, Pallas kernels, attention(): pl.pallas_call(attention_body, grid_spec=pltpu.PrefetchScalarGridSpec(num...  15.4 us
    pallas_call x2, Pallas kernels, local_states(): pl.pallas_call(functools.partial(state_body, slots), in_specs=[pl.BlockSp...  5.9 us
    pallas_call x1, Pallas kernels, ssd_out_of(): pl.pallas_call(ssd_body, in_specs=[pl.BlockSpec(memory_space=pltpu.SMEM)]...  5.04 us
    pallas_call x1, Pallas kernels, inside_spans(): pl.pallas_call(inside_body, grid_spec=pltpu.PrefetchScalarGridSpec(num_sc...  4.64 us
  transfers between devices with their start and end apart: 22, of which 9 were waited for; matrix products, arithmetic and copies ran while one was open for 0% of the time, Pallas kernels for 33%

profile of v5, /device:TPU:64, one launch (start us, length us, event | category | flops | bytes accessed | tf_op | source)
XLA Modules:
  0.0 94.9 jit_solution(14513414247601443729)
XLA Ops:
  0.6 0.0 copy-start.3
  0.6 0.0 copy-start.2
  0.7 0.1 pad_add_fusion.at_ref
  0.7 3.0 %local_states.2 = (f32[136,1024]{1,0:T(8,128)S(1)}, f32[136,1024]{1,0:T(8,128)S(1)}, f32[2,128,1024]{2,1,0:T(8,128)S(1)}) custom-call(s32[2]{0:T(128)S(1)} %pad_add_fusion.at_ref, bf16[256,4096]{1,0:T(8,128)(2,1)} %x_ref.1, bf16[256,512]{1,0:T(8,128)(2,1)} %w_ref.1, f32[32,256]{1,0:T(8,128)} %bitcast.5, f32[1,32]{1,0:T(1,128)} %bitcast.9), custom_call_target="tpu_custom_call" | custom-call | tf_op jit(solution)/shard_map/local_states/pallas_call | solution.py:179
  3.7 0.0 copy-start.6
  3.7 0.8 pack.1
  4.6 0.0 copy-start
  4.6 0.0 copy-start.4
  4.6 0.0 copy-start.5
  4.6 0.0 copy-start.7
  4.6 0.0 copy-start.8
  4.6 1.6 %collective-permute-start.3 = (bf16[256,768]{1,0:T(8,128)(2,1)S(1)}, bf16[256,768]{1,0:T(8,128)(2,1)S(1)}, u32[]{:S(2)}, u32[]{:S(2)}) collective-permute-start(bf16[256,768]{1,0:T(8,128)(2,1)S(1)} %get-tuple-element.80), channel_id=1, source_target_pairs={{0,4},{4,8},{8,12},{12,0},{1,5},{5,9},{9,13},{13,1},{2,6},{6,10},{... | collective-permute-start | bytes 1179656 | tf_op jit(solution)/shard_map/ppermute | solution.py:591
  6.2 1.6 %collective-permute-start = (f32[136,1024]{1,0:T(8,128)S(1)}, f32[136,1024]{1,0:T(8,128)S(1)}, u32[]{:S(2)}, u32[]{:S(2)}) collective-permute-start(f32[136,1024]{1,0:T(8,128)S(1)} %get-tuple-element.73), channel_id=1, source_target_pairs={{0,1},{1,2},{2,3},{3,0},{4,5},{5,6},{6,7},{7,4},{8,9},{9,10},{10,1... | collective-permute-start | bytes 1671176 | tf_op jit(solution)/shard_map/ppermute | solution.py:591
  7.8 1.7 %collective-permute-start.2 = (f32[136,1024]{1,0:T(8,128)S(1)}, f32[136,1024]{1,0:T(8,128)S(1)}, u32[]{:S(2)}, u32[]{:S(2)}) collective-permute-start(f32[136,1024]{1,0:T(8,128)S(1)} %get-tuple-element.75), channel_id=1, source_target_pairs={{0,3},{1,0},{2,1},{3,2},{4,7},{5,4},{6,5},{7,6},{8,11},{9,8},{10,9... | collective-permute-start | bytes 1671176 | tf_op jit(solution)/shard_map/ppermute | solution.py:591
  9.4 3.0 %local_states.3 = (f32[136,1024]{1,0:T(8,128)S(1)}, f32[136,1024]{1,0:T(8,128)S(1)}, f32[2,128,1024]{2,1,0:T(8,128)S(1)}) custom-call(s32[2]{0:T(128)S(1)} %pad_add_fusion.at_ref, bf16[256,4096]{1,0:T(8,128)(2,1)} %x_ref.1, bf16[256,512]{1,0:T(8,128)(2,1)} %w_ref.1, f32[32,256]{1,0:T(8,128)} %bitcast.6, f32[1,32]{1,0:T(1,128)} %bitcast.10), custom_call_target="tpu_custom_call" | custom-call | tf_op jit(solution)/shard_map/local_states/pallas_call | solution.py:179
  12.4 2.1 %collective-permute-start.1 = (f32[136,1024]{1,0:T(8,128)S(1)}, f32[136,1024]{1,0:T(8,128)S(1)}, u32[]{:S(2)}, u32[]{:S(2)}) collective-permute-start(f32[136,1024]{1,0:T(8,128)S(1)} %get-tuple-element.74), channel_id=1, source_target_pairs={{0,2},{1,3},{2,0},{3,1},{4,6},{5,7},{6,4},{7,5},{8,10},{9,11},{10,... | collective-permute-start | bytes 1671176 | tf_op jit(solution)/shard_map/ppermute | solution.py:591
  14.5 2.7 %collective-permute-start.4 = (bf16[256,768]{1,0:T(8,128)(2,1)S(1)}, bf16[256,768]{1,0:T(8,128)(2,1)S(1)}, u32[]{:S(2)}, u32[]{:S(2)}) collective-permute-start(bf16[256,768]{1,0:T(8,128)(2,1)S(1)} %get-tuple-element.81), channel_id=1, source_target_pairs={{0,8},{4,12},{8,0},{12,4},{1,9},{5,13},{9,1},{13,5},{2,10},{6,14},... | collective-permute-start | bytes 1179656 | tf_op jit(solution)/shard_map/ppermute | solution.py:591
  17.2 0.0 collective-permute-done.3.refs_1_.rest_1_
  17.2 1.5 %collective-permute-start.5 = (bf16[256,768]{1,0:T(8,128)(2,1)S(1)}, bf16[256,768]{1,0:T(8,128)(2,1)S(1)}, u32[]{:S(2)}, u32[]{:S(2)}) collective-permute-start(bf16[256,768]{1,0:T(8,128)(2,1)S(1)} %get-tuple-element.82), channel_id=1, source_target_pairs={{0,12},{4,0},{8,4},{12,8},{1,13},{5,1},{9,5},{13,9},{2,14},{6,2},{... | collective-permute-start | bytes 1179656 | tf_op jit(solution)/shard_map/ppermute | solution.py:591
  18.8 4.6 %inside_spans.1.inside_ref = f32[256,4096]{1,0:T(8,128)S(1)} custom-call(s32[2]{0:T(128)S(1)} %pad_add_fusion.at_ref, bf16[256,4096]{1,0:T(8,128)(2,1)S(1)} %copy-done, bf16[256,512]{1,0:T(8,128)(2,1)S(1)} %copy-done.4, bf16[256,512]{1,0:T(8,128)(2,1)S(1)} %copy-done.6, f32[32,256]{1,0:T(8,128)S(1)} %bitcast.7, f32[1,32]{1,0:T(1,128)S(1)} %bitcast.11, ...), custom_call_target="tpu_custom_call" | custom-call | tf_op jit(solution)/shard_map/inside_spans/pallas_call | solution.py:343
  23.4 2.8 %collective-permute-done.4.refs_2_.rest_2_ = bf16[256,768]{1,0:T(8,128)(2,1)S(1)} collective-permute-done((bf16[256,768]{1,0:T(8,128)(2,1)S(1)}, bf16[256,768]{1,0:T(8,128)(2,1)S(1)}, u32[]{:S(2)}, u32[]{:S(2)}) %collective-permute-start.4) | collective-permute-done | bytes 393248 | tf_op jit(solution)/shard_map/ppermute | solution.py:591
  26.2 7.1 %collective-permute-done.5.refs_3_.rest_3_ = bf16[256,768]{1,0:T(8,128)(2,1)S(1)} collective-permute-done((bf16[256,768]{1,0:T(8,128)(2,1)S(1)}, bf16[256,768]{1,0:T(8,128)(2,1)S(1)}, u32[]{:S(2)}, u32[]{:S(2)}) %collective-permute-start.5) | collective-permute-done | bytes 393248 | tf_op jit(solution)/shard_map/ppermute | solution.py:591
  33.3 1.1 %collective-permute-start.10 = (bf16[1024,256]{1,0:T(8,128)(2,1)S(1)}, bf16[1024,256]{1,0:T(8,128)(2,1)S(1)}, u32[]{:S(2)}, u32[]{:S(2)}) collective-permute-start(bf16[1024,256]{1,0:T(8,128)(2,1)S(1)} %stack.13.rest_4_), channel_id=1, source_target_pairs={{0,3},{1,0},{2,1},{3,2},{4,7},{5,4},{6,5},{7,6},{8,11},{9,8},{10,9... | collective-permute-start | bytes 1572872 | tf_op jit(solution)/shard_map/ppermute | solution.py:591
  34.4 1.0 %collective-permute-start.9 = (bf16[1024,256]{1,0:T(8,128)(2,1)S(1)}, bf16[1024,256]{1,0:T(8,128)(2,1)S(1)}, u32[]{:S(2)}, u32[]{:S(2)}) collective-permute-start(bf16[1024,256]{1,0:T(8,128)(2,1)S(1)} %stack.13.rest_4_), channel_id=1, source_target_pairs={{0,1},{1,2},{2,3},{3,0},{4,5},{5,6},{6,7},{7,4},{8,9},{9,10},{10,1... | collective-permute-start | bytes 1572872 | tf_op jit(solution)/shard_map/ppermute | solution.py:591
  35.4 0.0 collective-permute-done.refs_1_
  35.4 0.0 collective-permute-done.2.refs_3_
  35.4 0.0 collective-permute-done.1.refs_2_
  35.4 0.9 row_total.1
  36.3 2.3 %collective-permute-start.6 = (f32[136,256]{1,0:T(8,128)S(1)}, f32[136,256]{1,0:T(8,128)S(1)}, u32[]{:S(2)}, u32[]{:S(2)}) collective-permute-start(f32[136,256]{1,0:T(8,128)S(1)} %get-tuple-element.92), channel_id=1, source_target_pairs={{0,4},{4,8},{8,12},{12,0},{1,5},{5,9},{9,13},{13,1},{2,6},{6,10},{... | collective-permute-start | bytes 417800 | tf_op jit(solution)/shard_map/ppermute | solution.py:591
  38.6 1.9 %collective-permute-start.7 = (f32[136,256]{1,0:T(8,128)S(1)}, f32[136,256]{1,0:T(8,128)S(1)}, u32[]{:S(2)}, u32[]{:S(2)}) collective-permute-start(f32[136,256]{1,0:T(8,128)S(1)} %get-tuple-element.93), channel_id=1, source_target_pairs={{0,8},{4,12},{8,0},{12,4},{1,9},{5,13},{9,1},{13,5},{2,10},{6,14},... | collective-permute-start | bytes 417800 | tf_op jit(solution)/shard_map/ppermute | solution.py:591
  40.5 1.6 %collective-permute-start.8 = (f32[136,256]{1,0:T(8,128)S(1)}, f32[136,256]{1,0:T(8,128)S(1)}, u32[]{:S(2)}, u32[]{:S(2)}) collective-permute-start(f32[136,256]{1,0:T(8,128)S(1)} %get-tuple-element.94), channel_id=1, source_target_pairs={{0,12},{4,0},{8,4},{12,8},{1,13},{5,1},{9,5},{13,9},{2,14},{6,2},{... | collective-permute-start | bytes 417800 | tf_op jit(solution)/shard_map/ppermute | solution.py:591
  42.0 1.3 %collective-permute-done.6.refs_1_ = f32[136,256]{1,0:T(8,128)S(1)} collective-permute-done((f32[136,256]{1,0:T(8,128)S(1)}, f32[136,256]{1,0:T(8,128)S(1)}, u32[]{:S(2)}, u32[]{:S(2)}) %collective-permute-start.6) | collective-permute-done | bytes 139296 | tf_op jit(solution)/shard_map/ppermute | solution.py:591
  43.4 3.1 %collective-permute-done.7.refs_2_ = f32[136,256]{1,0:T(8,128)S(1)} collective-permute-done((f32[136,256]{1,0:T(8,128)S(1)}, f32[136,256]{1,0:T(8,128)S(1)}, u32[]{:S(2)}, u32[]{:S(2)}) %collective-permute-start.7) | collective-permute-done | bytes 139296 | tf_op jit(solution)/shard_map/ppermute | solution.py:591
  46.5 0.0 collective-permute-done.8.refs_3_
  46.5 0.7 entering_rows.1
  47.2 0.0 collective-permute-done.10.rest_7_
  47.2 0.4 collective-permute-done.9.rest_5_
  47.6 3.7 %collective-permute-start.11 = (f32[128,256]{1,0:T(8,128)S(1)}, f32[128,256]{1,0:T(8,128)S(1)}, u32[]{:S(2)}, u32[]{:S(2)}) collective-permute-start(f32[128,256]{1,0:T(8,128)S(1)} %get-tuple-element.104), channel_id=1, source_target_pairs={{0,12},{4,0},{8,4},{12,8},{1,13},{5,1},{9,5},{13,9},{2,14},{6,2},{... | collective-permute-start | bytes 393224 | tf_op jit(solution)/shard_map/ppermute | solution.py:591
  51.3 2.3 %collective-permute-start.12 = (f32[128,256]{1,0:T(8,128)S(1)}, f32[128,256]{1,0:T(8,128)S(1)}, u32[]{:S(2)}, u32[]{:S(2)}) collective-permute-start(f32[128,256]{1,0:T(8,128)S(1)} %get-tuple-element.105), channel_id=1, source_target_pairs={{0,8},{4,12},{8,0},{12,4},{1,9},{5,13},{9,1},{13,5},{2,10},{6,14},... | collective-permute-start | bytes 393224 | tf_op jit(solution)/shard_map/ppermute | solution.py:591
  53.6 0.0 collective-permute-start.13
  53.7 0.4 collective-permute-start.18
  54.0 1.7 %collective-permute-start.17 = (bf16[512,256]{1,0:T(8,128)(2,1)S(1)}, bf16[512,256]{1,0:T(8,128)(2,1)S(1)}, u32[]{:S(2)}, u32[]{:S(2)}) collective-permute-start(bf16[512,256]{1,0:T(8,128)(2,1)S(1)} %slice.6), channel_id=1, source_target_pairs={{0,1},{1,2},{2,3},{3,0},{4,5},{5,6},{6,7},{7,4},{8,9},{9,10},{10,1... | collective-permute-start | bytes 786440 | tf_op jit(solution)/shard_map/ppermute | solution.py:591
  55.8 0.0 collective-permute-done.11.refs_5_
  55.8 2.1 %collective-permute-done.12.refs_6_ = f32[128,256]{1,0:T(8,128)S(1)} collective-permute-done((f32[128,256]{1,0:T(8,128)S(1)}, f32[128,256]{1,0:T(8,128)S(1)}, u32[]{:S(2)}, u32[]{:S(2)}) %collective-permute-start.12) | collective-permute-done | bytes 131104 | tf_op jit(solution)/shard_map/ppermute | solution.py:591
  57.9 2.1 %collective-permute-done.13.refs_7_ = f32[128,256]{1,0:T(8,128)S(1)} collective-permute-done((f32[128,256]{1,0:T(8,128)S(1)}, f32[128,256]{1,0:T(8,128)S(1)}, u32[]{:S(2)}, u32[]{:S(2)}) %collective-permute-start.13) | collective-permute-done | bytes 131104 | tf_op jit(solution)/shard_map/ppermute | solution.py:591
  59.9 1.7 %start_states.1 = (f32[128,1024]{1,0:T(8,128)S(1)}, f32[128,1024]{1,0:T(8,128)S(1)}, f32[128,1024]{1,0:T(8,128)S(1)}, f32[128,1024]{1,0:T(8,128)S(1)}) custom-call(s32[2]{0:T(128)S(1)} %pad_add_fusion.at_ref, f32[136,1024]{1,0:T(8,128)S(1)} %get-tuple-element.87.refs_0_, f32[136,1024]{1,0:T(8,128)S(1)} %collective-permute-done.refs_1_, ...), custom_call_target="tpu_custom_call" | custom-call | flops 2000000000 | bytes 6000000 | tf_op jit(solution)/shard_map/start_states/pallas_call | solution.py:284
  61.6 0.9 collective-permute-start.14
  62.5 1.2 %collective-permute-start.15 = (f32[128,1024]{1,0:T(8,128)S(1)}, f32[128,1024]{1,0:T(8,128)S(1)}, u32[]{:S(2)}, u32[]{:S(2)}) collective-permute-start(f32[128,1024]{1,0:T(8,128)S(1)} %get-tuple-element.113), channel_id=1, source_target_pairs={{0,2},{1,3},{2,0},{3,1},{4,6},{5,7},{6,4},{7,5},{8,10},{9,11},{10,... | collective-permute-start | bytes 1572872 | tf_op jit(solution)/shard_map/ppermute | solution.py:591
  63.7 0.1 collective-permute-start.16
  63.8 0.0 collective-permute-done.18
  63.8 0.0 collective-permute-done.17
  63.8 0.0 copy-start.9
  63.8 15.4 %attention.1 = (bf16[256,512]{1,0:T(8,128)(2,1)S(1)}, bf16[256,512]{1,0:T(8,128)(2,1)S(1)}, bf16[256,512]{1,0:T(8,128)(2,1)S(1)}, bf16[256,512]{1,0:T(8,128)(2,1)S(1)}) custom-call(s32[2]{0:T(128)S(1)} %pad_add_fusion.at_ref, bf16[256,768]{1,0:T(8,128)(2,1)S(1)} %get-tuple-element.115.refs_0_.rest_0_, ...), custom_call_target="tpu_custom_call" | custom-call | flops 17999998976 | bytes 54000000 | tf_op jit(solution)/shard_map/attention/pallas_call | solution.py:540
  79.3 1.4 %collective-permute-start.19 = (bf16[256,512]{1,0:T(8,128)(2,1)S(1)}, bf16[256,512]{1,0:T(8,128)(2,1)S(1)}, u32[]{:S(2)}, u32[]{:S(2)}) collective-permute-start(bf16[256,512]{1,0:T(8,128)(2,1)S(1)} %get-tuple-element.122), channel_id=1, source_target_pairs={{0,12},{4,0},{8,4},{12,8},{1,13},{5,1},{9,5},{13,9},{2,14},{6,2},{... | collective-permute-start | bytes 786440 | tf_op jit(solution)/shard_map/ppermute | solution.py:591
  80.7 1.5 %collective-permute-start.20 = (bf16[256,512]{1,0:T(8,128)(2,1)S(1)}, bf16[256,512]{1,0:T(8,128)(2,1)S(1)}, u32[]{:S(2)}, u32[]{:S(2)}) collective-permute-start(bf16[256,512]{1,0:T(8,128)(2,1)S(1)} %get-tuple-element.123), channel_id=1, source_target_pairs={{0,8},{4,12},{8,0},{12,4},{1,9},{5,13},{9,1},{13,5},{2,10},{6,14},... | collective-permute-start | bytes 786440 | tf_op jit(solution)/shard_map/ppermute | solution.py:591
  82.1 0.0 collective-permute-done.14.rest_1_
  82.1 0.6 collective-permute-start.21
  82.7 0.0 collective-permute-done.15.rest_2_
  82.7 4.4 %collective-permute-done.16.rest_3_ = f32[128,1024]{1,0:T(8,128)S(1)} collective-permute-done((f32[128,1024]{1,0:T(8,128)S(1)}, f32[128,1024]{1,0:T(8,128)S(1)}, u32[]{:S(2)}, u32[]{:S(2)}) %collective-permute-start.16) | collective-permute-done | bytes 524320 | tf_op jit(solution)/shard_map/ppermute | solution.py:591
  87.1 5.0 %ssd_out.1 = bf16[256,4096]{1,0:T(8,128)(2,1)} custom-call(s32[2]{0:T(128)S(1)} %pad_add_fusion.at_ref, f32[256,4096]{1,0:T(8,128)S(1)} %inside_spans.1.inside_ref, bf16[256,4096]{1,0:T(8,128)(2,1)S(1)} %copy-done.9, bf16[256,512]{1,0:T(8,128)(2,1)S(1)} %copy-done.6, f32[32,256]{1,0:T(8,128)S(1)} %bitcast.8, f32[1,32]{1,0:T(1,128)S(1)} %bitcast.12, ...), custom_call_target="tpu_custom_call" | custom-call | flops 8000000000 | bytes 24000000 | tf_op jit(solution)/shard_map/ssd_out/pallas_call | solution.py:426
  92.2 0.0 collective-permute-done.19.refs_1_
  92.2 0.0 collective-permute-done.20.refs_2_
  92.2 1.0 %collective-permute-done.21.refs_3_ = bf16[256,512]{1,0:T(8,128)(2,1)S(1)} collective-permute-done((bf16[256,512]{1,0:T(8,128)(2,1)S(1)}, bf16[256,512]{1,0:T(8,128)(2,1)S(1)}, u32[]{:S(2)}, u32[]{:S(2)}) %collective-permute-start.21) | collective-permute-done | bytes 262176 | tf_op jit(solution)/shard_map/ppermute | solution.py:591
  93.2 1.5 %unpack.1 = bf16[256,2048]{1,0:T(8,128)(2,1)} custom-call(s32[2]{0:T(128)S(1)} %pad_add_fusion.at_ref, bf16[256,512]{1,0:T(8,128)(2,1)S(1)} %get-tuple-element.126.refs_0_, bf16[256,512]{1,0:T(8,128)(2,1)S(1)} %collective-permute-done.19.refs_1_, bf16[256,512]{1,0:T(8,128)(2,1)S(1)} %collective-permute-done.20.refs_2_, ...), custom_call_target="tpu_custom_call" | custom-call | flops 2000000000 | bytes 6000000 | tf_op jit(solution)/shard_map/unpack/pallas_call | solution.py:577
  (18 shorter events, 0.1 us)
Async XLA Ops:
  0.6 3.1 %copy-start.3 = (bf16[256,512]{1,0:T(8,128)(2,1)S(1)}, bf16[256,512]{1,0:T(8,128)(2,1)}, u32[]{:S(2)}) copy-start(bf16[256,512]{1,0:T(8,128)(2,1)} %refs_10_) | copy-start | bytes 786436
  0.6 3.1 %copy-start.2 = (bf16[256,512]{1,0:T(8,128)(2,1)S(1)}, bf16[256,512]{1,0:T(8,128)(2,1)}, u32[]{:S(2)}) copy-start(bf16[256,512]{1,0:T(8,128)(2,1)} %refs_9_) | copy-start | bytes 786436
  0.7 3.1 %copy-start.1 = (bf16[256,2048]{1,0:T(8,128)(2,1)S(1)}, bf16[256,2048]{1,0:T(8,128)(2,1)}, u32[]{:S(2)}) copy-start(bf16[256,2048]{1,0:T(8,128)(2,1)} %refs_11_) | copy-start | bytes 3145732
  3.7 15.0 %copy-start.6 = (bf16[256,512]{1,0:T(8,128)(2,1)S(1)}, bf16[256,512]{1,0:T(8,128)(2,1)}, u32[]{:S(2)}) copy-start(bf16[256,512]{1,0:T(8,128)(2,1)} %r_ref.3) | copy-start | bytes 786436
  4.6 14.2 %copy-start = (bf16[256,4096]{1,0:T(8,128)(2,1)S(1)}, bf16[256,4096]{1,0:T(8,128)(2,1)}, u32[]{:S(2)}) copy-start(bf16[256,4096]{1,0:T(8,128)(2,1)} %x_ref.1) | copy-start | bytes 6291460
  4.6 14.2 %copy-start.4 = (bf16[256,512]{1,0:T(8,128)(2,1)S(1)}, bf16[256,512]{1,0:T(8,128)(2,1)}, u32[]{:S(2)}) copy-start(bf16[256,512]{1,0:T(8,128)(2,1)} %w_ref.1) | copy-start | bytes 786436
  4.6 14.1 %copy-start.5 = (f32[256,32]{0,1:T(8,128)S(1)}, f32[256,32]{0,1:T(8,128)}, u32[]{:S(2)}) copy-start(f32[256,32]{0,1:T(8,128)} %param.15) | copy-start | bytes 98308
  4.6 14.1 %copy-start.7 = (f32[32]{0:T(128)S(1)}, f32[32]{0:T(128)}, u32[]{:S(2)}) copy-start(f32[32]{0:T(128)} %param.16) | copy-start | bytes 388
  4.6 14.1 %copy-start.8 = (f32[32]{0:T(128)S(1)}, f32[32]{0:T(128)}, u32[]{:S(2)}) copy-start(f32[32]{0:T(128)} %param.17) | copy-start | bytes 388
  4.6 12.6 %collective-permute-start.3 = (bf16[256,768]{1,0:T(8,128)(2,1)S(1)}, bf16[256,768]{1,0:T(8,128)(2,1)S(1)}, u32[]{:S(2)}, u32[]{:S(2)}) collective-permute-start(bf16[256,768]{1,0:T(8,128)(2,1)S(1)} %get-tuple-element.80), channel_id=1, source_target_pairs={{0,4},{4,8},{8,12},{12,0},{1,5},{5,9},{9,13},{13,1},{2,6},{6,10},{... | collective-permute-start | bytes 1179656 | tf_op jit(solution)/shard_map/ppermute | solution.py:591
  6.2 29.2 %collective-permute-start = (f32[136,1024]{1,0:T(8,128)S(1)}, f32[136,1024]{1,0:T(8,128)S(1)}, u32[]{:S(2)}, u32[]{:S(2)}) collective-permute-start(f32[136,1024]{1,0:T(8,128)S(1)} %get-tuple-element.73), channel_id=1, source_target_pairs={{0,1},{1,2},{2,3},{3,0},{4,5},{5,6},{6,7},{7,4},{8,9},{9,10},{10,1... | collective-permute-start | bytes 1671176 | tf_op jit(solution)/shard_map/ppermute | solution.py:591
  7.8 27.6 %collective-permute-start.2 = (f32[136,1024]{1,0:T(8,128)S(1)}, f32[136,1024]{1,0:T(8,128)S(1)}, u32[]{:S(2)}, u32[]{:S(2)}) collective-permute-start(f32[136,1024]{1,0:T(8,128)S(1)} %get-tuple-element.75), channel_id=1, source_target_pairs={{0,3},{1,0},{2,1},{3,2},{4,7},{5,4},{6,5},{7,6},{8,11},{9,8},{10,9... | collective-permute-start | bytes 1671176 | tf_op jit(solution)/shard_map/ppermute | solution.py:591
  12.4 23.0 %collective-permute-start.1 = (f32[136,1024]{1,0:T(8,128)S(1)}, f32[136,1024]{1,0:T(8,128)S(1)}, u32[]{:S(2)}, u32[]{:S(2)}) collective-permute-start(f32[136,1024]{1,0:T(8,128)S(1)} %get-tuple-element.74), channel_id=1, source_target_pairs={{0,2},{1,3},{2,0},{3,1},{4,6},{5,7},{6,4},{7,5},{8,10},{9,11},{10,... | collective-permute-start | bytes 1671176 | tf_op jit(solution)/shard_map/ppermute | solution.py:591
  14.5 11.7 %collective-permute-start.4 = (bf16[256,768]{1,0:T(8,128)(2,1)S(1)}, bf16[256,768]{1,0:T(8,128)(2,1)S(1)}, u32[]{:S(2)}, u32[]{:S(2)}) collective-permute-start(bf16[256,768]{1,0:T(8,128)(2,1)S(1)} %get-tuple-element.81), channel_id=1, source_target_pairs={{0,8},{4,12},{8,0},{12,4},{1,9},{5,13},{9,1},{13,5},{2,10},{6,14},... | collective-permute-start | bytes 1179656 | tf_op jit(solution)/shard_map/ppermute | solution.py:591
  17.2 16.1 %collective-permute-start.5 = (bf16[256,768]{1,0:T(8,128)(2,1)S(1)}, bf16[256,768]{1,0:T(8,128)(2,1)S(1)}, u32[]{:S(2)}, u32[]{:S(2)}) collective-permute-start(bf16[256,768]{1,0:T(8,128)(2,1)S(1)} %get-tuple-element.82), channel_id=1, source_target_pairs={{0,12},{4,0},{8,4},{12,8},{1,13},{5,1},{9,5},{13,9},{2,14},{6,2},{... | collective-permute-start | bytes 1179656 | tf_op jit(solution)/shard_map/ppermute | solution.py:591
  33.3 13.9 %collective-permute-start.10 = (bf16[1024,256]{1,0:T(8,128)(2,1)S(1)}, bf16[1024,256]{1,0:T(8,128)(2,1)S(1)}, u32[]{:S(2)}, u32[]{:S(2)}) collective-permute-start(bf16[1024,256]{1,0:T(8,128)(2,1)S(1)} %stack.13.rest_4_), channel_id=1, source_target_pairs={{0,3},{1,0},{2,1},{3,2},{4,7},{5,4},{6,5},{7,6},{8,11},{9,8},{10,9... | collective-permute-start | bytes 1572872 | tf_op jit(solution)/shard_map/ppermute | solution.py:591
  34.4 13.2 %collective-permute-start.9 = (bf16[1024,256]{1,0:T(8,128)(2,1)S(1)}, bf16[1024,256]{1,0:T(8,128)(2,1)S(1)}, u32[]{:S(2)}, u32[]{:S(2)}) collective-permute-start(bf16[1024,256]{1,0:T(8,128)(2,1)S(1)} %stack.13.rest_4_), channel_id=1, source_target_pairs={{0,1},{1,2},{2,3},{3,0},{4,5},{5,6},{6,7},{7,4},{8,9},{9,10},{10,1... | collective-permute-start | bytes 1572872 | tf_op jit(solution)/shard_map/ppermute | solution.py:591
  36.3 7.1 %collective-permute-start.6 = (f32[136,256]{1,0:T(8,128)S(1)}, f32[136,256]{1,0:T(8,128)S(1)}, u32[]{:S(2)}, u32[]{:S(2)}) collective-permute-start(f32[136,256]{1,0:T(8,128)S(1)} %get-tuple-element.92), channel_id=1, source_target_pairs={{0,4},{4,8},{8,12},{12,0},{1,5},{5,9},{9,13},{13,1},{2,6},{6,10},{... | collective-permute-start | bytes 417800 | tf_op jit(solution)/shard_map/ppermute | solution.py:591
  38.6 7.9 %collective-permute-start.7 = (f32[136,256]{1,0:T(8,128)S(1)}, f32[136,256]{1,0:T(8,128)S(1)}, u32[]{:S(2)}, u32[]{:S(2)}) collective-permute-start(f32[136,256]{1,0:T(8,128)S(1)} %get-tuple-element.93), channel_id=1, source_target_pairs={{0,8},{4,12},{8,0},{12,4},{1,9},{5,13},{9,1},{13,5},{2,10},{6,14},... | collective-permute-start | bytes 417800 | tf_op jit(solution)/shard_map/ppermute | solution.py:591
  40.5 6.0 %collective-permute-start.8 = (f32[136,256]{1,0:T(8,128)S(1)}, f32[136,256]{1,0:T(8,128)S(1)}, u32[]{:S(2)}, u32[]{:S(2)}) collective-permute-start(f32[136,256]{1,0:T(8,128)S(1)} %get-tuple-element.94), channel_id=1, source_target_pairs={{0,12},{4,0},{8,4},{12,8},{1,13},{5,1},{9,5},{13,9},{2,14},{6,2},{... | collective-permute-start | bytes 417800 | tf_op jit(solution)/shard_map/ppermute | solution.py:591
  46.5 9.3 %copy-start.10 = (bf16[4096]{0:T(1024)(128)(2,1)S(1)}, bf16[4096]{0:T(1024)(128)(2,1)}, u32[]{:S(2)}) copy-start(bf16[4096]{0:T(1024)(128)(2,1)} %param.18) | copy-start | bytes 24580
  47.6 8.2 %collective-permute-start.11 = (f32[128,256]{1,0:T(8,128)S(1)}, f32[128,256]{1,0:T(8,128)S(1)}, u32[]{:S(2)}, u32[]{:S(2)}) collective-permute-start(f32[128,256]{1,0:T(8,128)S(1)} %get-tuple-element.104), channel_id=1, source_target_pairs={{0,12},{4,0},{8,4},{12,8},{1,13},{5,1},{9,5},{13,9},{2,14},{6,2},{... | collective-permute-start | bytes 393224 | tf_op jit(solution)/shard_map/ppermute | solution.py:591
  51.3 6.6 %collective-permute-start.12 = (f32[128,256]{1,0:T(8,128)S(1)}, f32[128,256]{1,0:T(8,128)S(1)}, u32[]{:S(2)}, u32[]{:S(2)}) collective-permute-start(f32[128,256]{1,0:T(8,128)S(1)} %get-tuple-element.105), channel_id=1, source_target_pairs={{0,8},{4,12},{8,0},{12,4},{1,9},{5,13},{9,1},{13,5},{2,10},{6,14},... | collective-permute-start | bytes 393224 | tf_op jit(solution)/shard_map/ppermute | solution.py:591
  53.6 6.3 %collective-permute-start.13 = (f32[128,256]{1,0:T(8,128)S(1)}, f32[128,256]{1,0:T(8,128)S(1)}, u32[]{:S(2)}, u32[]{:S(2)}) collective-permute-start(f32[128,256]{1,0:T(8,128)S(1)} %get-tuple-element.106), channel_id=1, source_target_pairs={{0,4},{4,8},{8,12},{12,0},{1,5},{5,9},{9,13},{13,1},{2,6},{6,10},{... | collective-permute-start | bytes 393224 | tf_op jit(solution)/shard_map/ppermute | solution.py:591
  53.7 10.1 %collective-permute-start.18 = (bf16[512,256]{1,0:T(8,128)(2,1)S(1)}, bf16[512,256]{1,0:T(8,128)(2,1)S(1)}, u32[]{:S(2)}, u32[]{:S(2)}) collective-permute-start(bf16[512,256]{1,0:T(8,128)(2,1)S(1)} %slice.7), channel_id=1, source_target_pairs={{0,3},{1,0},{2,1},{3,2},{4,7},{5,4},{6,5},{7,6},{8,11},{9,8},{10,9... | collective-permute-start | bytes 786440 | tf_op jit(solution)/shard_map/ppermute | solution.py:591
  54.0 9.7 %collective-permute-start.17 = (bf16[512,256]{1,0:T(8,128)(2,1)S(1)}, bf16[512,256]{1,0:T(8,128)(2,1)S(1)}, u32[]{:S(2)}, u32[]{:S(2)}) collective-permute-start(bf16[512,256]{1,0:T(8,128)(2,1)S(1)} %slice.6), channel_id=1, source_target_pairs={{0,1},{1,2},{2,3},{3,0},{4,5},{5,6},{6,7},{7,4},{8,9},{9,10},{10,1... | collective-permute-start | bytes 786440 | tf_op jit(solution)/shard_map/ppermute | solution.py:591
  61.6 20.5 %collective-permute-start.14 = (f32[128,1024]{1,0:T(8,128)S(1)}, f32[128,1024]{1,0:T(8,128)S(1)}, u32[]{:S(2)}, u32[]{:S(2)}) collective-permute-start(f32[128,1024]{1,0:T(8,128)S(1)} %get-tuple-element.112), channel_id=1, source_target_pairs={{0,3},{1,0},{2,1},{3,2},{4,7},{5,4},{6,5},{7,6},{8,11},{9,8},{10,9... | collective-permute-start | bytes 1572872 | tf_op jit(solution)/shard_map/ppermute | solution.py:591
  62.5 20.2 %collective-permute-start.15 = (f32[128,1024]{1,0:T(8,128)S(1)}, f32[128,1024]{1,0:T(8,128)S(1)}, u32[]{:S(2)}, u32[]{:S(2)}) collective-permute-start(f32[128,1024]{1,0:T(8,128)S(1)} %get-tuple-element.113), channel_id=1, source_target_pairs={{0,2},{1,3},{2,0},{3,1},{4,6},{5,7},{6,4},{7,5},{8,10},{9,11},{10,... | collective-permute-start | bytes 1572872 | tf_op jit(solution)/shard_map/ppermute | solution.py:591
  63.7 23.4 %collective-permute-start.16 = (f32[128,1024]{1,0:T(8,128)S(1)}, f32[128,1024]{1,0:T(8,128)S(1)}, u32[]{:S(2)}, u32[]{:S(2)}) collective-permute-start(f32[128,1024]{1,0:T(8,128)S(1)} %get-tuple-element.114), channel_id=1, source_target_pairs={{0,1},{1,2},{2,3},{3,0},{4,5},{5,6},{6,7},{7,4},{8,9},{9,10},{10,1... | collective-permute-start | bytes 1572872 | tf_op jit(solution)/shard_map/ppermute | solution.py:591
  63.8 23.3 %copy-start.9 = (bf16[256,4096]{1,0:T(8,128)(2,1)S(1)}, bf16[256,4096]{1,0:T(8,128)(2,1)}, u32[]{:S(2)}) copy-start(bf16[256,4096]{1,0:T(8,128)(2,1)} %gate_ref.1) | copy-start | bytes 6291460
  79.3 12.9 %collective-permute-start.19 = (bf16[256,512]{1,0:T(8,128)(2,1)S(1)}, bf16[256,512]{1,0:T(8,128)(2,1)S(1)}, u32[]{:S(2)}, u32[]{:S(2)}) collective-permute-start(bf16[256,512]{1,0:T(8,128)(2,1)S(1)} %get-tuple-element.122), channel_id=1, source_target_pairs={{0,12},{4,0},{8,4},{12,8},{1,13},{5,1},{9,5},{13,9},{2,14},{6,2},{... | collective-permute-start | bytes 786440 | tf_op jit(solution)/shard_map/ppermute | solution.py:591
  80.7 11.5 %collective-permute-start.20 = (bf16[256,512]{1,0:T(8,128)(2,1)S(1)}, bf16[256,512]{1,0:T(8,128)(2,1)S(1)}, u32[]{:S(2)}, u32[]{:S(2)}) collective-permute-start(bf16[256,512]{1,0:T(8,128)(2,1)S(1)} %get-tuple-element.123), channel_id=1, source_target_pairs={{0,8},{4,12},{8,0},{12,4},{1,9},{5,13},{9,1},{13,5},{2,10},{6,14},... | collective-permute-start | bytes 786440 | tf_op jit(solution)/shard_map/ppermute | solution.py:591
  82.1 11.0 %collective-permute-start.21 = (bf16[256,512]{1,0:T(8,128)(2,1)S(1)}, bf16[256,512]{1,0:T(8,128)(2,1)S(1)}, u32[]{:S(2)}, u32[]{:S(2)}) collective-permute-start(bf16[256,512]{1,0:T(8,128)(2,1)S(1)} %get-tuple-element.124), channel_id=1, source_target_pairs={{0,4},{4,8},{8,12},{12,0},{1,5},{5,9},{9,13},{13,1},{2,6},{6,10},{... | collective-permute-start | bytes 786440 | tf_op jit(solution)/shard_map/ppermute | solution.py:591

commit v6 on v5

--- a/solution.py
+++ b/solution.py
@@ -610,8 +610,10 @@
     one, three, given, packed = tie((one, three, given, (key_rows, value_rows, query_rows)))
     two, mine, rest = local_states(at, (2, 0), *given)
     first = [sides, rest]
+    pieces = list(pack(at, *packed))
+    two, pieces[1], pieces[3] = tie((two, pieces[1], pieces[3]))
     states = exchange([mine, one, two, three], "y", 1)
-    pieces = exchange(pack(at, *packed), "x", 1)
+    pieces = exchange(pieces, "x", 1)
     inside = inside_spans(at, ssd_input, write_map, read_map, step_size, rate, skip)
     pieces, inside = tie((pieces, inside))
     own = stack(pieces)

time: 95.7 us -> 99.5 us (1.040)
  starting transfers between devices: 32.7 us -> 38.6 us
  waiting for transfers between devices: 24.2 us -> 22.6 us
    ppermute x22, starting transfers between devices: 32.7 us -> 38.6 us  [shifted(): lax.ppermute(value, axis, [(i, (i + by) % SIDE) for i in range(SIDE)])]
    ppermute x22, waiting for transfers between devices: 24.2 us -> 22.6 us  [shifted(): lax.ppermute(value, axis, [(i, (i + by) % SIDE) for i in range(SIDE)])]
  transfers between devices with their start and end apart: 22 -> 22, of which waited for: 9 -> 10; matrix products, arithmetic and copies ran while one was open for 0% -> 0% of each run, Pallas kernels for 33% -> 32%
where the time goes in v6:
time: 99.5 us; the launch traced here: 99.2 us
  starting transfers between devices  38.6 us (39%)
  Pallas kernels  36.7 us (37%)
  waiting for transfers between devices  22.6 us (23%)
  between operations  1.11 us (1%)
    ppermute x22, starting transfers between devices, shifted(): lax.ppermute(value, axis, [(i, (i + by) % SIDE) for i in range(SIDE)])  38.6 us
    ppermute x22, waiting for transfers between devices, shifted(): lax.ppermute(value, axis, [(i, (i + by) % SIDE) for i in range(SIDE)])  22.6 us
    pallas_call x1, Pallas kernels, attention(): pl.pallas_call(attention_body, grid_spec=pltpu.PrefetchScalarGridSpec(num...  15.4 us
    pallas_call x2, Pallas kernels, local_states(): pl.pallas_call(functools.partial(state_body, slots), in_specs=[pl.BlockSp...  5.91 us
    pallas_call x1, Pallas kernels, ssd_out_of(): pl.pallas_call(ssd_body, in_specs=[pl.BlockSpec(memory_space=pltpu.SMEM)]...  5.05 us
    pallas_call x1, Pallas kernels, inside_spans(): pl.pallas_call(inside_body, grid_spec=pltpu.PrefetchScalarGridSpec(num_sc...  4.65 us
  transfers between devices with their start and end apart: 22, of which 10 were waited for; matrix products, arithmetic and copies ran while one was open for 0% of the time, Pallas kernels for 32%

profile of v6, /device:TPU:64, one launch (start us, length us, event | category | flops | bytes accessed | tf_op | source)
XLA Modules:
  0.0 99.2 jit_solution(9544769585244275140)
XLA Ops:
  0.7 0.1 pad_add_fusion.at_ref
  0.7 3.0 %local_states.2 = (f32[136,1024]{1,0:T(8,128)S(1)}, f32[136,1024]{1,0:T(8,128)S(1)}, f32[2,128,1024]{2,1,0:T(8,128)S(1)}) custom-call(s32[2]{0:T(128)S(1)} %pad_add_fusion.at_ref, bf16[256,4096]{1,0:T(8,128)(2,1)} %x_ref.1, bf16[256,512]{1,0:T(8,128)(2,1)} %w_ref.1, f32[32,256]{1,0:T(8,128)} %bitcast.5, f32[1,32]{1,0:T(1,128)} %bitcast.9), custom_call_target="tpu_custom_call" | custom-call | tf_op jit(solution)/shard_map/local_states/pallas_call | solution.py:179
  3.7 0.0 copy-start.6
  3.7 0.8 pack.1
  4.6 0.0 copy-start
  4.6 0.0 copy-start.4
  4.6 0.0 copy-start.5
  4.6 0.0 copy-start.7
  4.6 0.0 copy-start.8
  4.6 3.1 %collective-permute-start.4 = (bf16[256,768]{1,0:T(8,128)(2,1)S(1)}, bf16[256,768]{1,0:T(8,128)(2,1)S(1)}, u32[]{:S(2)}, u32[]{:S(2)}) collective-permute-start(bf16[256,768]{1,0:T(8,128)(2,1)S(1)} %get-tuple-element.87), channel_id=1, source_target_pairs={{0,8},{4,12},{8,0},{12,4},{1,9},{5,13},{9,1},{13,5},{2,10},{6,14},... | collective-permute-start | bytes 1179656 | tf_op jit(solution)/shard_map/ppermute | solution.py:591
  7.7 1.6 %collective-permute-start = (f32[136,1024]{1,0:T(8,128)S(1)}, f32[136,1024]{1,0:T(8,128)S(1)}, u32[]{:S(2)}, u32[]{:S(2)}) collective-permute-start(f32[136,1024]{1,0:T(8,128)S(1)} %get-tuple-element.76), channel_id=1, source_target_pairs={{0,1},{1,2},{2,3},{3,0},{4,5},{5,6},{6,7},{7,4},{8,9},{9,10},{10,1... | collective-permute-start | bytes 1671176 | tf_op jit(solution)/shard_map/ppermute | solution.py:591
  9.3 1.7 %collective-permute-start.2 = (f32[136,1024]{1,0:T(8,128)S(1)}, f32[136,1024]{1,0:T(8,128)S(1)}, u32[]{:S(2)}, u32[]{:S(2)}) collective-permute-start(f32[136,1024]{1,0:T(8,128)S(1)} %get-tuple-element.84), channel_id=1, source_target_pairs={{0,3},{1,0},{2,1},{3,2},{4,7},{5,4},{6,5},{7,6},{8,11},{9,8},{10,9... | collective-permute-start | bytes 1671176 | tf_op jit(solution)/shard_map/ppermute | solution.py:591
  11.0 3.0 %local_states.3 = (f32[136,1024]{1,0:T(8,128)S(1)}, f32[136,1024]{1,0:T(8,128)S(1)}, f32[2,128,1024]{2,1,0:T(8,128)S(1)}) custom-call(s32[2]{0:T(128)S(1)} %pad_add_fusion.at_ref, bf16[256,4096]{1,0:T(8,128)(2,1)} %x_ref.1, bf16[256,512]{1,0:T(8,128)(2,1)} %w_ref.1, f32[32,256]{1,0:T(8,128)} %bitcast.6, f32[1,32]{1,0:T(1,128)} %bitcast.10), custom_call_target="tpu_custom_call" | custom-call | tf_op jit(solution)/shard_map/local_states/pallas_call | solution.py:179
  13.9 2.1 %collective-permute-start.1 = (f32[136,1024]{1,0:T(8,128)S(1)}, f32[136,1024]{1,0:T(8,128)S(1)}, u32[]{:S(2)}, u32[]{:S(2)}) collective-permute-start(f32[136,1024]{1,0:T(8,128)S(1)} %get-tuple-element.83), channel_id=1, source_target_pairs={{0,2},{1,3},{2,0},{3,1},{4,6},{5,7},{6,4},{7,5},{8,10},{9,11},{10,... | collective-permute-start | bytes 1671176 | tf_op jit(solution)/shard_map/ppermute | solution.py:591
  16.0 0.6 collective-permute-start.3
  16.6 0.5 collective-permute-done.4.refs_2_.rest_2_
  17.1 2.8 %collective-permute-start.5 = (bf16[256,768]{1,0:T(8,128)(2,1)S(1)}, bf16[256,768]{1,0:T(8,128)(2,1)S(1)}, u32[]{:S(2)}, u32[]{:S(2)}) collective-permute-start(bf16[256,768]{1,0:T(8,128)(2,1)S(1)} %get-tuple-element.88), channel_id=1, source_target_pairs={{0,12},{4,0},{8,4},{12,8},{1,13},{5,1},{9,5},{13,9},{2,14},{6,2},{... | collective-permute-start | bytes 1179656 | tf_op jit(solution)/shard_map/ppermute | solution.py:591
  19.8 0.0 copy-done.6
  19.8 0.0 copy-done.4
  19.9 4.6 %inside_spans.1.inside_ref = f32[256,4096]{1,0:T(8,128)S(1)} custom-call(s32[2]{0:T(128)S(1)} %pad_add_fusion.at_ref, bf16[256,4096]{1,0:T(8,128)(2,1)S(1)} %copy-done, bf16[256,512]{1,0:T(8,128)(2,1)S(1)} %copy-done.4, bf16[256,512]{1,0:T(8,128)(2,1)S(1)} %copy-done.6, f32[32,256]{1,0:T(8,128)S(1)} %bitcast.7, f32[1,32]{1,0:T(1,128)S(1)} %bitcast.11, ...), custom_call_target="tpu_custom_call" | custom-call | tf_op jit(solution)/shard_map/inside_spans/pallas_call | solution.py:343
  24.5 2.4 %collective-permute-done.3.refs_1_.rest_1_ = bf16[256,768]{1,0:T(8,128)(2,1)S(1)} collective-permute-done((bf16[256,768]{1,0:T(8,128)(2,1)S(1)}, bf16[256,768]{1,0:T(8,128)(2,1)S(1)}, u32[]{:S(2)}, u32[]{:S(2)}) %collective-permute-start.3) | collective-permute-done | bytes 393248 | tf_op jit(solution)/shard_map/ppermute | solution.py:591
  26.9 0.4 collective-permute-done.5.refs_3_.rest_3_
  27.4 3.1 %collective-permute-start.10 = (bf16[1024,256]{1,0:T(8,128)(2,1)S(1)}, bf16[1024,256]{1,0:T(8,128)(2,1)S(1)}, u32[]{:S(2)}, u32[]{:S(2)}) collective-permute-start(bf16[1024,256]{1,0:T(8,128)(2,1)S(1)} %stack.13.rest_4_), channel_id=1, source_target_pairs={{0,3},{1,0},{2,1},{3,2},{4,7},{5,4},{6,5},{7,6},{8,11},{9,8},{10,9... | collective-permute-start | bytes 1572872 | tf_op jit(solution)/shard_map/ppermute | solution.py:591
  30.5 0.0 collective-permute-start.9
  30.5 0.0 collective-permute-done.refs_1_
  30.5 0.0 collective-permute-done.2.refs_3_
  30.5 7.2 %collective-permute-done.1.refs_2_ = f32[136,1024]{1,0:T(8,128)S(1)} collective-permute-done((f32[136,1024]{1,0:T(8,128)S(1)}, f32[136,1024]{1,0:T(8,128)S(1)}, u32[]{:S(2)}, u32[]{:S(2)}) %collective-permute-start.1) | collective-permute-done | bytes 557088 | tf_op jit(solution)/shard_map/ppermute | solution.py:591
  37.7 0.9 row_total.1
  38.6 0.7 collective-permute-start.6
  39.3 2.0 %collective-permute-start.7 = (f32[136,256]{1,0:T(8,128)S(1)}, f32[136,256]{1,0:T(8,128)S(1)}, u32[]{:S(2)}, u32[]{:S(2)}) collective-permute-start(f32[136,256]{1,0:T(8,128)S(1)} %get-tuple-element.99), channel_id=1, source_target_pairs={{0,8},{4,12},{8,0},{12,4},{1,9},{5,13},{9,1},{13,5},{2,10},{6,14},... | collective-permute-start | bytes 417800 | tf_op jit(solution)/shard_map/ppermute | solution.py:591
  41.2 1.0 collective-permute-start.8
  42.2 4.2 %collective-permute-done.6.refs_1_ = f32[136,256]{1,0:T(8,128)S(1)} collective-permute-done((f32[136,256]{1,0:T(8,128)S(1)}, f32[136,256]{1,0:T(8,128)S(1)}, u32[]{:S(2)}, u32[]{:S(2)}) %collective-permute-start.6) | collective-permute-done | bytes 139296 | tf_op jit(solution)/shard_map/ppermute | solution.py:591
  46.4 0.0 collective-permute-done.7.refs_2_
  46.4 0.9 collective-permute-done.8.refs_3_
  47.3 0.7 entering_rows.1
  48.0 0.0 collective-permute-done.10.rest_7_
  48.0 0.0 collective-permute-done.9.rest_5_
  48.0 2.8 %collective-permute-start.11 = (f32[128,256]{1,0:T(8,128)S(1)}, f32[128,256]{1,0:T(8,128)S(1)}, u32[]{:S(2)}, u32[]{:S(2)}) collective-permute-start(f32[128,256]{1,0:T(8,128)S(1)} %get-tuple-element.110), channel_id=1, source_target_pairs={{0,12},{4,0},{8,4},{12,8},{1,13},{5,1},{9,5},{13,9},{2,14},{6,2},{... | collective-permute-start | bytes 393224 | tf_op jit(solution)/shard_map/ppermute | solution.py:591
  50.8 0.0 collective-permute-start.12
  50.8 1.0 collective-permute-start.13
  51.8 1.9 %collective-permute-start.18 = (bf16[512,256]{1,0:T(8,128)(2,1)S(1)}, bf16[512,256]{1,0:T(8,128)(2,1)S(1)}, u32[]{:S(2)}, u32[]{:S(2)}) collective-permute-start(bf16[512,256]{1,0:T(8,128)(2,1)S(1)} %slice.7), channel_id=1, source_target_pairs={{0,3},{1,0},{2,1},{3,2},{4,7},{5,4},{6,5},{7,6},{8,11},{9,8},{10,9... | collective-permute-start | bytes 786440 | tf_op jit(solution)/shard_map/ppermute | solution.py:591
  53.7 0.2 collective-permute-start.17
  53.9 1.2 %collective-permute-done.11.refs_5_ = f32[128,256]{1,0:T(8,128)S(1)} collective-permute-done((f32[128,256]{1,0:T(8,128)S(1)}, f32[128,256]{1,0:T(8,128)S(1)}, u32[]{:S(2)}, u32[]{:S(2)}) %collective-permute-start.11) | collective-permute-done | bytes 131104 | tf_op jit(solution)/shard_map/ppermute | solution.py:591
  55.1 2.3 %collective-permute-done.12.refs_6_ = f32[128,256]{1,0:T(8,128)S(1)} collective-permute-done((f32[128,256]{1,0:T(8,128)S(1)}, f32[128,256]{1,0:T(8,128)S(1)}, u32[]{:S(2)}, u32[]{:S(2)}) %collective-permute-start.12) | collective-permute-done | bytes 131104 | tf_op jit(solution)/shard_map/ppermute | solution.py:591
  57.3 1.0 %collective-permute-done.13.refs_7_ = f32[128,256]{1,0:T(8,128)S(1)} collective-permute-done((f32[128,256]{1,0:T(8,128)S(1)}, f32[128,256]{1,0:T(8,128)S(1)}, u32[]{:S(2)}, u32[]{:S(2)}) %collective-permute-start.13) | collective-permute-done | bytes 131104 | tf_op jit(solution)/shard_map/ppermute | solution.py:591
  58.4 1.7 %start_states.1 = (f32[128,1024]{1,0:T(8,128)S(1)}, f32[128,1024]{1,0:T(8,128)S(1)}, f32[128,1024]{1,0:T(8,128)S(1)}, f32[128,1024]{1,0:T(8,128)S(1)}) custom-call(s32[2]{0:T(128)S(1)} %pad_add_fusion.at_ref, f32[136,1024]{1,0:T(8,128)S(1)} %get-tuple-element.93.refs_0_, f32[136,1024]{1,0:T(8,128)S(1)} %collective-permute-done.refs_1_, ...), custom_call_target="tpu_custom_call" | custom-call | flops 2000000000 | bytes 6000000 | tf_op jit(solution)/shard_map/start_states/pallas_call | solution.py:284
  60.0 1.9 %collective-permute-start.14 = (f32[128,1024]{1,0:T(8,128)S(1)}, f32[128,1024]{1,0:T(8,128)S(1)}, u32[]{:S(2)}, u32[]{:S(2)}) collective-permute-start(f32[128,1024]{1,0:T(8,128)S(1)} %get-tuple-element.118), channel_id=1, source_target_pairs={{0,3},{1,0},{2,1},{3,2},{4,7},{5,4},{6,5},{7,6},{8,11},{9,8},{10,9... | collective-permute-start | bytes 1572872 | tf_op jit(solution)/shard_map/ppermute | solution.py:591
  61.9 1.7 %collective-permute-start.15 = (f32[128,1024]{1,0:T(8,128)S(1)}, f32[128,1024]{1,0:T(8,128)S(1)}, u32[]{:S(2)}, u32[]{:S(2)}) collective-permute-start(f32[128,1024]{1,0:T(8,128)S(1)} %get-tuple-element.119), channel_id=1, source_target_pairs={{0,2},{1,3},{2,0},{3,1},{4,6},{5,7},{6,4},{7,5},{8,10},{9,11},{10,... | collective-permute-start | bytes 1572872 | tf_op jit(solution)/shard_map/ppermute | solution.py:591
  63.6 0.0 collective-permute-start.16
  63.6 0.0 collective-permute-done.18
  63.6 0.0 collective-permute-done.17
  63.7 0.0 copy-start.9
  63.7 15.4 %attention.1 = (bf16[256,512]{1,0:T(8,128)(2,1)S(1)}, bf16[256,512]{1,0:T(8,128)(2,1)S(1)}, bf16[256,512]{1,0:T(8,128)(2,1)S(1)}, bf16[256,512]{1,0:T(8,128)(2,1)S(1)}) custom-call(s32[2]{0:T(128)S(1)} %pad_add_fusion.at_ref, bf16[256,768]{1,0:T(8,128)(2,1)S(1)} %get-tuple-element.121.refs_0_.rest_0_, ...), custom_call_target="tpu_custom_call" | custom-call | flops 17999998976 | bytes 54000000 | tf_op jit(solution)/shard_map/attention/pallas_call | solution.py:540
  79.1 1.2 %collective-permute-start.19 = (bf16[256,512]{1,0:T(8,128)(2,1)S(1)}, bf16[256,512]{1,0:T(8,128)(2,1)S(1)}, u32[]{:S(2)}, u32[]{:S(2)}) collective-permute-start(bf16[256,512]{1,0:T(8,128)(2,1)S(1)} %get-tuple-element.128), channel_id=1, source_target_pairs={{0,12},{4,0},{8,4},{12,8},{1,13},{5,1},{9,5},{13,9},{2,14},{6,2},{... | collective-permute-start | bytes 786440 | tf_op jit(solution)/shard_map/ppermute | solution.py:591
  80.3 9.6 %collective-permute-start.20 = (bf16[256,512]{1,0:T(8,128)(2,1)S(1)}, bf16[256,512]{1,0:T(8,128)(2,1)S(1)}, u32[]{:S(2)}, u32[]{:S(2)}) collective-permute-start(bf16[256,512]{1,0:T(8,128)(2,1)S(1)} %get-tuple-element.129), channel_id=1, source_target_pairs={{0,8},{4,12},{8,0},{12,4},{1,9},{5,13},{9,1},{13,5},{2,10},{6,14},... | collective-permute-start | bytes 786440 | tf_op jit(solution)/shard_map/ppermute | solution.py:591
  89.9 0.0 collective-permute-done.14.rest_1_
  89.9 0.0 collective-permute-start.21
  89.9 0.0 collective-permute-done.15.rest_2_
  89.9 0.0 collective-permute-done.16.rest_3_
  89.9 5.0 %ssd_out.1 = bf16[256,4096]{1,0:T(8,128)(2,1)} custom-call(s32[2]{0:T(128)S(1)} %pad_add_fusion.at_ref, f32[256,4096]{1,0:T(8,128)S(1)} %inside_spans.1.inside_ref, bf16[256,4096]{1,0:T(8,128)(2,1)S(1)} %copy-done.9, bf16[256,512]{1,0:T(8,128)(2,1)S(1)} %copy-done.6, f32[32,256]{1,0:T(8,128)S(1)} %bitcast.8, f32[1,32]{1,0:T(1,128)S(1)} %bitcast.12, ...), custom_call_target="tpu_custom_call" | custom-call | flops 8000000000 | bytes 24000000 | tf_op jit(solution)/shard_map/ssd_out/pallas_call | solution.py:426
  95.0 0.0 collective-permute-done.19.refs_1_
  95.0 0.0 collective-permute-done.20.refs_2_
  95.0 2.5 %collective-permute-done.21.refs_3_ = bf16[256,512]{1,0:T(8,128)(2,1)S(1)} collective-permute-done((bf16[256,512]{1,0:T(8,128)(2,1)S(1)}, bf16[256,512]{1,0:T(8,128)(2,1)S(1)}, u32[]{:S(2)}, u32[]{:S(2)}) %collective-permute-start.21) | collective-permute-done | bytes 262176 | tf_op jit(solution)/shard_map/ppermute | solution.py:591
  97.5 1.5 %unpack.1 = bf16[256,2048]{1,0:T(8,128)(2,1)} custom-call(s32[2]{0:T(128)S(1)} %pad_add_fusion.at_ref, bf16[256,512]{1,0:T(8,128)(2,1)S(1)} %get-tuple-element.132.refs_0_, bf16[256,512]{1,0:T(8,128)(2,1)S(1)} %collective-permute-done.19.refs_1_, bf16[256,512]{1,0:T(8,128)(2,1)S(1)} %collective-permute-done.20.refs_2_, ...), custom_call_target="tpu_custom_call" | custom-call | flops 2000000000 | bytes 6000000 | tf_op jit(solution)/shard_map/unpack/pallas_call | solution.py:577
  (18 shorter events, 0.1 us)
Async XLA Ops:
  0.6 3.1 %copy-start.3 = (bf16[256,512]{1,0:T(8,128)(2,1)S(1)}, bf16[256,512]{1,0:T(8,128)(2,1)}, u32[]{:S(2)}) copy-start(bf16[256,512]{1,0:T(8,128)(2,1)} %refs_10_) | copy-start | bytes 786436
  0.6 3.1 %copy-start.2 = (bf16[256,512]{1,0:T(8,128)(2,1)S(1)}, bf16[256,512]{1,0:T(8,128)(2,1)}, u32[]{:S(2)}) copy-start(bf16[256,512]{1,0:T(8,128)(2,1)} %refs_9_) | copy-start | bytes 786436
  0.7 3.1 %copy-start.1 = (bf16[256,2048]{1,0:T(8,128)(2,1)S(1)}, bf16[256,2048]{1,0:T(8,128)(2,1)}, u32[]{:S(2)}) copy-start(bf16[256,2048]{1,0:T(8,128)(2,1)} %refs_11_) | copy-start | bytes 3145732
  3.7 16.1 %copy-start.6 = (bf16[256,512]{1,0:T(8,128)(2,1)S(1)}, bf16[256,512]{1,0:T(8,128)(2,1)}, u32[]{:S(2)}) copy-start(bf16[256,512]{1,0:T(8,128)(2,1)} %r_ref.3) | copy-start | bytes 786436
  4.6 15.3 %copy-start = (bf16[256,4096]{1,0:T(8,128)(2,1)S(1)}, bf16[256,4096]{1,0:T(8,128)(2,1)}, u32[]{:S(2)}) copy-start(bf16[256,4096]{1,0:T(8,128)(2,1)} %x_ref.1) | copy-start | bytes 6291460
  4.6 15.3 %copy-start.4 = (bf16[256,512]{1,0:T(8,128)(2,1)S(1)}, bf16[256,512]{1,0:T(8,128)(2,1)}, u32[]{:S(2)}) copy-start(bf16[256,512]{1,0:T(8,128)(2,1)} %w_ref.1) | copy-start | bytes 786436
  4.6 15.3 %copy-start.5 = (f32[256,32]{0,1:T(8,128)S(1)}, f32[256,32]{0,1:T(8,128)}, u32[]{:S(2)}) copy-start(f32[256,32]{0,1:T(8,128)} %param.15) | copy-start | bytes 98308
  4.6 15.2 %copy-start.7 = (f32[32]{0:T(128)S(1)}, f32[32]{0:T(128)}, u32[]{:S(2)}) copy-start(f32[32]{0:T(128)} %param.16) | copy-start | bytes 388
  4.6 15.2 %copy-start.8 = (f32[32]{0:T(128)S(1)}, f32[32]{0:T(128)}, u32[]{:S(2)}) copy-start(f32[32]{0:T(128)} %param.17) | copy-start | bytes 388
  4.6 12.4 %collective-permute-start.4 = (bf16[256,768]{1,0:T(8,128)(2,1)S(1)}, bf16[256,768]{1,0:T(8,128)(2,1)S(1)}, u32[]{:S(2)}, u32[]{:S(2)}) collective-permute-start(bf16[256,768]{1,0:T(8,128)(2,1)S(1)} %get-tuple-element.87), channel_id=1, source_target_pairs={{0,8},{4,12},{8,0},{12,4},{1,9},{5,13},{9,1},{13,5},{2,10},{6,14},... | collective-permute-start | bytes 1179656 | tf_op jit(solution)/shard_map/ppermute | solution.py:591
  7.7 22.7 %collective-permute-start = (f32[136,1024]{1,0:T(8,128)S(1)}, f32[136,1024]{1,0:T(8,128)S(1)}, u32[]{:S(2)}, u32[]{:S(2)}) collective-permute-start(f32[136,1024]{1,0:T(8,128)S(1)} %get-tuple-element.76), channel_id=1, source_target_pairs={{0,1},{1,2},{2,3},{3,0},{4,5},{5,6},{6,7},{7,4},{8,9},{9,10},{10,1... | collective-permute-start | bytes 1671176 | tf_op jit(solution)/shard_map/ppermute | solution.py:591
  9.3 21.2 %collective-permute-start.2 = (f32[136,1024]{1,0:T(8,128)S(1)}, f32[136,1024]{1,0:T(8,128)S(1)}, u32[]{:S(2)}, u32[]{:S(2)}) collective-permute-start(f32[136,1024]{1,0:T(8,128)S(1)} %get-tuple-element.84), channel_id=1, source_target_pairs={{0,3},{1,0},{2,1},{3,2},{4,7},{5,4},{6,5},{7,6},{8,11},{9,8},{10,9... | collective-permute-start | bytes 1671176 | tf_op jit(solution)/shard_map/ppermute | solution.py:591
  13.9 23.8 %collective-permute-start.1 = (f32[136,1024]{1,0:T(8,128)S(1)}, f32[136,1024]{1,0:T(8,128)S(1)}, u32[]{:S(2)}, u32[]{:S(2)}) collective-permute-start(f32[136,1024]{1,0:T(8,128)S(1)} %get-tuple-element.83), channel_id=1, source_target_pairs={{0,2},{1,3},{2,0},{3,1},{4,6},{5,7},{6,4},{7,5},{8,10},{9,11},{10,... | collective-permute-start | bytes 1671176 | tf_op jit(solution)/shard_map/ppermute | solution.py:591
  16.0 10.9 %collective-permute-start.3 = (bf16[256,768]{1,0:T(8,128)(2,1)S(1)}, bf16[256,768]{1,0:T(8,128)(2,1)S(1)}, u32[]{:S(2)}, u32[]{:S(2)}) collective-permute-start(bf16[256,768]{1,0:T(8,128)(2,1)S(1)} %get-tuple-element.86), channel_id=1, source_target_pairs={{0,4},{4,8},{8,12},{12,0},{1,5},{5,9},{9,13},{13,1},{2,6},{6,10},{... | collective-permute-start | bytes 1179656 | tf_op jit(solution)/shard_map/ppermute | solution.py:591
  17.1 10.3 %collective-permute-start.5 = (bf16[256,768]{1,0:T(8,128)(2,1)S(1)}, bf16[256,768]{1,0:T(8,128)(2,1)S(1)}, u32[]{:S(2)}, u32[]{:S(2)}) collective-permute-start(bf16[256,768]{1,0:T(8,128)(2,1)S(1)} %get-tuple-element.88), channel_id=1, source_target_pairs={{0,12},{4,0},{8,4},{12,8},{1,13},{5,1},{9,5},{13,9},{2,14},{6,2},{... | collective-permute-start | bytes 1179656 | tf_op jit(solution)/shard_map/ppermute | solution.py:591
  27.4 20.6 %collective-permute-start.10 = (bf16[1024,256]{1,0:T(8,128)(2,1)S(1)}, bf16[1024,256]{1,0:T(8,128)(2,1)S(1)}, u32[]{:S(2)}, u32[]{:S(2)}) collective-permute-start(bf16[1024,256]{1,0:T(8,128)(2,1)S(1)} %stack.13.rest_4_), channel_id=1, source_target_pairs={{0,3},{1,0},{2,1},{3,2},{4,7},{5,4},{6,5},{7,6},{8,11},{9,8},{10,9... | collective-permute-start | bytes 1572872 | tf_op jit(solution)/shard_map/ppermute | solution.py:591
  30.5 17.5 %collective-permute-start.9 = (bf16[1024,256]{1,0:T(8,128)(2,1)S(1)}, bf16[1024,256]{1,0:T(8,128)(2,1)S(1)}, u32[]{:S(2)}, u32[]{:S(2)}) collective-permute-start(bf16[1024,256]{1,0:T(8,128)(2,1)S(1)} %stack.13.rest_4_), channel_id=1, source_target_pairs={{0,1},{1,2},{2,3},{3,0},{4,5},{5,6},{6,7},{7,4},{8,9},{9,10},{10,1... | collective-permute-start | bytes 1572872 | tf_op jit(solution)/shard_map/ppermute | solution.py:591
  38.6 7.8 %collective-permute-start.6 = (f32[136,256]{1,0:T(8,128)S(1)}, f32[136,256]{1,0:T(8,128)S(1)}, u32[]{:S(2)}, u32[]{:S(2)}) collective-permute-start(f32[136,256]{1,0:T(8,128)S(1)} %get-tuple-element.98), channel_id=1, source_target_pairs={{0,4},{4,8},{8,12},{12,0},{1,5},{5,9},{9,13},{13,1},{2,6},{6,10},{... | collective-permute-start | bytes 417800 | tf_op jit(solution)/shard_map/ppermute | solution.py:591
  39.3 7.2 %collective-permute-start.7 = (f32[136,256]{1,0:T(8,128)S(1)}, f32[136,256]{1,0:T(8,128)S(1)}, u32[]{:S(2)}, u32[]{:S(2)}) collective-permute-start(f32[136,256]{1,0:T(8,128)S(1)} %get-tuple-element.99), channel_id=1, source_target_pairs={{0,8},{4,12},{8,0},{12,4},{1,9},{5,13},{9,1},{13,5},{2,10},{6,14},... | collective-permute-start | bytes 417800 | tf_op jit(solution)/shard_map/ppermute | solution.py:591
  41.2 6.1 %collective-permute-start.8 = (f32[136,256]{1,0:T(8,128)S(1)}, f32[136,256]{1,0:T(8,128)S(1)}, u32[]{:S(2)}, u32[]{:S(2)}) collective-permute-start(f32[136,256]{1,0:T(8,128)S(1)} %get-tuple-element.100), channel_id=1, source_target_pairs={{0,12},{4,0},{8,4},{12,8},{1,13},{5,1},{9,5},{13,9},{2,14},{6,2},{... | collective-permute-start | bytes 417800 | tf_op jit(solution)/shard_map/ppermute | solution.py:591
  47.3 6.6 %copy-start.10 = (bf16[4096]{0:T(1024)(128)(2,1)S(1)}, bf16[4096]{0:T(1024)(128)(2,1)}, u32[]{:S(2)}) copy-start(bf16[4096]{0:T(1024)(128)(2,1)} %param.18) | copy-start | bytes 24580
  48.0 7.1 %collective-permute-start.11 = (f32[128,256]{1,0:T(8,128)S(1)}, f32[128,256]{1,0:T(8,128)S(1)}, u32[]{:S(2)}, u32[]{:S(2)}) collective-permute-start(f32[128,256]{1,0:T(8,128)S(1)} %get-tuple-element.110), channel_id=1, source_target_pairs={{0,12},{4,0},{8,4},{12,8},{1,13},{5,1},{9,5},{13,9},{2,14},{6,2},{... | collective-permute-start | bytes 393224 | tf_op jit(solution)/shard_map/ppermute | solution.py:591
  50.8 6.6 %collective-permute-start.12 = (f32[128,256]{1,0:T(8,128)S(1)}, f32[128,256]{1,0:T(8,128)S(1)}, u32[]{:S(2)}, u32[]{:S(2)}) collective-permute-start(f32[128,256]{1,0:T(8,128)S(1)} %get-tuple-element.111), channel_id=1, source_target_pairs={{0,8},{4,12},{8,0},{12,4},{1,9},{5,13},{9,1},{13,5},{2,10},{6,14},... | collective-permute-start | bytes 393224 | tf_op jit(solution)/shard_map/ppermute | solution.py:591
  50.8 7.6 %collective-permute-start.13 = (f32[128,256]{1,0:T(8,128)S(1)}, f32[128,256]{1,0:T(8,128)S(1)}, u32[]{:S(2)}, u32[]{:S(2)}) collective-permute-start(f32[128,256]{1,0:T(8,128)S(1)} %get-tuple-element.112), channel_id=1, source_target_pairs={{0,4},{4,8},{8,12},{12,0},{1,5},{5,9},{9,13},{13,1},{2,6},{6,10},{... | collective-permute-start | bytes 393224 | tf_op jit(solution)/shard_map/ppermute | solution.py:591
  51.8 11.8 %collective-permute-start.18 = (bf16[512,256]{1,0:T(8,128)(2,1)S(1)}, bf16[512,256]{1,0:T(8,128)(2,1)S(1)}, u32[]{:S(2)}, u32[]{:S(2)}) collective-permute-start(bf16[512,256]{1,0:T(8,128)(2,1)S(1)} %slice.7), channel_id=1, source_target_pairs={{0,3},{1,0},{2,1},{3,2},{4,7},{5,4},{6,5},{7,6},{8,11},{9,8},{10,9... | collective-permute-start | bytes 786440 | tf_op jit(solution)/shard_map/ppermute | solution.py:591
  53.7 9.9 %collective-permute-start.17 = (bf16[512,256]{1,0:T(8,128)(2,1)S(1)}, bf16[512,256]{1,0:T(8,128)(2,1)S(1)}, u32[]{:S(2)}, u32[]{:S(2)}) collective-permute-start(bf16[512,256]{1,0:T(8,128)(2,1)S(1)} %slice.6), channel_id=1, source_target_pairs={{0,1},{1,2},{2,3},{3,0},{4,5},{5,6},{6,7},{7,4},{8,9},{9,10},{10,1... | collective-permute-start | bytes 786440 | tf_op jit(solution)/shard_map/ppermute | solution.py:591
  60.0 29.8 %collective-permute-start.14 = (f32[128,1024]{1,0:T(8,128)S(1)}, f32[128,1024]{1,0:T(8,128)S(1)}, u32[]{:S(2)}, u32[]{:S(2)}) collective-permute-start(f32[128,1024]{1,0:T(8,128)S(1)} %get-tuple-element.118), channel_id=1, source_target_pairs={{0,3},{1,0},{2,1},{3,2},{4,7},{5,4},{6,5},{7,6},{8,11},{9,8},{10,9... | collective-permute-start | bytes 1572872 | tf_op jit(solution)/shard_map/ppermute | solution.py:591
  61.9 27.9 %collective-permute-start.15 = (f32[128,1024]{1,0:T(8,128)S(1)}, f32[128,1024]{1,0:T(8,128)S(1)}, u32[]{:S(2)}, u32[]{:S(2)}) collective-permute-start(f32[128,1024]{1,0:T(8,128)S(1)} %get-tuple-element.119), channel_id=1, source_target_pairs={{0,2},{1,3},{2,0},{3,1},{4,6},{5,7},{6,4},{7,5},{8,10},{9,11},{10,... | collective-permute-start | bytes 1572872 | tf_op jit(solution)/shard_map/ppermute | solution.py:591
  63.6 26.3 %collective-permute-start.16 = (f32[128,1024]{1,0:T(8,128)S(1)}, f32[128,1024]{1,0:T(8,128)S(1)}, u32[]{:S(2)}, u32[]{:S(2)}) collective-permute-start(f32[128,1024]{1,0:T(8,128)S(1)} %get-tuple-element.120), channel_id=1, source_target_pairs={{0,1},{1,2},{2,3},{3,0},{4,5},{5,6},{6,7},{7,4},{8,9},{9,10},{10,1... | collective-permute-start | bytes 1572872 | tf_op jit(solution)/shard_map/ppermute | solution.py:591
  63.7 26.2 %copy-start.9 = (bf16[256,4096]{1,0:T(8,128)(2,1)S(1)}, bf16[256,4096]{1,0:T(8,128)(2,1)}, u32[]{:S(2)}) copy-start(bf16[256,4096]{1,0:T(8,128)(2,1)} %gate_ref.1) | copy-start | bytes 6291460
  79.1 15.9 %collective-permute-start.19 = (bf16[256,512]{1,0:T(8,128)(2,1)S(1)}, bf16[256,512]{1,0:T(8,128)(2,1)S(1)}, u32[]{:S(2)}, u32[]{:S(2)}) collective-permute-start(bf16[256,512]{1,0:T(8,128)(2,1)S(1)} %get-tuple-element.128), channel_id=1, source_target_pairs={{0,12},{4,0},{8,4},{12,8},{1,13},{5,1},{9,5},{13,9},{2,14},{6,2},{... | collective-permute-start | bytes 786440 | tf_op jit(solution)/shard_map/ppermute | solution.py:591
  80.3 14.7 %collective-permute-start.20 = (bf16[256,512]{1,0:T(8,128)(2,1)S(1)}, bf16[256,512]{1,0:T(8,128)(2,1)S(1)}, u32[]{:S(2)}, u32[]{:S(2)}) collective-permute-start(bf16[256,512]{1,0:T(8,128)(2,1)S(1)} %get-tuple-element.129), channel_id=1, source_target_pairs={{0,8},{4,12},{8,0},{12,4},{1,9},{5,13},{9,1},{13,5},{2,10},{6,14},... | collective-permute-start | bytes 786440 | tf_op jit(solution)/shard_map/ppermute | solution.py:591
  89.9 7.6 %collective-permute-start.21 = (bf16[256,512]{1,0:T(8,128)(2,1)S(1)}, bf16[256,512]{1,0:T(8,128)(2,1)S(1)}, u32[]{:S(2)}, u32[]{:S(2)}) collective-permute-start(bf16[256,512]{1,0:T(8,128)(2,1)S(1)} %get-tuple-element.130), channel_id=1, source_target_pairs={{0,4},{4,8},{8,12},{12,0},{1,5},{5,9},{9,13},{13,1},{2,6},{6,10},{... | collective-permute-start | bytes 786440 | tf_op jit(solution)/shard_map/ppermute | solution.py:591
